TPU v7x, 128 devices: a whole 4x4x4 slice. The times are simulated.
128 devices in a mesh: grp: 8 (over x, y_hi), head: 16 (over z, y_lo, core).
Axes of the slice: x: 4, y: 4 (y_hi: 2, y_lo: 2; y = y_hi * 2 + y_lo), z: 4, core: 2. Of those that a mesh axis runs over, the one named last changes fastest.
Arguments:
- hidden_in: bfloat16 [128, 8192], replicated, may hold values from -6 to 6
- row_owner: int32 [128], replicated, may hold values from 0 to 15, as said below
- history_len: int32 [128], replicated, may hold values from 0 to 3
- pre_gain: bfloat16 [8192], replicated, may hold values from 0.099609375 to 1.8984375
- inner_proj: bfloat16 [8192, 2, 16384], P('head', None, 'grp'), may hold values from -0.0625 to 0.0625
- select_proj: bfloat16 [8192, 2, 1024], P('head', None, 'grp'), may hold values from -0.0625 to 0.0625
- step_proj: bfloat16 [8192, 256], P('head', 'grp'), may hold values from -0.0625 to 0.0625
- step_bias: float32 [256], P('grp'), may hold values from -4 to -1
- decay_log: float32 [256], P('grp'), may hold values from -1 to 2
- skip_gain: float32 [256], P('grp'), may hold values from 0.5 to 1.5
- conv_taps: bfloat16 [5, 8, 2304], P(None, 'grp'), may hold values from -3 to 3
- conv_window: bfloat16 [128, 3, 8, 2304], P('head', None, 'grp'), may hold values from -6 to 6
- state_cache: bfloat16 [128, 256, 64, 128], P('head', 'grp'), may hold values from -6 to 6
- mixer_gain: bfloat16 [8, 2048], P('grp'), may hold values from 0.099609375 to 1.8984375
- output_proj: bfloat16 [8, 2048, 8192], P('grp', None, 'head'), may hold values from -0.046875 to 0.046875
- channel_gain: bfloat16 [8192], replicated, may hold values from 0.099609375 to 1.8984375
- up_weight: bfloat16 [8192, 32768], P(None, ('grp', 'head')), may hold values from -0.0625 to 0.0625
- down_weight: bfloat16 [32768, 8192], P(('grp', 'head')), may hold values from -0.125 to 0.125
Outputs:
- block_out: bfloat16 [128, 8192], P(None, ('grp', 'head'))
- state_next: bfloat16 [128, 256, 64, 128], P('head', 'grp')
- window_next: bfloat16 [128, 3, 8, 2304], P('head', None, 'grp')
Inputs may be any that keep to these rules, and one draw needn't show every extreme that they name: Every owner is named by exactly 8 rows. Block h of 8 slots of state_cache, conv_window, state_next and window_next belongs to the rows that row_owner assigns to h, in increasing row order.
All inputs are finite; a program needn't handle non-finite values.
Results may differ from a plain program's by a relative error of at most 0.023.
Values may be sent and summed in bfloat16 or wider, within the bound.
No kernel may reach another device: no remote copies, remote signals or barrier semaphores. Data moves between devices by JAX's collectives and lax.ppermute only.
A program may use at most 128 MiB of HBM per device.

v0:
```python
import jax
import jax.numpy as jnp
from jax import lax
from jax.sharding import PartitionSpec as P

EPS = 1e-05
HIGHEST = lax.Precision.HIGHEST


def rms_scale(values):
    return lax.rsqrt(jnp.mean(values * values, axis=-1, keepdims=True) + EPS)


def mixer(
    inner_terms,
    select_terms,
    step_raw,
    history_slot,
    step_bias,
    decay_log,
    skip_gain,
    conv_taps,
    conv_window,
    state_groups,
    mixer_gain,
):
    count_rows = inner_terms.shape[0]
    groups = inner_terms.shape[2]
    channels = inner_terms.shape[3]
    state_size = select_terms.shape[3]
    head_count = state_groups.shape[2]
    head_width = state_groups.shape[3]
    tap_count = conv_taps.shape[0] - 1
    fresh_input = jnp.concatenate(
        [inner_terms[:, 1], select_terms[:, 0], select_terms[:, 1]], axis=-1
    ).astype(jnp.bfloat16)
    window = jnp.concatenate([conv_window, fresh_input[:, None]], axis=1).astype(jnp.float32)
    lag_index = jnp.arange(tap_count, dtype=jnp.int32)
    valid_mask = (lag_index[None, :] >= (tap_count - 1 - history_slot)[:, None]).astype(jnp.float32)
    window = window * valid_mask[:, :, None, None]
    weights = conv_taps.astype(jnp.float32)
    conv_sum = (
        jnp.einsum("rkgc,kgc->rgc", window, weights[:tap_count], precision=HIGHEST)
        + weights[tap_count]
    )
    activated = jax.nn.silu(conv_sum)
    inputs = activated[..., :channels].reshape(count_rows, groups, head_count, head_width)
    in_coef = activated[..., channels : channels + state_size]
    out_coef = activated[..., channels + state_size :]
    step_size = jax.nn.softplus(step_raw + step_bias)
    decay_rate = jnp.exp(-step_size * jnp.exp(decay_log))
    updated = (
        decay_rate[..., None, None] * state_groups.astype(jnp.float32)
        + (step_size[..., None] * inputs)[..., None] * in_coef[:, :, None, None, :]
    )
    readout = (
        jnp.einsum("rghpn,rgn->rghp", updated, out_coef, precision=HIGHEST)
        + skip_gain[..., None] * inputs
    )
    gated_out = readout.reshape(count_rows, groups, channels) * jax.nn.silu(inner_terms[:, 0])
    normed = (gated_out * rms_scale(gated_out) * mixer_gain.astype(jnp.float32)).astype(
        jnp.bfloat16
    )
    return (normed, updated.astype(jnp.bfloat16), window[:, 1:].astype(jnp.bfloat16))


def local(
    hidden_in,
    row_owner,
    history_len,
    pre_gain,
    inner_proj,
    select_proj,
    step_proj,
    step_bias,
    decay_log,
    skip_gain,
    conv_taps,
    conv_window,
    state_cache,
    mixer_gain,
    output_proj,
    channel_gain,
    up_weight,
    down_weight,
):
    total_rows, model_width = hidden_in.shape
    head_devices = lax.axis_size("head")
    group_devices = lax.axis_size("grp")
    own_rows = total_rows // head_devices
    local_groups = conv_taps.shape[1]
    channels = mixer_gain.shape[1]
    state_size = select_proj.shape[2] // local_groups
    per_group = step_proj.shape[1] // local_groups
    head_width = state_cache.shape[2]
    slice_width = model_width // head_devices
    head_index = lax.axis_index("head")
    group_index = lax.axis_index("grp")
    positions = jnp.arange(total_rows, dtype=jnp.int32)
    slot_order = jnp.argsort(row_owner * total_rows + positions)
    slot_of_row = jnp.argsort(slot_order)
    hidden_wide = hidden_in.astype(jnp.float32)
    normed = (hidden_wide * rms_scale(hidden_wide) * pre_gain.astype(jnp.float32)).astype(
        jnp.bfloat16
    )
    local_cols = lax.dynamic_slice_in_dim(normed, head_index * slice_width, slice_width, 1)
    sorted_rows = local_cols[slot_order]
    inner_flat = inner_proj.reshape(slice_width, -1)
    select_flat = select_proj.reshape(slice_width, -1)
    inner_size = inner_flat.shape[1]
    select_size = select_flat.shape[1]
    projected = lax.psum_scatter(
        jnp.concatenate(
            [
                jnp.dot(sorted_rows, inner_flat, preferred_element_type=jnp.float32),
                jnp.dot(sorted_rows, select_flat, preferred_element_type=jnp.float32),
                jnp.dot(sorted_rows, step_proj, preferred_element_type=jnp.float32),
            ],
            axis=1,
        ),
        "head",
        scatter_dimension=0,
        tiled=True,
    )
    inner_terms = projected[:, :inner_size].reshape(own_rows, 2, local_groups, channels)
    select_terms = projected[:, inner_size : inner_size + select_size].reshape(
        own_rows, 2, local_groups, state_size
    )
    step_raw = projected[:, inner_size + select_size :].reshape(own_rows, local_groups, per_group)
    history_slot = lax.dynamic_slice_in_dim(
        history_len[slot_order], head_index * own_rows, own_rows, 0
    )
    state_groups = state_cache.reshape(own_rows, local_groups, per_group, head_width, state_size)
    normed_mix, state_next, window_next = mixer(
        inner_terms,
        select_terms,
        step_raw,
        history_slot,
        step_bias.reshape(local_groups, per_group),
        decay_log.reshape(local_groups, per_group),
        skip_gain.reshape(local_groups, per_group),
        conv_taps,
        conv_window,
        state_groups,
        mixer_gain,
    )
    mixed_part = jnp.einsum(
        "rgc,gcd->rd",
        lax.all_gather(normed_mix, "head", axis=0, tiled=True),
        output_proj,
        preferred_element_type=jnp.float32,
    )
    mixed_cols = lax.psum(mixed_part.astype(jnp.bfloat16), "grp").astype(jnp.float32)
    base_cols = lax.dynamic_slice_in_dim(hidden_wide, head_index * slice_width, slice_width, 1)
    hidden_piece = (base_cols + mixed_cols[slot_of_row]).astype(jnp.bfloat16)
    residual = lax.all_gather(hidden_piece, "head", axis=1, tiled=True)
    residual_wide = residual.astype(jnp.float32)
    ffn_input = (
        residual_wide * rms_scale(residual_wide) * channel_gain.astype(jnp.float32)
    ).astype(jnp.bfloat16)
    raised = jnp.maximum(jnp.dot(ffn_input, up_weight, preferred_element_type=jnp.float32), 0.0)
    squared = (raised * raised).astype(jnp.bfloat16)
    down_terms = jnp.dot(squared, down_weight, preferred_element_type=jnp.float32)
    piece_width = model_width // (group_devices * head_devices)
    flat_index = group_index * head_devices + head_index
    residual_piece = lax.dynamic_slice_in_dim(
        residual_wide, flat_index * piece_width, piece_width, 1
    )
    down_total = lax.psum_scatter(down_terms, ("grp", "head"), scatter_dimension=1, tiled=True)
    block_out = (residual_piece + down_total).astype(jnp.bfloat16)
    state_flat = state_next.reshape(own_rows, local_groups * per_group, head_width, state_size)
    return (block_out, state_flat, window_next)


def solution(mesh):
    placed = (
        P(),
        P(),
        P(),
        P(),
        P("head", None, "grp"),
        P("head", None, "grp"),
        P("head", "grp"),
        P("grp"),
        P("grp"),
        P("grp"),
        P(None, "grp", None),
        P("head", None, "grp", None),
        P("head", "grp", None, None),
        P("grp", None),
        P("grp", None, "head"),
        P(),
        P(None, ("grp", "head")),
        P(("grp", "head"), None),
    )
    return jax.shard_map(
        local,
        mesh=mesh,
        in_specs=placed,
        out_specs=(
            P(None, ("grp", "head")),
            P("head", "grp", None, None),
            P("head", None, "grp", None),
        ),
        check_vma=False,
    )
```

profile of v0, /device:TPU:0, one launch (start us, length us, event | category | flops | bytes accessed | tf_op | source)
XLA Modules:
  0.0 987.8 jit_solution(4694069242667145984)
XLA Ops:
  7.2 0.0 copy-start
  7.2 0.0 all-reduce.6.cloned.1.call-start
  7.2 4.2 copy.35
  11.5 4.0 convert_element_type.97
  15.5 1.1 multiply_reduce_fusion.1
  16.6 0.8 dynamic-slice.2
  17.4 1.1 multiply_convert_fusion.10
  18.5 0.1 copy.36
  18.6 2.5 sort.31
  21.2 6.5 copy.53
  27.7 0.8 gather_fusion
  28.5 2.9 fusion.37
  31.4 0.0 copy-start.1
  31.4 0.0 copy-start.13
  31.5 0.0 copy-start.9
  31.5 0.0 copy-start.14
  31.5 0.0 copy-start.7
  31.5 0.2 fusion.19
  31.7 0.0 copy-done.6
  31.7 0.0 copy-start.4
  31.7 0.2 fusion.38
  31.9 0.0 copy-start.10
  31.9 1.5 pad_maximum_fusion
  33.4 0.0 all-reduce.6.cloned.1.call-update
  33.4 0.0 all-reduce.4.cloned.1.call-start
  33.5 0.0 copy-done.1
  33.5 1.2 gather_fusion.1
  34.8 2.5 sort.32
  37.3 0.0 copy-done.14
  37.3 0.6 dynamic-slice
  38.6 0.1 dynamic-slice_subtract_fusion
  38.7 123.3 %all-reduce.6.cloned.1.call-done = f32[128,4384]{1,0:T(8,128)} async-done(((f32[128,4384]{1,0:T(8,128)}), f32[128,4384]{1,0:T(8,128)}) %all-reduce.6.cloned.1.call-update) | async-done | bytes 2244624
  162.0 0.9 constant_dynamic-slice_fusion
  162.9 0.8 fusion.34
  163.7 0.1 multiply_reduce_fusion.2
  163.9 0.1 reshape.420
  164.0 0.1 squeeze.9
  164.1 0.8 multiply_exponential_fusion
  164.8 0.1 broadcast_multiply_fusion
  165.0 0.0 copy-start.11
  165.0 21.4 %fusion.1 = f32[8,1,32,64]{3,1,2,0:T(1,128)S(1)} fusion(f32[8,128,1,1]{1,2,3,0:T(1,128)S(1)} %bitcast.105, bf16[8,32,64,128]{3,2,1,0:T(8,128)(2,1)} %param.30, f32[8,128]{1,0:T(8,128)S(1)} %get-tuple-element.11, f32[8,32,64]{2,1,0:T(8,128)S(1)} %broadcast_multiply_fusion, f32[8,32]{1,0:T(8,128)S(1)} %get-tuple-element.9), kind=kOutput, calls=%fused_computation.5 | convolution fusion | flops 33554432 | bytes 4334592 | tf_op jit(solution)/shard_map/rghpn,rgn->rghp/dot_general | solution.py:57
  186.4 0.2 multiply_reduce_fusion.3
  186.7 0.1 reshape.422
  186.8 0.1 fusion.32
  186.8 18.7 %all_gather.6 = bf16[128,1,2048]{2,0,1:T(8,128)(2,1)S(1)} all-gather(bf16[8,1,2048]{2,0,1:T(8,128)(2,1)S(1)} %fusion.32), channel_id=1, replica_groups=mesh['grp'=8,'head'=16] {'head'}, dimensions={0}, use_global_device_ids=true | all-gather | bytes 557056 | tf_op jit(solution)/shard_map/all_gather | solution.py:149
  205.6 1.1 fusion.11
  206.7 0.0 all-reduce.4.cloned.1.call-update
  206.7 0.0 all-gather.2.cloned.1.call-start
  206.8 82.4 %all-reduce.4.cloned.1.call-done = bf16[128,512]{1,0:T(8,128)(2,1)} async-done(((bf16[128,512]{1,0:T(8,128)(2,1)}), bf16[128,512]{1,0:T(8,128)(2,1)}) %all-reduce.4.cloned.1.call-update) | async-done | bytes 131088 | tf_op jit(solution)/shard_map/psum | solution.py:153
  289.1 0.9 convert_element_type.107
  290.1 0.8 gather_fusion.2
  290.8 0.1 copy.41
  291.0 1.6 add_convert_fusion
  292.6 0.0 all-gather.2.cloned.1.call-update
  292.6 0.2 reduce-scatter.2.cloned.1.call-start
  292.9 31.8 %all-gather.2.cloned.1.call-done = bf16[128,8192]{0,1:T(8,128)(2,1)} async-done(((bf16[128,512]{0,1:T(8,128)(2,1)}), bf16[128,8192]{0,1:T(8,128)(2,1)}) %all-gather.2.cloned.1.call-update) | async-done | bytes 2097168 | tf_op jit(solution)/shard_map/all_gather | solution.py:156
  324.7 2.7 multiply_reduce_fusion
  327.4 9.7 fusion.17
  337.1 0.0 reduce-scatter.2.cloned.1.call-update
  337.2 6.2 fusion
  343.3 0.7 multiply_convert_fusion.11
  344.1 2.2 convert_element_type.109
  346.3 633.6 %reduce-scatter.2.cloned.1.call-done = f32[128,64]{0,1:T(8,128)} async-done(((f32[128,8192]{0,1:T(8,128)}), f32[128,64]{0,1:T(8,128)}) %reduce-scatter.2.cloned.1.call-update) | async-done | bytes 32784 | tf_op jit(solution)/shard_map/reduce_scatter | solution.py:169
  979.9 1.4 add_convert_fusion.1
  (42 shorter events, 0.2 us)
Async XLA Ops:
  7.2 198.4 %copy-start = (bf16[1,2048,512]{2,1,0:T(8,128)(2,1)S(1)}, bf16[1,2048,512]{2,1,0:T(8,128)(2,1)}, u32[]{:S(2)}) copy-start(bf16[1,2048,512]{2,1,0:T(8,128)(2,1)} %param.32) | copy-start | bytes 6291460
  7.2 154.8 %all-reduce.6.cloned.1.call-start = ((), (), s32[]{:S(2)}) async-start(), calls=%async_computation.4 | async-start | bytes 4587520
  11.5 4.0 copy-start.2
  11.5 7.1 copy-start.12
  27.7 3.8 copy-start.5
  27.7 4.0 copy-start.6
  31.4 2.1 copy-start.1
  31.4 3.3 copy-start.13
  31.5 3.3 copy-start.9
  31.5 5.9 copy-start.14
  31.5 7.2 copy-start.7
  31.7 132.0 %copy-start.4 = (bf16[8,3,1,2304]{3,0,2,1:T(8,128)(2,1)S(1)}, bf16[8,3,1,2304]{3,0,2,1:T(8,128)(2,1)}, u32[]{:S(2)}) copy-start(bf16[8,3,1,2304]{3,0,2,1:T(8,128)(2,1)} %param.29) | copy-start | bytes 331780
  31.9 132.2 %copy-start.10 = (f32[32]{0:T(128)S(1)}, f32[32]{0:T(128)}, u32[]{:S(2)}) copy-start(f32[32]{0:T(128)} %param.25) | copy-start | bytes 388
  33.4 255.7 %all-reduce.4.cloned.1.call-start = ((), (), s32[]{:S(2)}) async-start(), calls=%async_computation.1 | async-start | bytes 262144 | tf_op jit(solution)/shard_map/psum | solution.py:153
  165.0 21.4 %copy-start.11 = (f32[32]{0:T(128)S(1)}, f32[32]{0:T(128)}, u32[]{:S(2)}) copy-start(f32[32]{0:T(128)} %param.27) | copy-start | bytes 388
  186.4 106.4 %copy-start.8 = (bf16[8192]{0:T(1024)(128)(2,1)S(1)}, bf16[8192]{0:T(1024)(128)(2,1)}, u32[]{:S(2)}) copy-start(bf16[8192]{0:T(1024)(128)(2,1)} %param.33) | copy-start | bytes 49156
  206.7 118.0 %all-gather.2.cloned.1.call-start = ((), (), s32[]{:S(2)}) async-start(), calls=%async_computation.2 | async-start | bytes 2228224 | tf_op jit(solution)/shard_map/all_gather | solution.py:156
  292.6 687.3 %reduce-scatter.2.cloned.1.call-start = ((), (), s32[]{:S(2)}) async-start(), calls=%async_computation.3 | async-start | bytes 4227072 | tf_op jit(solution)/shard_map/reduce_scatter | solution.py:169
  337.2 6.9 copy-start.3
Sparse Core Ops, SparseCore 0:
  33.5 128.4 all-reduce.5
  206.8 82.2 all-reduce.3
  292.7 31.9 all-gather.1
  337.3 642.5 reduce-scatter.1
where the time goes:
time: 988 us
  waiting for transfers between devices  871 us (88%)
  matrix products  35.5 us (4%)
  other arithmetic  30 us (3%)
  blocking collectives  18.7 us (2%)
  local copies, waits for them, and re-layouts  17.3 us (2%)
  between operations  14.8 us (1%)
    reduce_scatter x1, waiting for transfers between devices, local(): lax.psum_scatter(down_terms, ('grp', 'head'), scatter_dimension=1, tiled=...  634 us
    unnamed x5, waiting for transfers between devices  123 us
    psum x1, waiting for transfers between devices, local(): lax.psum(mixed_part.astype(jnp.bfloat16), 'grp').astype(jnp.float32)  82.4 us
    all_gather x1, waiting for transfers between devices, local(): residual = lax.all_gather(hidden_piece, 'head', axis=1, tiled=True)  31.8 us
    dot_general x1, matrix products, mixer(): jnp.einsum('rghpn,rgn->rghp', updated, out_coef, precision=HIGHEST)  21.4 us
  transfers between devices with their start and end apart: 4, of which 4 were waited for; matrix products, arithmetic and copies ran while one was open for 1% of the time, Pallas kernels for 0%

commit v1 on v0

v1 whole, which is shorter than its diff:
```python
import jax
import jax.numpy as jnp
from jax import lax
from jax.sharding import Mesh, PartitionSpec as P

EPS = 1e-05
HIGHEST = lax.Precision.HIGHEST
GRP = ("x", "yh")
HEAD = ("z", "yl", "c")
CHIPS = ("x", "yh", "z", "yl")


def rms_scale(values):
    return lax.rsqrt(jnp.mean(values * values, axis=-1, keepdims=True) + EPS)


def swap(value, axis, bit):
    size = lax.axis_size(axis)
    return lax.ppermute(value, axis, [(i, i ^ bit) for i in range(size)])


def mixer(
    inner_terms,
    select_terms,
    step_raw,
    history_slot,
    step_bias,
    decay_log,
    skip_gain,
    conv_taps,
    conv_window,
    state_groups,
    mixer_gain,
):
    count_rows = inner_terms.shape[0]
    groups = inner_terms.shape[2]
    channels = inner_terms.shape[3]
    state_size = select_terms.shape[3]
    head_count = state_groups.shape[2]
    head_width = state_groups.shape[3]
    tap_count = conv_taps.shape[0] - 1
    fresh_input = jnp.concatenate(
        [inner_terms[:, 1], select_terms[:, 0], select_terms[:, 1]], axis=-1
    ).astype(jnp.bfloat16)
    window = jnp.concatenate([conv_window, fresh_input[:, None]], axis=1).astype(jnp.float32)
    lag_index = jnp.arange(tap_count, dtype=jnp.int32)
    valid_mask = (lag_index[None, :] >= (tap_count - 1 - history_slot)[:, None]).astype(jnp.float32)
    window = window * valid_mask[:, :, None, None]
    weights = conv_taps.astype(jnp.float32)
    conv_sum = (
        jnp.einsum("rkgc,kgc->rgc", window, weights[:tap_count], precision=HIGHEST)
        + weights[tap_count]
    )
    activated = jax.nn.silu(conv_sum)
    inputs = activated[..., :channels].reshape(count_rows, groups, head_count, head_width)
    in_coef = activated[..., channels : channels + state_size]
    out_coef = activated[..., channels + state_size :]
    step_size = jax.nn.softplus(step_raw + step_bias)
    decay_rate = jnp.exp(-step_size * jnp.exp(decay_log))
    updated = (
        decay_rate[..., None, None] * state_groups.astype(jnp.float32)
        + (step_size[..., None] * inputs)[..., None] * in_coef[:, :, None, None, :]
    )
    readout = (
        jnp.einsum("rghpn,rgn->rghp", updated, out_coef, precision=HIGHEST)
        + skip_gain[..., None] * inputs
    )
    gated_out = readout.reshape(count_rows, groups, channels) * jax.nn.silu(inner_terms[:, 0])
    normed = (gated_out * rms_scale(gated_out) * mixer_gain.astype(jnp.float32)).astype(
        jnp.bfloat16
    )
    return (normed, updated.astype(jnp.bfloat16), window[:, 1:].astype(jnp.bfloat16))


def local(
    hidden_in,
    row_owner,
    history_len,
    pre_gain,
    inner_proj,
    select_proj,
    step_proj,
    step_bias,
    decay_log,
    skip_gain,
    conv_taps,
    conv_window,
    state_cache,
    mixer_gain,
    output_proj,
    channel_gain,
    up_weight,
    down_weight,
):
    total_rows, model_width = hidden_in.shape
    head_devices = lax.axis_size(HEAD)
    group_devices = lax.axis_size(GRP)
    own_rows = total_rows // head_devices
    local_groups = conv_taps.shape[1]
    channels = mixer_gain.shape[1]
    state_size = select_proj.shape[2] // local_groups
    per_group = step_proj.shape[1] // local_groups
    head_width = state_cache.shape[2]
    slice_width = model_width // head_devices
    head_index = lax.axis_index(HEAD)
    group_index = lax.axis_index(GRP)
    core = lax.axis_index("c")
    positions = jnp.arange(total_rows, dtype=jnp.int32)
    sort_key = row_owner * total_rows + positions
    slot_of_row = jnp.sum((sort_key[None, :] < sort_key[:, None]).astype(jnp.int32), axis=1)
    to_slot = (slot_of_row[None, :] == positions[:, None]).astype(jnp.bfloat16)
    hidden_wide = hidden_in.astype(jnp.float32)
    scale = rms_scale(hidden_wide)
    base_cols = lax.dynamic_slice_in_dim(
        hidden_in, head_index * slice_width, slice_width, 1
    ).astype(jnp.float32)
    gain_cols = lax.dynamic_slice_in_dim(pre_gain, head_index * slice_width, slice_width, 0)
    local_cols = (base_cols * scale * gain_cols.astype(jnp.float32)).astype(jnp.bfloat16)
    sorted_rows = jnp.dot(to_slot, local_cols)
    inner_flat = inner_proj.reshape(slice_width, -1)
    select_flat = select_proj.reshape(slice_width, -1)
    inner_size = inner_flat.shape[1]
    select_size = select_flat.shape[1]
    terms = jnp.concatenate(
        [
            jnp.dot(sorted_rows, inner_flat, preferred_element_type=jnp.float32),
            jnp.dot(sorted_rows, select_flat, preferred_element_type=jnp.float32),
            jnp.dot(sorted_rows, step_proj, preferred_element_type=jnp.float32),
        ],
        axis=1,
    ).astype(jnp.bfloat16)
    pieces = lax.all_to_all(
        terms.reshape(head_devices, own_rows, -1), HEAD, split_axis=0, concat_axis=0, tiled=True
    )
    projected = jnp.sum(pieces.astype(jnp.float32), axis=0)
    inner_terms = projected[:, :inner_size].reshape(own_rows, 2, local_groups, channels)
    select_terms = projected[:, inner_size : inner_size + select_size].reshape(
        own_rows, 2, local_groups, state_size
    )
    step_raw = projected[:, inner_size + select_size :].reshape(own_rows, local_groups, per_group)
    own_slots = head_index * own_rows + jnp.arange(own_rows, dtype=jnp.int32)
    history_slot = jnp.sum(
        jnp.where(slot_of_row[None, :] == own_slots[:, None], history_len[None, :], 0), axis=1
    )
    state_groups = state_cache.reshape(own_rows, local_groups, per_group, head_width, state_size)
    normed_mix, state_next, window_next = mixer(
        inner_terms,
        select_terms,
        step_raw,
        history_slot,
        step_bias.reshape(local_groups, per_group),
        decay_log.reshape(local_groups, per_group),
        skip_gain.reshape(local_groups, per_group),
        conv_taps,
        conv_window,
        state_groups,
        mixer_gain,
    )
    all_mix = lax.all_to_all(
        jnp.broadcast_to(normed_mix.reshape(1, own_rows, -1), (head_devices, own_rows, channels)),
        HEAD,
        split_axis=0,
        concat_axis=0,
        tiled=True,
    ).reshape(total_rows, channels)
    mixed = jnp.dot(
        all_mix, output_proj.reshape(channels, -1), preferred_element_type=jnp.float32
    ).astype(jnp.bfloat16)
    for axis, bit in (("x", 1), ("x", 3), ("yh", 1)):
        other = swap(mixed, axis, bit)
        mixed = (mixed.astype(jnp.float32) + other.astype(jnp.float32)).astype(jnp.bfloat16)
    mixed_rows = jnp.dot(to_slot.T, mixed, preferred_element_type=jnp.float32)
    hidden_piece = (base_cols + mixed_rows).astype(jnp.bfloat16)
    near = lax.all_to_all(
        jnp.broadcast_to(hidden_piece[None], (head_devices // 2,) + hidden_piece.shape),
        ("z", "yl"),
        split_axis=0,
        concat_axis=0,
        tiled=True,
    )
    far = swap(near, "c", 1)
    even = jnp.where(core == 0, near, far)
    odd = jnp.where(core == 0, far, near)
    residual = jnp.stack([even, odd], axis=1).reshape(head_devices, total_rows, slice_width)
    residual_wide = residual.astype(jnp.float32)
    row_scale = lax.rsqrt(
        jnp.sum(residual_wide * residual_wide, axis=(0, 2)) / model_width + EPS
    )
    ffn_input = (
        residual_wide
        * row_scale[None, :, None]
        * channel_gain.astype(jnp.float32).reshape(head_devices, 1, slice_width)
    ).astype(jnp.bfloat16)
    raised = jnp.maximum(
        jnp.einsum(
            "krd,kdf->rf",
            ffn_input,
            up_weight.reshape(head_devices, slice_width, -1),
            preferred_element_type=jnp.float32,
        ),
        0.0,
    )
    squared = (raised * raised).astype(jnp.bfloat16)
    down_terms = lax.dot_general(
        down_weight, squared, (((0,), (1,)), ((), ())), preferred_element_type=jnp.float32
    ).astype(jnp.bfloat16)
    chips = group_devices * head_devices // 2
    piece_width = model_width // (group_devices * head_devices)
    paired = down_terms.reshape(chips, 2, piece_width, total_rows)
    keep = lax.dynamic_index_in_dim(paired, core, 1, keepdims=False)
    give = lax.dynamic_index_in_dim(paired, 1 - core, 1, keepdims=False)
    chip_sum = (keep.astype(jnp.float32) + swap(give, "c", 1).astype(jnp.float32)).astype(
        jnp.bfloat16
    )
    spread = lax.all_to_all(chip_sum, CHIPS, split_axis=0, concat_axis=0, tiled=True)
    down_total = jnp.sum(spread.astype(jnp.float32), axis=0)
    flat_index = group_index * head_devices + head_index
    per_slice = slice_width // piece_width
    residual_piece = lax.dynamic_slice(
        residual,
        (flat_index // per_slice, 0, (flat_index % per_slice) * piece_width),
        (1, total_rows, piece_width),
    )[0].astype(jnp.float32)
    block_out = (residual_piece.T + down_total).astype(jnp.bfloat16).T
    state_flat = state_next.reshape(own_rows, local_groups * per_group, head_width, state_size)
    return (block_out, state_flat, window_next)


def solution(mesh):
    fine = Mesh(mesh.devices.reshape(4, 2, 4, 2, 2), ("x", "yh", "z", "yl", "c"))
    placed = (
        P(),
        P(),
        P(),
        P(),
        P(HEAD, None, GRP),
        P(HEAD, None, GRP),
        P(HEAD, GRP),
        P(GRP),
        P(GRP),
        P(GRP),
        P(None, GRP, None),
        P(HEAD, None, GRP, None),
        P(HEAD, GRP, None, None),
        P(GRP, None),
        P(GRP, None, HEAD),
        P(),
        P(None, GRP + HEAD),
        P(GRP + HEAD, None),
    )
    return jax.shard_map(
        local,
        mesh=fine,
        in_specs=placed,
        out_specs=(
            P(None, GRP + HEAD),
            P(HEAD, GRP, None, None),
            P(HEAD, None, GRP, None),
        ),
        check_vma=False,
    )
```

time: 988 us -> 175 us (0.18)
  waiting for transfers between devices: 871 us -> 43.9 us
  starting transfers between devices: 0.34 us -> 22.1 us
  between operations: 14.8 us -> 0.99 us
  blocking collectives: 18.7 us -> 29.7 us
    reduce_scatter x1 -> x0, waiting for transfers between devices: 634 us -> none  [local(): lax.psum_scatter(down_terms, ('grp', 'head'), scatter_dimension=1, tiled=...]
    unnamed x5 -> x0, waiting for transfers between devices: 123 us -> none
    psum x1 -> x0, waiting for transfers between devices: 82.4 us -> none  [local(): lax.psum(mixed_part.astype(jnp.bfloat16), 'grp').astype(jnp.float32)]
    all_gather x1 -> x0, waiting for transfers between devices: 31.8 us -> none  [local(): residual = lax.all_gather(hidden_piece, 'head', axis=1, tiled=True)]
    all_to_all x0 -> x2, blocking collectives: none -> 29.7 us  [the longest x1 16.2 us: local(): lax.all_to_all(jnp.broadcast_to(hidden_piece[None], (head_devices // 2,)...]
    all_to_all x0 -> x2, waiting for transfers between devices: none -> 28 us  [the longest x1 15.7 us: local(): lax.all_to_all(terms.reshape(head_devices, own_rows, -1), HEAD, split_axi...]
    all_gather x1 -> x0, blocking collectives: 18.7 us -> none  [local(): lax.all_gather(normed_mix, 'head', axis=0, tiled=True)]
    ppermute x0 -> x5, waiting for transfers between devices: none -> 15.9 us  [swap(): return lax.ppermute(value, axis, [(i, i ^ bit) for i in range(size)])]
  transfers between devices with their start and end apart: 4 -> 7, of which waited for: 4 -> 7; matrix products, arithmetic and copies ran while one was open for 1% -> 5% of each run, Pallas kernels for 0% -> 0%
where the time goes in v1:
time: 175 us; the launch traced here: 173 us
  waiting for transfers between devices  43.9 us (25%)
  matrix products  37.4 us (21%)
  blocking collectives  29.7 us (17%)
  other arithmetic  23.8 us (14%)
  starting transfers between devices  22.1 us (13%)
  local copies, waits for them, and re-layouts  15.7 us (9%)
    dot_general x1, matrix products, mixer(): jnp.einsum('rghpn,rgn->rghp', updated, out_coef, precision=HIGHEST)  21.4 us
    all_to_all x1, blocking collectives, local(): lax.all_to_all(jnp.broadcast_to(hidden_piece[None], (head_devices // 2,)...  16.2 us
    ppermute x5, waiting for transfers between devices, swap(): return lax.ppermute(value, axis, [(i, i ^ bit) for i in range(size)])  15.9 us
    all_to_all x1, waiting for transfers between devices, local(): lax.all_to_all(terms.reshape(head_devices, own_rows, -1), HEAD, split_axi...  15.7 us
    all_to_all x1, blocking collectives, local(): lax.all_to_all(jnp.broadcast_to(normed_mix.reshape(1, own_rows, -1), (hea...  13.5 us
    all_to_all x1, waiting for transfers between devices, local(): lax.all_to_all(chip_sum, CHIPS, split_axis=0, concat_axis=0, tiled=True)  12.3 us
    dot_general x1, matrix products, local(): lax.dot_general(down_weight, squared, (((0,), (1,)), ((), ())), preferred...  9.2 us
    all_to_all x1, starting transfers between devices, local(): lax.all_to_all(chip_sum, CHIPS, split_axis=0, concat_axis=0, tiled=True)  7.93 us
  transfers between devices with their start and end apart: 7, of which 7 were waited for; matrix products, arithmetic and copies ran while one was open for 5% of the time, Pallas kernels for 0%

profile of v1, /device:TPU:0, one launch (start us, length us, event | category | flops | bytes accessed | tf_op | source)
XLA Modules:
  0.0 173.5 jit_solution(11718120546565644772)
XLA Ops:
  0.6 0.0 copy-start
  0.7 2.2 %multiply_reduce_fusion.1 = f32[128]{0:T(128)S(1)} fusion(bf16[128,8192]{1,0:T(8,128)(2,1)} %param.18), kind=kLoop, calls=%fused_computation.11 | loop fusion | flops 3145600 | bytes 2097664 | tf_op jit(solution)/shard_map/reduce_sum | solution.py:14
  2.9 0.7 iota_add_fusion.1
  3.6 0.2 convert_reduce_fusion.2
  3.7 0.8 dynamic-slice_convert_fusion
  4.5 1.2 fusion.23
  5.7 0.9 convolution_convert_fusion.3
  6.6 0.1 copy.28
  6.7 1.1 reshape.425
  7.8 0.2 convolution_convert_fusion.2
  8.0 7.8 %reshape.424 = bf16[512,4096,1]{1,0,2:T(8,128)(2,1)} reshape(bf16[512,2,2048]{2,1,0:T(2,128)(2,1)} %param.22) | data formatting | bytes 8388608 | tf_op jit(solution)/shard_map/reshape | solution.py:120
  15.8 2.9 %convolution_convert_fusion.1 = bf16[16,8,4096]{2,1,0:T(8,128)(2,1)S(1)} fusion(bf16[512,4096,1]{1,0,2:T(8,128)(2,1)} %reshape.424, bf16[128,512]{1,0:T(8,128)(2,1)S(1)} %fusion.23), kind=kOutput, calls=%fused_computation.5 | convolution fusion | flops 537395200 | bytes 5373952 | tf_op jit(solution)/shard_map/dot_general | solution.py:126
  18.8 0.0 copy-start.1
  18.8 1.1 pad_maximum_fusion.1
  19.9 6.5 %all-to-all-start = ((bf16[16,8,4384]{2,1,0:T(8,128)(2,1)}), bf16[16,8,4384]{2,1,0:T(8,128)(2,1)S(1)}, u32[]{:S(2)}, u32[]{:S(2)}) async-start(bf16[16,8,4384]{2,1,0:T(8,128)(2,1)} %pad_maximum_fusion.1), calls=%async_computation | async-start | bytes 2293760 | tf_op jit(solution)/shard_map/all_to_all | solution.py:132
  26.4 0.2 select_reduce_fusion
  26.6 0.5 exp.33
  27.2 0.0 copy-done.2
  27.2 0.6 fusion.46
  27.8 0.6 bitcast_convert_fusion
  28.4 15.7 %all-to-all-done = bf16[16,8,4384]{2,1,0:T(8,128)(2,1)S(1)} async-done(((bf16[16,8,4384]{2,1,0:T(8,128)(2,1)}), bf16[16,8,4384]{2,1,0:T(8,128)(2,1)S(1)}, u32[]{:S(2)}, u32[]{:S(2)}) %all-to-all-start) | async-done | bytes 1122336 | tf_op jit(solution)/shard_map/all_to_all | solution.py:132
  44.1 0.2 convert_reduce_fusion
  44.3 0.9 multiply_reduce_fusion.2
  45.3 0.1 squeeze.15
  45.4 0.1 reshape.410
  45.5 0.7 multiply_exponential_fusion
  46.2 0.1 broadcast_multiply_fusion
  46.3 0.0 copy-start.11
  46.3 21.4 %fusion.2 = f32[8,1,32,64]{3,1,2,0:T(1,128)S(1)} fusion(f32[8,128,1,1]{1,2,3,0:T(1,128)S(1)} %bitcast.132, bf16[8,32,64,128]{3,2,1,0:T(8,128)(2,1)} %param.30, f32[8,128]{1,0:T(8,128)S(1)} %get-tuple-element.9, f32[8,32,64]{2,1,0:T(8,128)S(1)} %broadcast_multiply_fusion, f32[8,32]{1,0:T(8,128)S(1)} %get-tuple-element.5), kind=kOutput, calls=%fused_computation.4 | convolution fusion | flops 33554432 | bytes 4334592 | tf_op jit(solution)/shard_map/rghpn,rgn->rghp/dot_general | solution.py:65
  67.7 0.2 multiply_reduce_fusion.3
  68.0 0.1 reshape.412
  68.1 0.1 fusion.40
  68.2 0.1 broadcast_in_dim.18
  68.2 0.0 copy-start.6
  68.2 13.5 %all_to_all.20 = bf16[16,8,2048]{2,1,0:T(8,128)(2,1)S(1)} all-to-all(bf16[16,8,2048]{2,1,0:T(8,128)(2,1)S(1)} %broadcast_in_dim.18), channel_id=1, replica_groups=mesh['x'=4,'yh'=2,'z'=4,'yl'=2,'c'=2] {'z','yl','c'}, dimensions={0} | all-to-all | bytes 1048576 | tf_op jit(solution)/shard_map/all_to_all | solution.py:159
  81.7 0.0 copy-done
  81.7 0.4 fusion.13
  82.2 1.6 collective-permute-start
  83.8 3.5 %collective-permute-done = bf16[128,512]{1,0:T(8,128)(2,1)S(1)} collective-permute-done((bf16[128,512]{1,0:T(8,128)(2,1)S(1)}, bf16[128,512]{1,0:T(8,128)(2,1)S(1)}, u32[]{:S(2)}, u32[]{:S(2)}) %collective-permute-start) | collective-permute-done | bytes 131104 | tf_op jit(solution)/shard_map/ppermute | solution.py:19
  87.3 2.8 %collective-permute-start.1 = (bf16[128,512]{1,0:T(8,128)(2,1)S(1)}, bf16[128,512]{1,0:T(8,128)(2,1)S(1)}, u32[]{:S(2)}, u32[]{:S(2)}) collective-permute-start(bf16[128,512]{1,0:T(8,128)(2,1)S(1)} %add_convert_fusion.2), channel_id=1, source_target_pairs={{0,96},{32,64},{64,32},{96,0},{1,97},{33,65},{65,33},{97,1},{2,98}... | collective-permute-start | bytes 393224 | tf_op jit(solution)/shard_map/ppermute | solution.py:19
  90.1 3.4 %collective-permute-done.1 = bf16[128,512]{1,0:T(8,128)(2,1)S(1)} collective-permute-done((bf16[128,512]{1,0:T(8,128)(2,1)S(1)}, bf16[128,512]{1,0:T(8,128)(2,1)S(1)}, u32[]{:S(2)}, u32[]{:S(2)}) %collective-permute-start.1) | collective-permute-done | bytes 131104 | tf_op jit(solution)/shard_map/ppermute | solution.py:19
  93.6 3.0 %collective-permute-start.2 = (bf16[128,512]{1,0:T(8,128)(2,1)S(1)}, bf16[128,512]{1,0:T(8,128)(2,1)S(1)}, u32[]{:S(2)}, u32[]{:S(2)}) collective-permute-start(bf16[128,512]{1,0:T(8,128)(2,1)S(1)} %add_convert_fusion.1), channel_id=1, source_target_pairs={{0,16},{16,0},{1,17},{17,1},{2,18},{18,2},{3,19},{19,3},{4,20},{20... | collective-permute-start | bytes 393224 | tf_op jit(solution)/shard_map/ppermute | solution.py:19
  96.5 3.6 %collective-permute-done.2 = bf16[128,512]{1,0:T(8,128)(2,1)S(1)} collective-permute-done((bf16[128,512]{1,0:T(8,128)(2,1)S(1)}, bf16[128,512]{1,0:T(8,128)(2,1)S(1)}, u32[]{:S(2)}, u32[]{:S(2)}) %collective-permute-start.2) | collective-permute-done | bytes 131104 | tf_op jit(solution)/shard_map/ppermute | solution.py:19
  100.1 1.1 fusion.12
  101.2 0.1 copy.29
  101.4 0.1 broadcast_in_dim.19
  101.5 16.2 %all_to_all.21 = bf16[8,128,512]{1,2,0:T(8,128)(2,1)S(1)} all-to-all(bf16[8,128,512]{1,2,0:T(8,128)(2,1)S(1)} %broadcast_in_dim.19), channel_id=1, replica_groups=mesh['x'=4,'yh'=2,'z'=4,'yl'=2,'c'=2] {'z','yl'}, dimensions={0} | all-to-all | bytes 2097152 | tf_op jit(solution)/shard_map/all_to_all | solution.py:174
  117.7 0.0 collective-permute-start.3
  117.8 2.8 %collective-permute-done.3 = bf16[8,128,512]{1,2,0:T(8,128)(2,1)} collective-permute-done((bf16[8,128,512]{1,2,0:T(8,128)(2,1)S(1)}, bf16[8,128,512]{1,2,0:T(8,128)(2,1)}, u32[]{:S(2)}, u32[]{:S(2)}) %collective-permute-start.3) | collective-permute-done | bytes 1048608 | tf_op jit(solution)/shard_map/ppermute | solution.py:19
  120.5 1.4 select_bitcast_fusion.1
  121.9 1.5 pad_maximum_fusion
  123.4 1.1 multiply_reduce_fusion
  124.5 9.2 %fusion = bf16[8192,128]{0,1:T(8,128)(2,1)} fusion(bf16[256,8192]{1,0:T(8,128)(2,1)} %param.35, bf16[16,512,256]{2,1,0:T(8,128)(2,1)} %bitcast.124, bf16[16,128,512]{1,2,0:T(8,128)(2,1)} %bitcast.120, f32[16,512]{1,0:T(8,128)S(1)} %reshape.422, f32[128]{0:T(128)S(1)} %add_rsqrt_fusion), kind=kOutput, calls=%fused_computation.1 | convolution fusion | flops 1079083008 | bytes 12616192 | tf_op jit(solution)/shard_map/dot_general | solution.py:204
  133.7 4.1 %copy.32 = bf16[8192,128]{1,0:T(8,128)(2,1)} copy(bf16[8192,128]{0,1:T(8,128)(2,1)} %fusion) | data formatting | bytes 4194304 | tf_op jit(solution)/shard_map/convert_element_type | solution.py:206
  137.8 1.3 dynamic-slice_bitcast_fusion
  139.1 0.2 collective-permute-start.4
  139.3 2.6 %collective-permute-done.4 = bf16[64,64,128]{2,1,0:T(8,128)(2,1)} collective-permute-done((bf16[64,64,128]{2,1,0:T(8,128)(2,1)S(1)}, bf16[64,64,128]{2,1,0:T(8,128)(2,1)}, u32[]{:S(2)}, u32[]{:S(2)}) %collective-permute-start.4) | collective-permute-done | bytes 1048608 | tf_op jit(solution)/shard_map/ppermute | solution.py:19
  142.0 2.9 %fusion.7 = bf16[64,64,128]{2,1,0:T(8,128)(2,1)} fusion(bf16[64,64,128]{2,1,0:T(8,128)(2,1)} %collective-permute-done.4, bf16[64,2,64,128]{3,2,1,0:T(8,128)(2,1)} %bitcast.123, s32[]{:T(128)S(6)} %select_n.59), kind=kLoop, calls=%fused_computation.16 | loop fusion | flops 2097152 | bytes 3145732 | tf_op jit(solution)/shard_map/convert_element_type | solution.py:212
  144.9 7.9 %all-to-all-start.3 = ((bf16[64,64,128]{2,1,0:T(8,128)(2,1)}), bf16[64,64,128]{2,1,0:T(8,128)(2,1)S(1)}, u32[]{:S(2)}, u32[]{:S(2)}) async-start(bf16[64,64,128]{2,1,0:T(8,128)(2,1)} %fusion.7), calls=%async_computation.3 | async-start | bytes 2097152 | tf_op jit(solution)/shard_map/all_to_all | solution.py:215
  152.9 6.0 %fusion.1 = bf16[8,32,64,128]{3,2,1,0:T(8,128)(2,1)} fusion(bf16[8,32,64,128]{3,2,1,0:T(8,128)(2,1)} %param.30, f32[8,128]{1,0:T(8,128)S(1)} %get-tuple-element.9, f32[8,32,64]{2,1,0:T(8,128)S(1)} %broadcast_multiply_fusion, f32[8,32]{1,0:T(8,128)S(1)} %get-tuple-element.5), kind=kLoop, calls=%fused_computation.3 | loop fusion | flops 10485760 | bytes 8459264 | tf_op jit(solution)/shard_map/convert_element_type | solution.py:72
  158.9 0.7 multiply_convert_fusion.12
  159.6 12.3 %all-to-all-done.3 = bf16[64,64,128]{2,1,0:T(8,128)(2,1)S(1)} async-done(((bf16[64,64,128]{2,1,0:T(8,128)(2,1)}), bf16[64,64,128]{2,1,0:T(8,128)(2,1)S(1)}, u32[]{:S(2)}, u32[]{:S(2)}) %all-to-all-start.3) | async-done | bytes 1048608 | tf_op jit(solution)/shard_map/all_to_all | solution.py:215
  172.0 0.2 convert_reduce_fusion.1
  172.1 1.3 fusion.42
  (40 shorter events, 0.3 us)
Async XLA Ops:
  0.6 81.1 %copy-start = (bf16[1,2048,512]{2,1,0:T(8,128)(2,1)S(1)}, bf16[1,2048,512]{2,1,0:T(8,128)(2,1)}, u32[]{:S(2)}) copy-start(bf16[1,2048,512]{2,1,0:T(8,128)(2,1)} %param.32) | copy-start | bytes 6291460
  3.7 22.7 %copy-start.8 = (s32[128]{0:T(128)}, s32[128]{0:T(128)S(1)}, u32[]{:S(2)}) copy-start(s32[128]{0:T(128)S(1)} %convert_reduce_fusion.2) | copy-start | bytes 1540
  15.8 10.6 %copy-start.10 = (s32[128]{0:T(128)S(1)}, s32[128]{0:T(128)}, u32[]{:S(2)}) copy-start(s32[128]{0:T(128)} %param.20) | copy-start | bytes 1540
  15.8 10.8 %copy-start.12 = (f32[32]{0:T(128)S(1)}, f32[32]{0:T(128)}, u32[]{:S(2)}) copy-start(f32[32]{0:T(128)} %param.26) | copy-start | bytes 388
  15.8 11.4 %copy-start.7 = (bf16[1,2048]{1,0:T(2,128)(2,1)S(1)}, bf16[1,2048]{1,0:T(2,128)(2,1)}, u32[]{:S(2)}) copy-start(bf16[1,2048]{1,0:T(2,128)(2,1)} %param.31) | copy-start | bytes 12292
  15.8 11.4 %copy-start.2 = (bf16[5,1,2304]{2,0,1:T(8,128)(2,1)S(1)}, bf16[5,1,2304]{2,0,1:T(8,128)(2,1)}, u32[]{:S(2)}) copy-start(bf16[5,1,2304]{2,0,1:T(8,128)(2,1)} %param.28) | copy-start | bytes 69124
  18.8 25.6 %copy-start.1 = (bf16[8,3,1,2304]{3,0,2,1:T(8,128)(2,1)S(1)}, bf16[8,3,1,2304]{3,0,2,1:T(8,128)(2,1)}, u32[]{:S(2)}) copy-start(bf16[8,3,1,2304]{3,0,2,1:T(8,128)(2,1)} %param.29) | copy-start | bytes 331780
  19.9 24.2 %all-to-all-start = ((bf16[16,8,4384]{2,1,0:T(8,128)(2,1)}), bf16[16,8,4384]{2,1,0:T(8,128)(2,1)S(1)}, u32[]{:S(2)}, u32[]{:S(2)}) async-start(bf16[16,8,4384]{2,1,0:T(8,128)(2,1)} %pad_maximum_fusion.1), calls=%async_computation | async-start | bytes 2293760 | tf_op jit(solution)/shard_map/all_to_all | solution.py:132
  44.3 1.0 copy-start.3
  46.3 21.4 %copy-start.11 = (f32[32]{0:T(128)S(1)}, f32[32]{0:T(128)}, u32[]{:S(2)}) copy-start(f32[32]{0:T(128)} %param.27) | copy-start | bytes 388
  67.7 32.4 %copy-start.9 = (s32[128]{0:T(128)S(1)}, s32[128]{0:T(128)}, u32[]{:S(2)}) copy-start(s32[128]{0:T(128)} %copy-done.8) | copy-start | bytes 1540
  68.2 49.5 %copy-start.6 = (bf16[8192]{0:T(1024)(128)(2,1)S(1)}, bf16[8192]{0:T(1024)(128)(2,1)}, u32[]{:S(2)}) copy-start(bf16[8192]{0:T(1024)(128)(2,1)} %param.33) | copy-start | bytes 49156
  82.2 5.0 %collective-permute-start = (bf16[128,512]{1,0:T(8,128)(2,1)S(1)}, bf16[128,512]{1,0:T(8,128)(2,1)S(1)}, u32[]{:S(2)}, u32[]{:S(2)}) collective-permute-start(bf16[128,512]{1,0:T(8,128)(2,1)S(1)} %fusion.13), channel_id=1, source_target_pairs={{0,32},{32,0},{64,96},{96,64},{1,33},{33,1},{65,97},{97,65},{2,34}... | collective-permute-start | bytes 393224 | tf_op jit(solution)/shard_map/ppermute | solution.py:19
  87.3 6.3 %collective-permute-start.1 = (bf16[128,512]{1,0:T(8,128)(2,1)S(1)}, bf16[128,512]{1,0:T(8,128)(2,1)S(1)}, u32[]{:S(2)}, u32[]{:S(2)}) collective-permute-start(bf16[128,512]{1,0:T(8,128)(2,1)S(1)} %add_convert_fusion.2), channel_id=1, source_target_pairs={{0,96},{32,64},{64,32},{96,0},{1,97},{33,65},{65,33},{97,1},{2,98}... | collective-permute-start | bytes 393224 | tf_op jit(solution)/shard_map/ppermute | solution.py:19
  93.6 6.6 %collective-permute-start.2 = (bf16[128,512]{1,0:T(8,128)(2,1)S(1)}, bf16[128,512]{1,0:T(8,128)(2,1)S(1)}, u32[]{:S(2)}, u32[]{:S(2)}) collective-permute-start(bf16[128,512]{1,0:T(8,128)(2,1)S(1)} %add_convert_fusion.1), channel_id=1, source_target_pairs={{0,16},{16,0},{1,17},{17,1},{2,18},{18,2},{3,19},{19,3},{4,20},{20... | collective-permute-start | bytes 393224 | tf_op jit(solution)/shard_map/ppermute | solution.py:19
  117.7 2.8 %collective-permute-start.3 = (bf16[8,128,512]{1,2,0:T(8,128)(2,1)S(1)}, bf16[8,128,512]{1,2,0:T(8,128)(2,1)}, u32[]{:S(2)}, u32[]{:S(2)}) collective-permute-start(bf16[8,128,512]{1,2,0:T(8,128)(2,1)S(1)} %all_to_all.21), channel_id=1, source_target_pairs={{0,1},{1,0},{2,3},{3,2},{4,5},{5,4},{6,7},{7,6},{8,9},{9,8},{10,11... | collective-permute-start | bytes 3145736 | tf_op jit(solution)/shard_map/ppermute | solution.py:19
  133.7 5.6 %copy-start.5 = (f32[8,4]{0,1:T(4,128)S(1)}, f32[8,4]{0,1:T(4,128)}, u32[]{:S(2)}) copy-start(f32[8,4]{0,1:T(4,128)} %fusion.46) | copy-start | bytes 388
  139.1 2.9 %collective-permute-start.4 = (bf16[64,64,128]{2,1,0:T(8,128)(2,1)S(1)}, bf16[64,64,128]{2,1,0:T(8,128)(2,1)}, u32[]{:S(2)}, u32[]{:S(2)}) collective-permute-start(bf16[64,64,128]{2,1,0:T(8,128)(2,1)S(1)} %dynamic-slice_bitcast_fusion), channel_id=1, source_target_pairs={{0,1},{1,0},{2,3},{3,2},{4,5},{5,4},{6,7},{7,6},{8,9},{9,8},{10,11... | collective-permute-start | bytes 3145736 | tf_op jit(solution)/shard_map/ppermute | solution.py:19
  144.9 27.0 %all-to-all-start.3 = ((bf16[64,64,128]{2,1,0:T(8,128)(2,1)}), bf16[64,64,128]{2,1,0:T(8,128)(2,1)S(1)}, u32[]{:S(2)}, u32[]{:S(2)}) async-start(bf16[64,64,128]{2,1,0:T(8,128)(2,1)} %fusion.7), calls=%async_computation.3 | async-start | bytes 2097152 | tf_op jit(solution)/shard_map/all_to_all | solution.py:215
  152.9 6.0 %copy-start.4 = (bf16[8,1,128]{2,0,1:T(8,128)(2,1)S(1)}, bf16[8,1,128]{2,0,1:T(8,128)(2,1)}, u32[]{:S(2)}) copy-start(bf16[8,1,128]{2,0,1:T(8,128)(2,1)} %copy-done.3) | copy-start | bytes 6148

commit v2 on v1

v2 whole, which is shorter than its diff:
```python
import jax
import jax.numpy as jnp
from jax import lax
from jax.experimental import pallas as pl
from jax.experimental.pallas import tpu as pltpu
from jax.sharding import Mesh, PartitionSpec as P

EPS = 1e-05
GRP = ("x", "yh")
HEAD = ("z", "yl", "c")
CHIPS = ("x", "yh", "z", "yl")
NEAR = ("z", "yl")
F32 = jnp.float32
BF16 = jnp.bfloat16
HBM = pl.BlockSpec(memory_space=pltpu.HBM)
ANY = pl.BlockSpec(memory_space=pl.ANY)
VMEM = pl.BlockSpec(memory_space=pltpu.VMEM)
SMEM = pl.BlockSpec(memory_space=pltpu.SMEM)
LANES = 128


def swap(value, axis, bit):
    size = lax.axis_size(axis)
    return lax.ppermute(value, axis, [(i, i ^ bit) for i in range(size)])


def add(left, right):
    return (left.astype(F32) + right.astype(F32)).astype(BF16)


def params(mib):
    return pltpu.CompilerParams(vmem_limit_bytes=mib << 20)


def contract(left, right, left_dim, right_dim):
    return lax.dot_general(
        left, right, (((left_dim,), (right_dim,)), ((), ())), preferred_element_type=F32
    )


def split3(values):
    high = values.astype(BF16)
    rest = values - high.astype(F32)
    middle = rest.astype(BF16)
    low = (rest - middle.astype(F32)).astype(BF16)
    return high, middle, low


def prepare_kernel(
    place,
    hidden,
    owner,
    history,
    gain,
    weights,
    tiles,
    pairs,
    plain,
    order,
    past,
    held,
    gains,
    sems,
    hidden_sems,
):
    head = place[0]
    core = place[1]
    count = tiles.shape[0]
    rows, width = hidden.shape
    part = plain.shape[1]
    blocks = width // part
    own_rows = rows // blocks
    loads = [
        pltpu.make_async_copy(
            hidden.at[:, pl.ds(i * part, part)], held.at[i], hidden_sems.at[i]
        )
        for i in range(blocks)
    ]
    copies = [
        pltpu.make_async_copy(weights.at[:, i], tiles.at[i], sems.at[i]) for i in range(count)
    ]
    for copy in loads + copies:
        copy.start()
    gains[...] = gain[...].astype(F32)
    position = lax.broadcasted_iota(jnp.int32, (rows, rows), 1)
    key = (owner[...] * rows + position).astype(F32)
    before = (key.T < key).astype(F32)
    rank = jnp.sum(before, axis=0, keepdims=True)
    slot = lax.broadcasted_iota(jnp.int32, (rows, rows), 0)
    to_slot = jnp.where(rank == slot.astype(F32), 1.0, 0.0)
    slot_history = jnp.sum(to_slot * history[...].astype(F32), axis=1, keepdims=True)
    past[...] = jnp.broadcast_to(slot_history, (rows, LANES))
    half = rows // 2
    near = slot < half
    inner = jnp.where(near, slot, slot - half)
    shift = jnp.where(near, core, 1 - core) * own_rows
    sent = (inner // own_rows) * (2 * own_rows) + lax.rem(inner, own_rows) + shift
    order[...] = jnp.where(rank == sent.astype(F32), 1.0, 0.0).astype(BF16)
    squares = jnp.zeros((rows, LANES), F32)
    for i in range(blocks):
        loads[i].wait()
        for q in range(part // LANES):
            chunk = held[i, :, q * LANES : (q + 1) * LANES].astype(F32)
            squares += chunk * chunk
    scale = lax.rsqrt(jnp.sum(squares, axis=1, keepdims=True) / width + EPS)
    normed = []
    for q in range(part // LANES):
        chunk = held[head, :, q * LANES : (q + 1) * LANES].astype(F32)
        row = gains[pl.ds(head * (part // LANES) + q, 1), :]
        normed.append((chunk * scale * row).astype(BF16))
    ordered = jnp.dot(
        order[...], jnp.concatenate(normed, axis=1), preferred_element_type=F32
    ).astype(BF16)
    plain[...] = ordered
    source = lax.broadcasted_iota(jnp.int32, (part, 2 * part), 0)
    target = lax.broadcasted_iota(jnp.int32, (part, 2 * part), 1)
    for which in range(2):
        spread = jnp.where(target == 2 * source + which, 1.0, 0.0).astype(BF16)
        pairs[which * rows : (which + 1) * rows, :] = jnp.dot(
            ordered, spread, preferred_element_type=F32
        ).astype(BF16)
    for copy in copies:
        copy.wait()


def project_kernel(pairs, plain, tiles, select, step, keep, give):
    count = tiles.shape[0]
    rows = plain.shape[0]
    half = rows // 2
    left = pairs[...]

    def put(at, values):
        width = values.shape[1]
        for out, part in ((keep, values[:half]), (give, values[half:])):
            out[:, :, at : at + width] = part.reshape(out.shape[0], out.shape[1], width).astype(BF16)

    for i in range(0, count, 2):
        right = jnp.concatenate([tiles[i], tiles[i + 1]], axis=1)
        both = jnp.dot(left, right, preferred_element_type=F32)
        put(i * LANES, both[:rows])
        put((count + i) * LANES, both[rows:])
    both = jnp.dot(left, select[...], preferred_element_type=F32)
    at = 2 * count * LANES
    put(at, both[:rows])
    put(at + LANES, both[rows:])
    steps = contract(plain[...], step[...], 1, 1)
    missing = LANES - steps.shape[1]
    put(at + 2 * LANES, jnp.concatenate([steps, jnp.zeros((rows, missing), F32)], axis=1))


def mixer_kernel(
    place,
    pieces,
    past,
    window,
    taps,
    bias,
    decay_log,
    skip,
    gain,
    state,
    mixed,
    window_next,
    inputs_step,
    in_coef,
    decay,
    held,
    sems,
):
    senders, own, _ = pieces.shape
    channels = mixed.shape[1]
    heads = bias.shape[1]
    width = channels // heads
    copies = [pltpu.make_async_copy(state.at[s], held.at[s], sems.at[s]) for s in range(own)]
    for copy in copies:
        copy.start()
    total = pieces[0].astype(F32)
    for i in range(1, senders):
        total += pieces[i].astype(F32)
    gate = total[:, :channels]
    fresh = total[:, channels : 2 * channels + 2 * LANES].astype(BF16).astype(F32)
    step_raw = total[:, 2 * channels + 2 * LANES : 2 * channels + 2 * LANES + heads]
    valid = past[pl.ds(pl.multiple_of(place[0] * own, own), own), 0:1]
    lags = window.shape[0]
    entries = []
    for k in range(lags):
        mask = jnp.where(valid >= lags - k, 1.0, 0.0)
        entries.append(window[k].astype(F32) * mask)
    entries.append(fresh)
    weights = taps[...].astype(F32)
    conv = weights[lags + 1 : lags + 2]
    for k in range(lags + 1):
        conv = conv + entries[k] * weights[k : k + 1]
    for k in range(lags):
        window_next[k] = entries[k + 1].astype(BF16)
    active = conv * (1.0 / (1.0 + jnp.exp(-conv)))
    u = active[:, :channels]
    b = active[:, channels : channels + LANES]
    c = active[:, channels + LANES :]
    shifted = step_raw + bias[...]
    step = jnp.maximum(shifted, 0.0) + jnp.log1p(jnp.exp(-jnp.abs(shifted)))
    rate = jnp.exp(-step * jnp.exp(decay_log[...]))
    both = jnp.sum(b * c, axis=1, keepdims=True)
    direct = step * both + skip[...]
    head_of = lax.broadcasted_iota(jnp.int32, (heads, channels), 0)
    channel = lax.broadcasted_iota(jnp.int32, (heads, channels), 1)
    first = head_of * width
    spread = jnp.where((channel >= first) & (channel < first + width), 1.0, 0.0).astype(BF16)
    stacked = jnp.concatenate([rate, step, direct], axis=0)
    wide = sum(jnp.dot(part, spread, preferred_element_type=F32) for part in split3(stacked))
    rate_wide = wide[:own]
    step_wide = wide[own : 2 * own]
    direct_wide = wide[2 * own :]
    inputs_step[...] = step_wide * u
    in_coef[...] = b
    decay[...] = rate
    c_high = c.astype(BF16)
    c_low = (c - c_high.astype(F32)).astype(BF16)
    coefs = jnp.concatenate([c_high, c_low], axis=0)
    row = lax.broadcasted_iota(jnp.int32, (own, channels), 0)
    read = jnp.zeros((own, channels), F32)
    for s in range(own):
        copies[s].wait()
        found = contract(coefs, held[s], 1, 1)
        read = jnp.where(row == s, found[:own] + found[own:], read)
    gated = (rate_wide * read + direct_wide * u) * (gate * (1.0 / (1.0 + jnp.exp(-gate))))
    scale = lax.rsqrt(jnp.sum(gated * gated, axis=1, keepdims=True) / channels + EPS)
    mixed[...] = (gated * scale * gain[...].astype(F32)).astype(BF16)


def ffn_kernel(
    place, near, far, gain, up, down, keep, give, slice_out, up_held, down_held, turned, gains, sems
):
    core = place[1]
    flat = place[2]
    chunks, rows, part = near.shape
    hidden = up.shape[2]
    model = 2 * chunks * part
    piece = keep.shape[1]
    ups = [pltpu.make_async_copy(up.at[k], up_held.at[k], sems.at[0, k]) for k in range(2 * chunks)]
    downs = [
        pltpu.make_async_copy(
            down.at[:, pl.ds(k * part, part)], down_held.at[k], sems.at[1, k]
        )
        for k in range(2 * chunks)
    ]
    for copy in ups + downs:
        copy.start()
    gains[...] = gain[...].astype(F32)
    squares = jnp.zeros((rows, LANES), F32)
    total = jnp.zeros((rows, hidden), F32)
    lanes = part // LANES
    for j in range(chunks):
        ups[2 * j].wait()
        ups[2 * j + 1].wait()
        for source, which in ((near, core), (far, 1 - core)):
            scaled = []
            for q in range(lanes):
                chunk = source[j, :, q * LANES : (q + 1) * LANES].astype(F32)
                squares += chunk * chunk
                row = gains[pl.ds((2 * j + which) * lanes + q, 1), :]
                scaled.append((chunk * row).astype(BF16))
            total += jnp.dot(
                jnp.concatenate(scaled, axis=1),
                up_held[2 * j + which],
                preferred_element_type=F32,
            )
    scale = lax.rsqrt(jnp.sum(squares, axis=1, keepdims=True) / model + EPS)
    raised = jnp.maximum(total * scale, 0.0)
    squared = (raised * raised).astype(BF16)
    per_part = part // piece
    owner = flat // per_part
    mine = near[owner // 2].astype(F32)
    other = far[owner // 2].astype(F32)
    turned[...] = jnp.where(lax.rem(owner, 2) == core, mine, other).T
    slice_out[...] = turned[pl.ds(pl.multiple_of(lax.rem(flat, per_part) * piece, piece), piece), :]
    for k in range(2 * chunks):
        downs[k].wait()
        out = jnp.dot(squared, down_held[k], preferred_element_type=F32).astype(BF16).T
        for q in range(part // (2 * piece)):
            low = out[2 * q * piece : (2 * q + 1) * piece]
            high = out[(2 * q + 1) * piece : (2 * q + 2) * piece]
            chip = k * (part // (2 * piece)) + q
            keep[chip] = jnp.where(core == 0, low, high)
            give[chip] = jnp.where(core == 0, high, low)


def local(
    hidden_in,
    row_owner,
    history_len,
    pre_gain,
    inner_proj,
    select_proj,
    step_proj,
    step_bias,
    decay_log,
    skip_gain,
    conv_taps,
    conv_window,
    state_cache,
    mixer_gain,
    output_proj,
    channel_gain,
    up_weight,
    down_weight,
):
    rows, model = hidden_in.shape
    heads_axis = lax.axis_size(HEAD)
    groups_axis = lax.axis_size(GRP)
    own = rows // heads_axis
    part = model // heads_axis
    channels = mixer_gain.shape[1]
    heads = step_proj.shape[1]
    state_size = state_cache.shape[3]
    head_width = state_cache.shape[2]
    taps = conv_taps.shape[0]
    conv_width = conv_taps.shape[2]
    hidden_units = up_weight.shape[1]
    tile_count = channels // LANES
    head_index = lax.axis_index(HEAD)
    group_index = lax.axis_index(GRP)
    core = lax.axis_index("c")
    flat_index = group_index * heads_axis + head_index
    place = jnp.stack([head_index, core, flat_index]).astype(jnp.int32)
    shape = jax.ShapeDtypeStruct

    tiled = inner_proj.reshape(part, 2, tile_count, LANES).transpose(0, 2, 1, 3)
    tiles, pairs, plain, order, past = pl.pallas_call(
        prepare_kernel,
        out_shape=(
            shape((tile_count, part, 2, LANES), BF16),
            shape((2 * rows, 2 * part), BF16),
            shape((rows, part), BF16),
            shape((rows, rows), BF16),
            shape((rows, LANES), F32),
        ),
        in_specs=[SMEM, HBM, VMEM, VMEM, VMEM, HBM],
        out_specs=(ANY, VMEM, VMEM, VMEM, VMEM),
        scratch_shapes=[
            pltpu.VMEM((heads_axis, rows, part), BF16),
            pltpu.VMEM((model // LANES, LANES), F32),
            pltpu.SemaphoreType.DMA((tile_count,)),
            pltpu.SemaphoreType.DMA((heads_axis,)),
        ],
        compiler_params=params(16),
    )(
        place,
        hidden_in,
        row_owner.reshape(1, rows),
        history_len.reshape(1, rows),
        pre_gain.reshape(model // LANES, LANES),
        tiled,
    )
    sent_width = 2 * channels + 2 * state_size + LANES
    near_owners = heads_axis // 2
    keep, give = pl.pallas_call(
        project_kernel,
        out_shape=(shape((near_owners, own, sent_width), BF16),) * 2,
        in_specs=[VMEM] * 5,
        out_specs=(VMEM,) * 2,
        compiler_params=params(16),
    )(
        pairs,
        plain,
        tiles.reshape(tile_count, 2 * part, LANES),
        select_proj.reshape(2 * part, state_size),
        step_proj.T,
    )
    chip_terms = add(keep, swap(give, "c", 1))
    pieces = lax.all_to_all(chip_terms, NEAR, split_axis=0, concat_axis=0, tiled=True)
    mixed_own, window_next, inputs_step, in_coef, decay = pl.pallas_call(
        mixer_kernel,
        out_shape=(
            shape((own, channels), BF16),
            shape((taps - 2, own, conv_width), BF16),
            shape((own, channels), F32),
            shape((own, state_size), F32),
            shape((own, heads), F32),
        ),
        in_specs=[SMEM] + [VMEM] * 8 + [ANY],
        out_specs=(VMEM,) * 5,
        scratch_shapes=[
            pltpu.VMEM((own, heads * head_width, state_size), BF16),
            pltpu.SemaphoreType.DMA((own,)),
        ],
        compiler_params=params(16),
    )(
        place,
        pieces,
        past,
        conv_window.transpose(1, 2, 0, 3).reshape(taps - 2, own, conv_width),
        conv_taps.reshape(taps, conv_width),
        step_bias.reshape(1, heads),
        decay_log.reshape(1, heads),
        skip_gain.reshape(1, heads),
        mixer_gain,
        state_cache.reshape(own, heads * head_width, state_size),
    )
    near_mix = lax.all_to_all(
        jnp.broadcast_to(mixed_own[None], (near_owners, own, channels)),
        NEAR,
        split_axis=0,
        concat_axis=0,
        tiled=True,
    )
    far_mix = swap(near_mix, "c", 1)
    out_weight = output_proj.reshape(channels, part)
    mixed = jnp.concatenate(
        [
            jnp.dot(mix.reshape(rows // 2, channels), out_weight, preferred_element_type=F32)
            for mix in (near_mix, far_mix)
        ]
    ).astype(BF16)
    for axis, bit in (("x", 1), ("x", 3), ("yh", 1)):
        mixed = add(mixed, swap(mixed, axis, bit))
    base_cols = lax.dynamic_slice_in_dim(hidden_in, head_index * part, part, 1).astype(F32)
    mixed_rows = contract(order, mixed, 0, 0)
    hidden_piece = (base_cols + mixed_rows).astype(BF16)
    near = lax.all_to_all(
        jnp.broadcast_to(hidden_piece[None], (heads_axis // 2,) + hidden_piece.shape),
        NEAR,
        split_axis=0,
        concat_axis=0,
        tiled=True,
    )
    far = swap(near, "c", 1)
    chips = groups_axis * heads_axis // 2
    piece = model // (groups_axis * heads_axis)
    keep, give, residual_slice = pl.pallas_call(
        ffn_kernel,
        out_shape=(
            shape((chips, piece, rows), BF16),
            shape((chips, piece, rows), BF16),
            shape((piece, rows), F32),
        ),
        in_specs=[SMEM, VMEM, VMEM, VMEM, HBM, HBM],
        out_specs=(VMEM,) * 3,
        scratch_shapes=[
            pltpu.VMEM((heads_axis, part, hidden_units), BF16),
            pltpu.VMEM((heads_axis, hidden_units, part), BF16),
            pltpu.VMEM((part, rows), F32),
            pltpu.VMEM((model // LANES, LANES), F32),
            pltpu.SemaphoreType.DMA((2, heads_axis)),
        ],
        compiler_params=params(24),
    )(
        place,
        near,
        far,
        channel_gain.reshape(model // LANES, LANES),
        up_weight.reshape(heads_axis, part, hidden_units),
        down_weight,
    )
    chip_sum = add(keep, swap(give, "c", 1))
    spread = lax.all_to_all(chip_sum, CHIPS, split_axis=0, concat_axis=0, tiled=True)
    block_out = (residual_slice + jnp.sum(spread.astype(F32), axis=0)).astype(BF16).T
    step_input = inputs_step.reshape(own, heads, head_width)
    state_next = (
        decay[..., None, None] * state_cache.astype(F32)
        + step_input[..., None] * in_coef[:, None, None, :]
    ).astype(BF16)
    window_out = window_next.reshape(taps - 2, 1, own, conv_width).transpose(2, 0, 1, 3)
    return (block_out, state_next, window_out)


def solution(mesh):
    fine = Mesh(mesh.devices.reshape(4, 2, 4, 2, 2), ("x", "yh", "z", "yl", "c"))
    placed = (
        P(),
        P(),
        P(),
        P(),
        P(HEAD, None, GRP),
        P(HEAD, None, GRP),
        P(HEAD, GRP),
        P(GRP),
        P(GRP),
        P(GRP),
        P(None, GRP, None),
        P(HEAD, None, GRP, None),
        P(HEAD, GRP, None, None),
        P(GRP, None),
        P(GRP, None, HEAD),
        P(),
        P(None, GRP + HEAD),
        P(GRP + HEAD, None),
    )
    return jax.shard_map(
        local,
        mesh=fine,
        in_specs=placed,
        out_specs=(
            P(None, GRP + HEAD),
            P(HEAD, GRP, None, None),
            P(HEAD, None, GRP, None),
        ),
        check_vma=False,
    )
```

time: 175 us -> 131 us (0.75)
  matrix products: 37.4 us -> 2.06 us
  Pallas kernels: 0 us -> 18.1 us
  other arithmetic: 23.8 us -> 8.55 us
  blocking collectives: 29.7 us -> 42.6 us
  waiting for transfers between devices: 43.9 us -> 32.2 us
  starting transfers between devices: 22.1 us -> 15.6 us
  local copies, waits for them, and re-layouts: 15.7 us -> 10.6 us
    dot_general x8 -> x3, matrix products: 37.4 us -> 2.06 us  [the longest x1 1.11 us: contract(): lax.dot_general(left, right, (((left_dim,), (right_dim,)), ((), ())), pre...]
    pallas_call x0 -> x4, Pallas kernels: none -> 18.1 us  [the longest x1 7.37 us: local(): pl.pallas_call(ffn_kernel, out_shape=(shape((chips, piece, rows), BF16),...]
    all_to_all x1 -> x0, waiting for transfers between devices: 15.7 us -> none  [local(): lax.all_to_all(terms.reshape(head_devices, own_rows, -1), HEAD, split_axi...]
    all_to_all x2 -> x3, blocking collectives: 29.7 us -> 42.6 us  [the longest x1 17.3 us: local(): lax.all_to_all(chip_terms, NEAR, split_axis=0, concat_axis=0, tiled=True)]
    unnamed x26 -> x36, local copies, waits for them, and re-layouts: 0.06 us -> 10.4 us
    reshape x4 -> x0, local copies, waits for them, and re-layouts: 9.09 us -> none  [the longest x1 7.77 us: local(): inner_flat = inner_proj.reshape(slice_width, -1)]
    all_to_all x1 -> x0, starting transfers between devices: 6.51 us -> none  [local(): lax.all_to_all(terms.reshape(head_devices, own_rows, -1), HEAD, split_axi...]
    convert_element_type x2 -> x0, local copies, waits for them, and re-layouts: 4.2 us -> none  [the longest x1 4.08 us: local(): down_terms = lax.dot_general(down_weight, squared, (((0,), (1,)), ((), ()...]
  transfers between devices with their start and end apart: 7 -> 8, of which waited for: 7 -> 8; matrix products, arithmetic and copies ran while one was open for 5% -> 5% of each run, Pallas kernels for 0% -> 0%
where the time goes in v2:
time: 131 us
  blocking collectives  42.6 us (33%)
  waiting for transfers between devices  32.2 us (25%)
  Pallas kernels  18.1 us (14%)
  starting transfers between devices  15.6 us (12%)
  local copies, waits for them, and re-layouts  10.6 us (8%)
  other arithmetic  8.55 us (7%)
  matrix products  2.06 us (2%)
    ppermute x7, waiting for transfers between devices, swap(): return lax.ppermute(value, axis, [(i, i ^ bit) for i in range(size)])  19.2 us
    all_to_all x1, blocking collectives, local(): lax.all_to_all(chip_terms, NEAR, split_axis=0, concat_axis=0, tiled=True)  17.3 us
    all_to_all x1, blocking collectives, local(): lax.all_to_all(jnp.broadcast_to(hidden_piece[None], (heads_axis // 2,) +...  15.6 us
    all_to_all x1, waiting for transfers between devices, local(): lax.all_to_all(chip_sum, CHIPS, split_axis=0, concat_axis=0, tiled=True)  13 us
    unnamed x36, local copies, waits for them, and re-layouts  10.4 us
    all_to_all x1, blocking collectives, local(): lax.all_to_all(jnp.broadcast_to(mixed_own[None], (near_owners, own, chann...  9.7 us
    all_to_all x1, starting transfers between devices, local(): lax.all_to_all(chip_sum, CHIPS, split_axis=0, concat_axis=0, tiled=True)  7.93 us
    ppermute x7, starting transfers between devices, swap(): return lax.ppermute(value, axis, [(i, i ^ bit) for i in range(size)])  7.71 us
  transfers between devices with their start and end apart: 8, of which 8 were waited for; matrix products, arithmetic and copies ran while one was open for 5% of the time, Pallas kernels for 0%

profile of v2, /device:TPU:0, one launch (start us, length us, event | category | flops | bytes accessed | tf_op | source)
XLA Modules:
  0.0 130.5 jit_solution(1364604790546612690)
XLA Ops:
  0.6 0.0 copy-start
  0.7 0.1 pad_add_fusion.place
  0.7 0.0 copy-start.2
  0.7 2.3 %copy-done.2 = bf16[512,2,2048]{2,1,0:T(2,128)(2,1)S(1)} copy-done((bf16[512,2,2048]{2,1,0:T(2,128)(2,1)S(1)}, bf16[512,2,2048]{2,1,0:T(2,128)(2,1)}, u32[]{:S(2)}) %copy-start.2) | copy-done | bytes 4194328
  3.1 0.0 copy-start.5
  3.1 1.6 %copy-done.5 = bf16[128,8192]{1,0:T(8,128)(2,1)S(1)} copy-done((bf16[128,8192]{1,0:T(8,128)(2,1)S(1)}, bf16[128,8192]{1,0:T(8,128)(2,1)}, u32[]{:S(2)}) %copy-start.5) | copy-done | bytes 2097176
  4.6 0.0 copy-start.10
  4.6 0.7 copy-done.10
  5.4 0.7 copy-done.13
  6.0 0.7 copy-done.14
  6.7 5.5 %shard_map.193 = (bf16[16,512,2,128]{3,2,1,0:T(2,128)(2,1)S(1)}, bf16[256,1024]{1,0:T(8,128)(2,1)S(1)}, bf16[128,512]{1,0:T(8,128)(2,1)S(1)}, bf16[128,128]{1,0:T(8,128)(2,1)S(1)}, f32[128,128]{1,0:T(8,128)S(1)}) custom-call(s32[3]{0:T(128)S(1)} %pad_add_fusion.place, bf16[128,8192]{1,0:T(8,128)(2,1)S(1)} %copy-done.5, s32[1,128]{1,0:T(1,128)S(1)} %bitcast.57, ...), custom_call_target="tpu_custom_call" | custom-call | tf_op jit(solution)/shard_map/pallas_call | solution.py:329
  12.2 0.0 copy-done.6
  12.2 0.0 copy-done.9
  12.2 0.0 copy-start.1
  12.2 1.4 %shard_map.194 = (bf16[8,8,4480]{2,1,0:T(8,128)(2,1)S(1)}, bf16[8,8,4480]{2,1,0:T(8,128)(2,1)S(1)}) custom-call(bf16[256,1024]{1,0:T(8,128)(2,1)S(1)} %get-tuple-element.19.pairs, bf16[128,512]{1,0:T(8,128)(2,1)S(1)} %get-tuple-element.20.plain, bf16[16,1024,128]{2,1,0:T(8,128)(2,1)S(1)} %bitcast.48, bf16[1024,128]{1,0:T(8,128)(2,1)S(1)} %bitcast.51, ...), custom_call_target="tpu_custom_call" | custom-call | tf_op jit(solution)/shard_map/pallas_call | solution.py:357
  13.7 0.0 copy-start.7
  13.7 0.0 copy-start.8
  13.7 0.0 copy-start.12
  13.7 0.0 copy-start.15
  13.7 0.0 copy-start.16
  13.7 0.0 copy-start.17
  13.7 0.1 collective-permute-start
  13.8 2.0 %collective-permute-done = bf16[8,8,4480]{2,1,0:T(8,128)(2,1)S(1)} collective-permute-done((bf16[8,8,4480]{2,1,0:T(8,128)(2,1)S(1)}, bf16[8,8,4480]{2,1,0:T(8,128)(2,1)S(1)}, u32[]{:S(2)}, u32[]{:S(2)}) %collective-permute-start) | collective-permute-done | bytes 573472 | tf_op jit(solution)/shard_map/ppermute | solution.py:24
  15.8 0.1 add_convert_fusion.2
  15.9 17.3 %all_to_all.20.pieces = bf16[8,8,4480]{2,1,0:T(8,128)(2,1)S(1)} all-to-all(bf16[8,8,4480]{2,1,0:T(8,128)(2,1)S(1)} %add_convert_fusion.2), channel_id=1, replica_groups=mesh['x'=4,'yh'=2,'z'=4,'yl'=2,'c'=2] {'z','yl'}, dimensions={0} | all-to-all | bytes 1146880 | tf_op jit(solution)/shard_map/all_to_all | solution.py:371
  33.2 0.0 copy-done.1
  33.2 0.0 copy-done.7
  33.2 0.0 copy-done.8
  33.2 0.0 copy-done.12
  33.2 0.0 copy-done.15
  33.3 0.0 copy-done.16
  33.3 0.0 copy-done.17
  33.3 3.7 %shard_map.195 = (bf16[8,2048]{1,0:T(8,128)(2,1)S(1)}, bf16[3,8,2304]{2,1,0:T(8,128)(2,1)}, f32[8,2048]{1,0:T(8,128)S(1)}, f32[8,128]{1,0:T(8,128)S(1)}, f32[8,32]{1,0:T(8,128)S(1)}) custom-call(s32[3]{0:T(128)S(1)} %pad_add_fusion.place, bf16[8,8,4480]{2,1,0:T(8,128)(2,1)S(1)} %all_to_all.20.pieces, f32[128,128]{1,0:T(8,128)S(1)} %get-tuple-element.24.past, ...), custom_call_target="tpu_custom_call" | custom-call | tf_op jit(solution)/shard_map/pallas_call | solution.py:372
  37.1 9.7 %all_to_all.21 = bf16[8,8,2048]{2,1,0:T(8,128)(2,1)S(1)} all-to-all(bf16[8,8,2048]{2,1,0:T(8,128)(2,1)S(1)} %broadcast_in_dim.4), channel_id=1, replica_groups=mesh['x'=4,'yh'=2,'z'=4,'yl'=2,'c'=2] {'z','yl'}, dimensions={0} | all-to-all | bytes 524288 | tf_op jit(solution)/shard_map/all_to_all | solution.py:400
  46.8 0.0 collective-permute-start.1
  46.8 0.0 copy-done
  46.8 0.5 fusion.5
  47.2 1.0 collective-permute-done.1
  48.3 0.5 fusion.8
  48.8 1.6 %collective-permute-start.2 = (bf16[128,512]{1,0:T(8,128)(2,1)S(1)}, bf16[128,512]{1,0:T(8,128)(2,1)S(1)}, u32[]{:S(2)}, u32[]{:S(2)}) collective-permute-start(bf16[128,512]{1,0:T(8,128)(2,1)S(1)} %pad_maximum_fusion), channel_id=1, source_target_pairs={{0,32},{32,0},{64,96},{96,64},{1,33},{33,1},{65,97},{97,65},{2,34}... | collective-permute-start | bytes 393224 | tf_op jit(solution)/shard_map/ppermute | solution.py:24
  50.4 4.0 %collective-permute-done.2 = bf16[128,512]{1,0:T(8,128)(2,1)S(1)} collective-permute-done((bf16[128,512]{1,0:T(8,128)(2,1)S(1)}, bf16[128,512]{1,0:T(8,128)(2,1)S(1)}, u32[]{:S(2)}, u32[]{:S(2)}) %collective-permute-start.2) | collective-permute-done | bytes 131104 | tf_op jit(solution)/shard_map/ppermute | solution.py:24
  54.4 0.0 copy-start.11
  54.5 2.8 %collective-permute-start.3 = (bf16[128,512]{1,0:T(8,128)(2,1)S(1)}, bf16[128,512]{1,0:T(8,128)(2,1)S(1)}, u32[]{:S(2)}, u32[]{:S(2)}) collective-permute-start(bf16[128,512]{1,0:T(8,128)(2,1)S(1)} %add_convert_fusion.5), channel_id=1, source_target_pairs={{0,96},{32,64},{64,32},{96,0},{1,97},{33,65},{65,33},{97,1},{2,98}... | collective-permute-start | bytes 393224 | tf_op jit(solution)/shard_map/ppermute | solution.py:24
  57.3 3.4 %collective-permute-done.3 = bf16[128,512]{1,0:T(8,128)(2,1)S(1)} collective-permute-done((bf16[128,512]{1,0:T(8,128)(2,1)S(1)}, bf16[128,512]{1,0:T(8,128)(2,1)S(1)}, u32[]{:S(2)}, u32[]{:S(2)}) %collective-permute-start.3) | collective-permute-done | bytes 131104 | tf_op jit(solution)/shard_map/ppermute | solution.py:24
  60.8 3.0 %collective-permute-start.4 = (bf16[128,512]{1,0:T(8,128)(2,1)S(1)}, bf16[128,512]{1,0:T(8,128)(2,1)S(1)}, u32[]{:S(2)}, u32[]{:S(2)}) collective-permute-start(bf16[128,512]{1,0:T(8,128)(2,1)S(1)} %add_convert_fusion.4), channel_id=1, source_target_pairs={{0,16},{16,0},{1,17},{17,1},{2,18},{18,2},{3,19},{19,3},{4,20},{20... | collective-permute-start | bytes 393224 | tf_op jit(solution)/shard_map/ppermute | solution.py:24
  63.7 3.6 %collective-permute-done.4 = bf16[128,512]{1,0:T(8,128)(2,1)S(1)} collective-permute-done((bf16[128,512]{1,0:T(8,128)(2,1)S(1)}, bf16[128,512]{1,0:T(8,128)(2,1)S(1)}, u32[]{:S(2)}, u32[]{:S(2)}) %collective-permute-start.4) | collective-permute-done | bytes 131104 | tf_op jit(solution)/shard_map/ppermute | solution.py:24
  67.3 1.1 fusion.4
  68.4 0.1 broadcast_in_dim.5
  68.5 15.6 %all_to_all.22.near = bf16[8,128,512]{2,1,0:T(8,128)(2,1)S(1)} all-to-all(bf16[8,128,512]{2,1,0:T(8,128)(2,1)S(1)} %broadcast_in_dim.5), channel_id=1, replica_groups=mesh['x'=4,'yh'=2,'z'=4,'yl'=2,'c'=2] {'z','yl'}, dimensions={0} | all-to-all | bytes 2097152 | tf_op jit(solution)/shard_map/all_to_all | solution.py:420
  84.1 0.0 collective-permute-start.5
  84.1 2.7 %collective-permute-done.5.far = bf16[8,128,512]{2,1,0:T(8,128)(2,1)S(1)} collective-permute-done((bf16[8,128,512]{2,1,0:T(8,128)(2,1)S(1)}, bf16[8,128,512]{2,1,0:T(8,128)(2,1)S(1)}, u32[]{:S(2)}, u32[]{:S(2)}) %collective-permute-start.5) | collective-permute-done | bytes 1048608 | tf_op jit(solution)/shard_map/ppermute | solution.py:24
  86.8 0.0 copy-done.11
  86.8 2.2 %copy-done.3 = bf16[8192,256]{1,0:T(8,128)(2,1)S(1)} copy-done((bf16[8192,256]{1,0:T(8,128)(2,1)S(1)}, bf16[8192,256]{1,0:T(8,128)(2,1)}, u32[]{:S(2)}) %copy-start.3) | copy-done | bytes 4194328
  89.0 2.2 %copy-done.4 = bf16[256,8192]{1,0:T(8,128)(2,1)S(1)} copy-done((bf16[256,8192]{1,0:T(8,128)(2,1)S(1)}, bf16[256,8192]{1,0:T(8,128)(2,1)}, u32[]{:S(2)}) %copy-start.4) | copy-done | bytes 4194328
  91.2 7.4 %shard_map.196 = (bf16[64,64,128]{2,1,0:T(8,128)(2,1)S(1)}, bf16[64,64,128]{2,1,0:T(8,128)(2,1)S(1)}, f32[64,128]{1,0:T(8,128)S(1)}) custom-call(s32[3]{0:T(128)S(1)} %pad_add_fusion.place, bf16[8,128,512]{2,1,0:T(8,128)(2,1)S(1)} %all_to_all.22.near, bf16[8,128,512]{2,1,0:T(8,128)(2,1)S(1)} %collective-permute-done.5.far, bf16[64,128]{1,0:T(8,128)(2,1)S(1)} %bitcast.56, ...), custom_call_target="tpu_custom_call" | custom-call | tf_op jit(solution)/shard_map/pallas_call | solution.py:430
  98.6 0.2 collective-permute-start.6
  98.8 2.5 %collective-permute-done.6 = bf16[64,64,128]{2,1,0:T(8,128)(2,1)S(1)} collective-permute-done((bf16[64,64,128]{2,1,0:T(8,128)(2,1)S(1)}, bf16[64,64,128]{2,1,0:T(8,128)(2,1)S(1)}, u32[]{:S(2)}, u32[]{:S(2)}) %collective-permute-start.6) | collective-permute-done | bytes 1048608 | tf_op jit(solution)/shard_map/ppermute | solution.py:24
  101.3 1.4 %add_convert_fusion.1 = bf16[64,64,128]{2,1,0:T(8,128)(2,1)} fusion(bf16[64,64,128]{2,1,0:T(8,128)(2,1)S(1)} %collective-permute-done.6, bf16[64,64,128]{2,1,0:T(8,128)(2,1)S(1)} %get-tuple-element.27), kind=kLoop, calls=%fused_computation.6 | loop fusion | flops 2097152 | bytes 3145728 | tf_op jit(solution)/shard_map/convert_element_type | solution.py:28
  102.7 7.9 %all-to-all-start.3 = ((bf16[64,64,128]{2,1,0:T(8,128)(2,1)}), bf16[64,64,128]{2,1,0:T(8,128)(2,1)S(1)}, u32[]{:S(2)}, u32[]{:S(2)}) async-start(bf16[64,64,128]{2,1,0:T(8,128)(2,1)} %add_convert_fusion.1), calls=%async_computation.3 | async-start | bytes 2097152 | tf_op jit(solution)/shard_map/all_to_all | solution.py:456
  110.6 0.1 mul.45
  110.7 6.1 %add_convert_fusion = bf16[8,32,64,128]{3,2,1,0:T(8,128)(2,1)} fusion(bf16[8,32,64,128]{3,2,1,0:T(8,128)(2,1)} %param.30, f32[8,128]{1,0:T(8,128)S(1)} %get-tuple-element.31, f32[8,32,64]{2,1,0:T(8,128)S(1)} %mul.45, f32[8,32]{1,0:T(8,128)S(1)} %get-tuple-element.29), kind=kLoop, calls=%fused_computation | loop fusion | flops 10485760 | bytes 8459264 | tf_op jit(solution)/shard_map/convert_element_type | solution.py:462
  116.8 13.0 %all-to-all-done.3 = bf16[64,64,128]{2,1,0:T(8,128)(2,1)S(1)} async-done(((bf16[64,64,128]{2,1,0:T(8,128)(2,1)}), bf16[64,64,128]{2,1,0:T(8,128)(2,1)S(1)}, u32[]{:S(2)}, u32[]{:S(2)}) %all-to-all-start.3) | async-done | bytes 1048608 | tf_op jit(solution)/shard_map/all_to_all | solution.py:456
  129.8 0.2 convert_reduce_fusion
  129.9 0.6 fusion.13
  (10 shorter events, 0.1 us)
Async XLA Ops:
  0.6 46.1 %copy-start = (bf16[1,2048,512]{2,1,0:T(8,128)(2,1)S(1)}, bf16[1,2048,512]{2,1,0:T(8,128)(2,1)}, u32[]{:S(2)}) copy-start(bf16[1,2048,512]{2,1,0:T(8,128)(2,1)} %param.32) | copy-start | bytes 6291460
  0.7 2.3 %copy-start.2 = (bf16[512,2,2048]{2,1,0:T(2,128)(2,1)S(1)}, bf16[512,2,2048]{2,1,0:T(2,128)(2,1)}, u32[]{:S(2)}) copy-start(bf16[512,2,2048]{2,1,0:T(2,128)(2,1)} %param.22) | copy-start | bytes 12582916
  3.1 1.6 %copy-start.5 = (bf16[128,8192]{1,0:T(8,128)(2,1)S(1)}, bf16[128,8192]{1,0:T(8,128)(2,1)}, u32[]{:S(2)}) copy-start(bf16[128,8192]{1,0:T(8,128)(2,1)} %hidden.1) | copy-start | bytes 6291460
  4.6 0.7 copy-start.10
  5.4 0.7 copy-start.13
  6.0 0.7 copy-start.14
  6.7 5.5 %copy-start.6 = (bf16[512,2,128]{2,1,0:T(2,128)(2,1)S(1)}, bf16[512,2,128]{2,1,0:T(2,128)(2,1)}, u32[]{:S(2)}) copy-start(bf16[512,2,128]{2,1,0:T(2,128)(2,1)} %param.23) | copy-start | bytes 786436
  6.7 5.5 %copy-start.9 = (bf16[512,32]{0,1:T(8,128)(2,1)S(1)}, bf16[512,32]{0,1:T(8,128)(2,1)}, u32[]{:S(2)}) copy-start(bf16[512,32]{0,1:T(8,128)(2,1)} %param.24) | copy-start | bytes 98308
  12.2 21.0 %copy-start.1 = (bf16[8,32,64,128]{3,2,1,0:T(8,128)(2,1)S(1)}, bf16[8,32,64,128]{3,2,1,0:T(8,128)(2,1)}, u32[]{:S(2)}) copy-start(bf16[8,32,64,128]{3,2,1,0:T(8,128)(2,1)} %param.30) | copy-start | bytes 12582916
  13.7 19.6 %copy-start.7 = (bf16[8,3,1,2304]{3,0,2,1:T(8,128)(2,1)S(1)}, bf16[8,3,1,2304]{3,0,2,1:T(8,128)(2,1)}, u32[]{:S(2)}) copy-start(bf16[8,3,1,2304]{3,0,2,1:T(8,128)(2,1)} %param.29) | copy-start | bytes 331780
  13.7 19.5 %copy-start.8 = (bf16[5,1,2304]{2,0,1:T(8,128)(2,1)S(1)}, bf16[5,1,2304]{2,0,1:T(8,128)(2,1)}, u32[]{:S(2)}) copy-start(bf16[5,1,2304]{2,0,1:T(8,128)(2,1)} %param.28) | copy-start | bytes 69124
  13.7 19.5 %copy-start.12 = (bf16[1,2048]{1,0:T(2,128)(2,1)S(1)}, bf16[1,2048]{1,0:T(2,128)(2,1)}, u32[]{:S(2)}) copy-start(bf16[1,2048]{1,0:T(2,128)(2,1)} %gain.1) | copy-start | bytes 12292
  13.7 19.5 %copy-start.15 = (f32[32]{0:T(128)S(1)}, f32[32]{0:T(128)}, u32[]{:S(2)}) copy-start(f32[32]{0:T(128)} %param.25) | copy-start | bytes 388
  13.7 19.5 %copy-start.16 = (f32[32]{0:T(128)S(1)}, f32[32]{0:T(128)}, u32[]{:S(2)}) copy-start(f32[32]{0:T(128)} %param.26) | copy-start | bytes 388
  13.7 19.5 %copy-start.17 = (f32[32]{0:T(128)S(1)}, f32[32]{0:T(128)}, u32[]{:S(2)}) copy-start(f32[32]{0:T(128)} %param.27) | copy-start | bytes 388
  13.7 2.1 %collective-permute-start = (bf16[8,8,4480]{2,1,0:T(8,128)(2,1)S(1)}, bf16[8,8,4480]{2,1,0:T(8,128)(2,1)S(1)}, u32[]{:S(2)}, u32[]{:S(2)}) collective-permute-start(bf16[8,8,4480]{2,1,0:T(8,128)(2,1)S(1)} %get-tuple-element.23), channel_id=1, source_target_pairs={{0,1},{1,0},{2,3},{3,2},{4,5},{5,4},{6,7},{7,6},{8,9},{9,8},{10,11... | collective-permute-start | bytes 1720328 | tf_op jit(solution)/shard_map/ppermute | solution.py:24
  46.8 1.5 %collective-permute-start.1 = (bf16[8,8,2048]{2,1,0:T(8,128)(2,1)S(1)}, bf16[8,8,2048]{2,1,0:T(8,128)(2,1)S(1)}, u32[]{:S(2)}, u32[]{:S(2)}) collective-permute-start(bf16[8,8,2048]{2,1,0:T(8,128)(2,1)S(1)} %all_to_all.21), channel_id=1, source_target_pairs={{0,1},{1,0},{2,3},{3,2},{4,5},{5,4},{6,7},{7,6},{8,9},{9,8},{10,11... | collective-permute-start | bytes 786440 | tf_op jit(solution)/shard_map/ppermute | solution.py:24
  48.8 5.6 %collective-permute-start.2 = (bf16[128,512]{1,0:T(8,128)(2,1)S(1)}, bf16[128,512]{1,0:T(8,128)(2,1)S(1)}, u32[]{:S(2)}, u32[]{:S(2)}) collective-permute-start(bf16[128,512]{1,0:T(8,128)(2,1)S(1)} %pad_maximum_fusion), channel_id=1, source_target_pairs={{0,32},{32,0},{64,96},{96,64},{1,33},{33,1},{65,97},{97,65},{2,34}... | collective-permute-start | bytes 393224 | tf_op jit(solution)/shard_map/ppermute | solution.py:24
  54.4 32.4 %copy-start.11 = (bf16[8192]{0:T(1024)(128)(2,1)S(1)}, bf16[8192]{0:T(1024)(128)(2,1)}, u32[]{:S(2)}) copy-start(bf16[8192]{0:T(1024)(128)(2,1)} %param.33) | copy-start | bytes 49156
  54.5 6.3 %collective-permute-start.3 = (bf16[128,512]{1,0:T(8,128)(2,1)S(1)}, bf16[128,512]{1,0:T(8,128)(2,1)S(1)}, u32[]{:S(2)}, u32[]{:S(2)}) collective-permute-start(bf16[128,512]{1,0:T(8,128)(2,1)S(1)} %add_convert_fusion.5), channel_id=1, source_target_pairs={{0,96},{32,64},{64,32},{96,0},{1,97},{33,65},{65,33},{97,1},{2,98}... | collective-permute-start | bytes 393224 | tf_op jit(solution)/shard_map/ppermute | solution.py:24
  60.8 6.6 %collective-permute-start.4 = (bf16[128,512]{1,0:T(8,128)(2,1)S(1)}, bf16[128,512]{1,0:T(8,128)(2,1)S(1)}, u32[]{:S(2)}, u32[]{:S(2)}) collective-permute-start(bf16[128,512]{1,0:T(8,128)(2,1)S(1)} %add_convert_fusion.4), channel_id=1, source_target_pairs={{0,16},{16,0},{1,17},{17,1},{2,18},{18,2},{3,19},{19,3},{4,20},{20... | collective-permute-start | bytes 393224 | tf_op jit(solution)/shard_map/ppermute | solution.py:24
  84.1 2.7 %collective-permute-start.5 = (bf16[8,128,512]{2,1,0:T(8,128)(2,1)S(1)}, bf16[8,128,512]{2,1,0:T(8,128)(2,1)S(1)}, u32[]{:S(2)}, u32[]{:S(2)}) collective-permute-start(bf16[8,128,512]{2,1,0:T(8,128)(2,1)S(1)} %all_to_all.22.near), channel_id=1, source_target_pairs={{0,1},{1,0},{2,3},{3,2},{4,5},{5,4},{6,7},{7,6},{8,9},{9,8},{10,11... | collective-permute-start | bytes 3145736 | tf_op jit(solution)/shard_map/ppermute | solution.py:24
  86.8 2.2 %copy-start.3 = (bf16[8192,256]{1,0:T(8,128)(2,1)S(1)}, bf16[8192,256]{1,0:T(8,128)(2,1)}, u32[]{:S(2)}) copy-start(bf16[8192,256]{1,0:T(8,128)(2,1)} %param.34) | copy-start | bytes 12582916
  89.0 2.2 %copy-start.4 = (bf16[256,8192]{1,0:T(8,128)(2,1)S(1)}, bf16[256,8192]{1,0:T(8,128)(2,1)}, u32[]{:S(2)}) copy-start(bf16[256,8192]{1,0:T(8,128)(2,1)} %down.1) | copy-start | bytes 12582916
  98.6 2.7 %collective-permute-start.6 = (bf16[64,64,128]{2,1,0:T(8,128)(2,1)S(1)}, bf16[64,64,128]{2,1,0:T(8,128)(2,1)S(1)}, u32[]{:S(2)}, u32[]{:S(2)}) collective-permute-start(bf16[64,64,128]{2,1,0:T(8,128)(2,1)S(1)} %get-tuple-element.28), channel_id=1, source_target_pairs={{0,1},{1,0},{2,3},{3,2},{4,5},{5,4},{6,7},{7,6},{8,9},{9,8},{10,11... | collective-permute-start | bytes 3145736 | tf_op jit(solution)/shard_map/ppermute | solution.py:24
  102.7 27.0 %all-to-all-start.3 = ((bf16[64,64,128]{2,1,0:T(8,128)(2,1)}), bf16[64,64,128]{2,1,0:T(8,128)(2,1)S(1)}, u32[]{:S(2)}, u32[]{:S(2)}) async-start(bf16[64,64,128]{2,1,0:T(8,128)(2,1)} %add_convert_fusion.1), calls=%async_computation.3 | async-start | bytes 2097152 | tf_op jit(solution)/shard_map/all_to_all | solution.py:456

commit v3 on v2

v3 whole, which is shorter than its diff:
```python
import jax
import jax.numpy as jnp
from jax import lax
from jax.experimental import pallas as pl
from jax.experimental.pallas import tpu as pltpu
from jax.sharding import Mesh, PartitionSpec as P

EPS = 1e-05
GRP = ("x", "yh")
HEAD = ("z", "yl", "c")
CHIPS = ("x", "yh", "z", "yl")
NEAR = ("z", "yl")
F32 = jnp.float32
BF16 = jnp.bfloat16
HBM = pl.BlockSpec(memory_space=pltpu.HBM)
ANY = pl.BlockSpec(memory_space=pl.ANY)
VMEM = pl.BlockSpec(memory_space=pltpu.VMEM)
LANES = 128
PREP = 20
FFN = 8
FETCH = 8


def swap(value, axis, bit):
    size = lax.axis_size(axis)
    return lax.ppermute(value, axis, [(i, i ^ bit) for i in range(size)])


def add(left, right):
    return (left.astype(F32) + right.astype(F32)).astype(BF16)


def in_hbm(value):
    return pltpu.with_memory_space_constraint(value, pltpu.HBM)


def params(mib):
    return pltpu.CompilerParams(vmem_limit_bytes=mib << 20)


def contract(left, right, left_dim, right_dim):
    return lax.dot_general(
        left, right, (((left_dim,), (right_dim,)), ((), ())), preferred_element_type=F32
    )


def split3(values):
    high = values.astype(BF16)
    rest = values - high.astype(F32)
    middle = rest.astype(BF16)
    low = (rest - middle.astype(F32)).astype(BF16)
    return high, middle, low


def project_kernel(
    owner,
    history,
    hidden,
    gain,
    weights,
    select,
    step,
    keep,
    give,
    order,
    past,
    base,
    held,
    owner_held,
    history_held,
    gain_held,
    gains,
    tiles,
    select_held,
    step_held,
    sems,
    hidden_sems,
    small_sems,
):
    head = lax.axis_index(HEAD)
    core = lax.axis_index("c")
    count, part = tiles.shape[:2]
    rows, width = hidden.shape
    blocks = width // part
    own_rows = rows // blocks
    half = rows // 2
    smalls = [
        pltpu.make_async_copy(source, target, small_sems.at[i])
        for i, (source, target) in enumerate(
            (
                (owner, owner_held),
                (history, history_held),
                (gain, gain_held),
                (select, select_held),
                (step, step_held),
            )
        )
    ]
    loads = [
        pltpu.make_async_copy(
            hidden.at[:, pl.ds(i * part, part)], held.at[i], hidden_sems.at[i]
        )
        for i in range(blocks)
    ]
    copies = [
        pltpu.make_async_copy(weights.at[:, i], tiles.at[i], sems.at[i]) for i in range(count)
    ]
    for copy in smalls[:3] + loads:
        copy.start()
    later = copies + smalls[3:]
    for copy in smalls[:3]:
        copy.wait()
    gains[...] = gain_held[...].astype(F32)
    position = lax.broadcasted_iota(jnp.int32, (rows, rows), 1)
    key = (owner_held[...] * rows + position).astype(F32)
    before = (key.T < key).astype(F32)
    rank = jnp.sum(before, axis=0, keepdims=True)
    slot = lax.broadcasted_iota(jnp.int32, (rows, rows), 0)
    to_slot = jnp.where(rank == slot.astype(F32), 1.0, 0.0)
    slot_history = jnp.sum(to_slot * history_held[...].astype(F32), axis=1, keepdims=True)
    past[...] = jnp.broadcast_to(slot_history, (rows, LANES))
    near = slot < half
    inner = jnp.where(near, slot, slot - half)
    shift = jnp.where(near, core, 1 - core) * own_rows
    sent = (inner // own_rows) * (2 * own_rows) + lax.rem(inner, own_rows) + shift
    ordering = jnp.where(rank == sent.astype(F32), 1.0, 0.0).astype(BF16)
    order[...] = ordering
    source = lax.broadcasted_iota(jnp.int32, (part, 2 * part), 0)
    target = lax.broadcasted_iota(jnp.int32, (part, 2 * part), 1)
    spread = jnp.where(target == 2 * source, 1.0, 0.0).astype(BF16)
    squares = jnp.zeros((rows, LANES), F32)
    for i in range(blocks):
        loads[i].wait()
        for copy in later[2 * i : 2 * i + 2]:
            copy.start()
        for q in range(part // LANES):
            chunk = held[i, :, q * LANES : (q + 1) * LANES].astype(F32)
            squares += chunk * chunk
    scale = lax.rsqrt(jnp.sum(squares, axis=1, keepdims=True) / width + EPS)
    normed = []
    for q in range(part // LANES):
        chunk = held[head, :, q * LANES : (q + 1) * LANES].astype(F32)
        row = gains[pl.ds(head * (part // LANES) + q, 1), :]
        normed.append((chunk * scale * row).astype(BF16))
    base[...] = held[head]
    plain = jnp.dot(ordering, jnp.concatenate(normed, axis=1), preferred_element_type=F32).astype(
        BF16
    )
    even = jnp.dot(plain, spread, preferred_element_type=F32)
    odd = pltpu.roll(even, 1, axis=1)
    left = jnp.concatenate([even.astype(BF16), odd.astype(BF16)], axis=0)

    def put(at, values):
        width = values.shape[1]
        for out, part in ((keep, values[:half]), (give, values[half:])):
            out[:, at : at + width] = part.astype(BF16)

    for i in range(0, count, 2):
        copies[i].wait()
        copies[i + 1].wait()
        right = jnp.concatenate(
            [tiles.at[i + k].reshape(2 * part, LANES)[...] for k in range(2)], axis=1
        )
        both = jnp.dot(left, right, preferred_element_type=F32)
        put(i * LANES, both[:rows])
        put((count + i) * LANES, both[rows:])
    for copy in smalls[3:]:
        copy.wait()
    both = jnp.dot(left, select_held[...], preferred_element_type=F32)
    at = 2 * count * LANES
    put(at, both[:rows])
    put(at + LANES, both[rows:])
    steps = contract(plain, step_held[...], 1, 1)
    missing = LANES - steps.shape[1]
    put(at + 2 * LANES, jnp.concatenate([steps, jnp.zeros((rows, missing), F32)], axis=1))


def mixer_kernel(
    pieces,
    past,
    window,
    taps,
    bias,
    decay_log,
    skip,
    gain,
    state,
    mixed,
    window_next,
    inputs_step,
    in_coef,
    decay,
):
    senders, own, _ = pieces.shape
    channels = mixed.shape[1]
    heads = bias.shape[1]
    width = channels // heads
    total = pieces[0].astype(F32)
    for i in range(1, senders):
        total += pieces[i].astype(F32)
    gate = total[:, :channels]
    fresh = total[:, channels : 2 * channels + 2 * LANES].astype(BF16).astype(F32)
    step_raw = total[:, 2 * channels + 2 * LANES : 2 * channels + 2 * LANES + heads]
    valid = past[pl.ds(pl.multiple_of(lax.axis_index(HEAD) * own, own), own), 0:1]
    lags = window.shape[0]
    entries = []
    for k in range(lags):
        mask = jnp.where(valid >= lags - k, 1.0, 0.0)
        entries.append(window[k].astype(F32) * mask)
    entries.append(fresh)
    weights = taps[...].astype(F32)
    conv = weights[lags + 1 : lags + 2]
    for k in range(lags + 1):
        conv = conv + entries[k] * weights[k : k + 1]
    for k in range(lags):
        window_next[k] = entries[k + 1].astype(BF16)
    active = conv * (1.0 / (1.0 + jnp.exp(-conv)))
    u = active[:, :channels]
    b = active[:, channels : channels + LANES]
    c = active[:, channels + LANES :]
    shifted = step_raw + bias[...]
    step = jnp.maximum(shifted, 0.0) + jnp.log1p(jnp.exp(-jnp.abs(shifted)))
    rate = jnp.exp(-step * jnp.exp(decay_log[...]))
    both = jnp.sum(b * c, axis=1, keepdims=True)
    direct = step * both + skip[...]
    head_of = lax.broadcasted_iota(jnp.int32, (heads, channels), 0)
    channel = lax.broadcasted_iota(jnp.int32, (heads, channels), 1)
    first = head_of * width
    spread = jnp.where((channel >= first) & (channel < first + width), 1.0, 0.0).astype(BF16)
    stacked = jnp.concatenate([rate, step, direct], axis=0)
    wide = sum(jnp.dot(part, spread, preferred_element_type=F32) for part in split3(stacked))
    rate_wide = wide[:own]
    step_wide = wide[own : 2 * own]
    direct_wide = wide[2 * own :]
    inputs_step[...] = step_wide * u
    in_coef[...] = b
    decay[...] = rate
    c_high = c.astype(BF16)
    c_low = (c - c_high.astype(F32)).astype(BF16)
    coefs = jnp.concatenate([c_high, c_low], axis=0)
    row = lax.broadcasted_iota(jnp.int32, (own, channels), 0)
    read = jnp.zeros((own, channels), F32)
    for s in range(own):
        found = contract(coefs, state[s], 1, 1)
        read = jnp.where(row == s, found[:own] + found[own:], read)
    gated = (rate_wide * read + direct_wide * u) * (gate * (1.0 / (1.0 + jnp.exp(-gate))))
    scale = lax.rsqrt(jnp.sum(gated * gated, axis=1, keepdims=True) / channels + EPS)
    mixed[...] = (gated * scale * gain[...].astype(F32)).astype(BF16)


def add_kernel(left, right, out):
    for i in range(out.shape[0]):
        out[i] = (left[i].astype(F32) + right[i].astype(F32)).astype(BF16)


def residual_kernel(mixed, other, order, base, out):
    total = (mixed[...].astype(F32) + other[...].astype(F32)).astype(BF16)
    piece = (base[...].astype(F32) + contract(order[...], total, 0, 0)).astype(BF16)
    for i in range(out.shape[0]):
        out[i] = piece


def fetch_kernel(after, source, out, sem):
    copy = pltpu.make_async_copy(source, out, sem)
    copy.start()
    copy.wait()


def fetch(after, source):
    return pl.pallas_call(
        fetch_kernel,
        out_shape=pltpu.VMEM(source.shape, source.dtype),
        in_specs=[ANY, HBM],
        out_specs=VMEM,
        scratch_shapes=[pltpu.SemaphoreType.DMA],
        compiler_params=params(FETCH),
        cost_estimate=pl.CostEstimate(
            flops=0, bytes_accessed=2 * source.size * source.dtype.itemsize, transcendentals=0
        ),
    )(after, in_hbm(source))


def ffn_kernel(
    near,
    far,
    gain,
    up,
    down,
    keep,
    give,
    slice_out,
    turned,
    gains,
):
    core = lax.axis_index("c")
    flat = lax.axis_index(GRP + HEAD)
    chunks, rows, part = near.shape
    hidden = up.shape[2]
    model = 2 * chunks * part
    piece = keep.shape[1]
    turns = [(j, which) for which in range(2) for j in range(chunks)]
    gains[...] = gain[...].astype(F32)
    squares = jnp.zeros((rows, LANES), F32)
    total = jnp.zeros((rows, hidden), F32)
    lanes = part // LANES
    for k, (j, which) in enumerate(turns):
        source = near if which == 0 else far
        at = 2 * j + (core if which == 0 else 1 - core)
        scaled = []
        for q in range(lanes):
            chunk = source[j, :, q * LANES : (q + 1) * LANES].astype(F32)
            squares += chunk * chunk
            row = gains[pl.ds(at * lanes + q, 1), :]
            scaled.append((chunk * row).astype(BF16))
        total += jnp.dot(jnp.concatenate(scaled, axis=1), up[at], preferred_element_type=F32)
    scale = lax.rsqrt(jnp.sum(squares, axis=1, keepdims=True) / model + EPS)
    raised = jnp.maximum(total * scale, 0.0)
    squared = (raised * raised).astype(BF16)
    per_part = part // piece
    owner = flat // per_part
    mine = near[owner // 2].astype(F32)
    other = far[owner // 2].astype(F32)
    turned[...] = jnp.where(lax.rem(owner, 2) == core, mine, other).T
    slice_out[...] = turned[pl.ds(pl.multiple_of(lax.rem(flat, per_part) * piece, piece), piece), :]
    for k in range(2 * chunks):
        right = down[:, k * part : (k + 1) * part]
        out = jnp.dot(squared, right, preferred_element_type=F32).astype(BF16).T
        for q in range(part // (2 * piece)):
            low = out[2 * q * piece : (2 * q + 1) * piece]
            high = out[(2 * q + 1) * piece : (2 * q + 2) * piece]
            chip = k * (part // (2 * piece)) + q
            keep[chip] = jnp.where(core == 0, low, high)
            give[chip] = jnp.where(core == 0, high, low)


def local(
    hidden_in,
    row_owner,
    history_len,
    pre_gain,
    inner_proj,
    select_proj,
    step_proj,
    step_bias,
    decay_log,
    skip_gain,
    conv_taps,
    conv_window,
    state_cache,
    mixer_gain,
    output_proj,
    channel_gain,
    up_weight,
    down_weight,
):
    rows, model = hidden_in.shape
    heads_axis = lax.axis_size(HEAD)
    groups_axis = lax.axis_size(GRP)
    own = rows // heads_axis
    part = model // heads_axis
    channels = mixer_gain.shape[1]
    heads = step_proj.shape[1]
    state_size = state_cache.shape[3]
    head_width = state_cache.shape[2]
    taps = conv_taps.shape[0]
    conv_width = conv_taps.shape[2]
    hidden_units = up_weight.shape[1]
    tile_count = channels // LANES
    head_index = lax.axis_index(HEAD)
    shape = jax.ShapeDtypeStruct

    tiled = inner_proj.reshape(part, 2, tile_count, LANES).transpose(0, 2, 1, 3)
    sent_width = 2 * channels + 2 * state_size + LANES
    near_owners = heads_axis // 2
    keep, give, order, past, base = pl.pallas_call(
        project_kernel,
        out_shape=(
            pltpu.VMEM((rows // 2, sent_width), BF16),
            pltpu.VMEM((rows // 2, sent_width), BF16),
            shape((rows, rows), BF16),
            pltpu.VMEM((rows, LANES), F32),
            shape((rows, part), BF16),
        ),
        in_specs=[HBM] * 7,
        out_specs=(VMEM,) * 5,
        scratch_shapes=[
            pltpu.VMEM((heads_axis, rows, part), BF16),
            pltpu.VMEM((1, rows), jnp.int32),
            pltpu.VMEM((1, rows), jnp.int32),
            pltpu.VMEM((model // LANES, LANES), BF16),
            pltpu.VMEM((model // LANES, LANES), F32),
            pltpu.VMEM((tile_count, part, 2, LANES), BF16),
            pltpu.VMEM((2 * part, state_size), BF16),
            pltpu.VMEM((heads, part), BF16),
            pltpu.SemaphoreType.DMA((tile_count,)),
            pltpu.SemaphoreType.DMA((heads_axis,)),
            pltpu.SemaphoreType.DMA((5,)),
        ],
        compiler_params=params(PREP),
    )(
        *(
            in_hbm(value)
            for value in (
                row_owner.reshape(1, rows),
                history_len.reshape(1, rows),
                hidden_in,
                pre_gain.reshape(model // LANES, LANES),
                tiled,
                select_proj.reshape(2 * part, state_size),
                step_proj.T,
            )
        )
    )
    keep, give = (value.reshape(near_owners, own, sent_width) for value in (keep, give))
    chip_terms = add(keep, swap(give, "c", 1))
    pieces = lax.all_to_all(chip_terms, NEAR, split_axis=0, concat_axis=0, tiled=True)
    mixed_own, window_next, inputs_step, in_coef, decay = pl.pallas_call(
        mixer_kernel,
        out_shape=(
            shape((own, channels), BF16),
            shape((taps - 2, own, conv_width), BF16),
            shape((own, channels), F32),
            shape((own, state_size), F32),
            shape((own, heads), F32),
        ),
        in_specs=[VMEM] * 9,
        out_specs=(VMEM,) * 5,
        compiler_params=params(16),
    )(
        pieces,
        past,
        conv_window.transpose(1, 2, 0, 3).reshape(taps - 2, own, conv_width),
        conv_taps.reshape(taps, conv_width),
        step_bias.reshape(1, heads),
        decay_log.reshape(1, heads),
        skip_gain.reshape(1, heads),
        mixer_gain,
        state_cache.reshape(own, heads * head_width, state_size),
    )
    near_mix = lax.all_to_all(
        jnp.broadcast_to(mixed_own[None], (near_owners, own, channels)),
        NEAR,
        split_axis=0,
        concat_axis=0,
        tiled=True,
    )
    far_mix = swap(near_mix, "c", 1)
    out_weight = output_proj.reshape(channels, part)
    mixed = jnp.concatenate(
        [
            jnp.dot(mix.reshape(rows // 2, channels), out_weight, preferred_element_type=F32)
            for mix in (near_mix, far_mix)
        ]
    ).astype(BF16)
    for bit in (1, 3):
        mixed = add(mixed, swap(mixed, "x", bit))
    other = swap(mixed, "yh", 1)
    down_near = fetch(mixed, down_weight)
    other, down_near = lax.optimization_barrier((other, down_near))
    spread_piece = pl.pallas_call(
        residual_kernel,
        out_shape=shape((near_owners, rows, part), BF16),
        in_specs=[VMEM] * 4,
        out_specs=VMEM,
        compiler_params=params(4),
    )(mixed, other, order, base)
    near = lax.all_to_all(spread_piece, NEAR, split_axis=0, concat_axis=0, tiled=True)
    far = swap(near, "c", 1)
    up_near = fetch(near, up_weight.reshape(heads_axis, part, hidden_units))
    far, up_near = lax.optimization_barrier((far, up_near))
    chips = groups_axis * heads_axis // 2
    piece = model // (groups_axis * heads_axis)
    keep, give, residual_slice = pl.pallas_call(
        ffn_kernel,
        out_shape=(
            shape((chips, piece, rows), BF16),
            shape((chips, piece, rows), BF16),
            shape((piece, rows), F32),
        ),
        in_specs=[VMEM] * 5,
        out_specs=(VMEM,) * 3,
        scratch_shapes=[
            pltpu.VMEM((part, rows), F32),
            pltpu.VMEM((model // LANES, LANES), F32),
        ],
        compiler_params=params(FFN),
    )(
        near,
        far,
        channel_gain.reshape(model // LANES, LANES),
        up_near,
        down_near,
    )
    chip_sum = pl.pallas_call(
        add_kernel,
        out_shape=pltpu.VMEM(keep.shape, BF16),
        in_specs=[VMEM] * 2,
        out_specs=VMEM,
        compiler_params=params(4),
    )(keep, swap(give, "c", 1))
    spread = lax.all_to_all(chip_sum, CHIPS, split_axis=0, concat_axis=0, tiled=True)
    block_out = (residual_slice + jnp.sum(spread.astype(F32), axis=0)).astype(BF16).T
    step_input = inputs_step.reshape(own, heads, head_width)
    state_next = (
        decay[..., None, None] * state_cache.astype(F32)
        + step_input[..., None] * in_coef[:, None, None, :]
    ).astype(BF16)
    window_out = window_next.reshape(taps - 2, 1, own, conv_width).transpose(2, 0, 1, 3)
    return (block_out, state_next, window_out)


def solution(mesh):
    fine = Mesh(mesh.devices.reshape(4, 2, 4, 2, 2), ("x", "yh", "z", "yl", "c"))
    placed = (
        P(),
        P(),
        P(),
        P(),
        P(HEAD, None, GRP),
        P(HEAD, None, GRP),
        P(HEAD, GRP),
        P(GRP),
        P(GRP),
        P(GRP),
        P(None, GRP, None),
        P(HEAD, None, GRP, None),
        P(HEAD, GRP, None, None),
        P(GRP, None),
        P(GRP, None, HEAD),
        P(),
        P(None, GRP + HEAD),
        P(GRP + HEAD, None),
    )
    return jax.shard_map(
        local,
        mesh=fine,
        in_specs=placed,
        out_specs=(
            P(None, GRP + HEAD),
            P(HEAD, GRP, None, None),
            P(HEAD, None, GRP, None),
        ),
        check_vma=False,
    )
```

time: 131 us -> 113 us (0.86)
  local copies, waits for them, and re-layouts: 10.6 us -> 0.15 us
  waiting for transfers between devices: 32.2 us -> 27.8 us
  other arithmetic: 8.55 us -> 7.03 us
    unnamed x36 -> x18, local copies, waits for them, and re-layouts: 10.4 us -> 0.04 us
    pallas_call x2 -> x5, Pallas kernels: 6.95 us -> 13.4 us  [the longest x1 7.52 us: local(): pl.pallas_call(project_kernel, out_shape=(pltpu.VMEM((rows // 2, sent_wid...]
    pallas_call x1, Pallas kernels: 7.37 us -> 2.48 us  [local(): pl.pallas_call(ffn_kernel, out_shape=(shape((chips, piece, rows), BF16),...]
    ppermute x7, waiting for transfers between devices: 19.2 us -> 14.8 us  [swap(): return lax.ppermute(value, axis, [(i, i ^ bit) for i in range(size)])]
    pallas_call x1, Pallas kernels: 3.74 us -> 2.14 us  [local(): pl.pallas_call(mixer_kernel, out_shape=(shape((own, channels), BF16), sha...]
    convert_element_type x4 -> x3, other arithmetic: 1.61 us -> 0.2 us  [add(): return (left.astype(F32) + right.astype(F32)).astype(BF16)]
  transfers between devices with their start and end apart: 8 -> 8, of which waited for: 8 -> 8; matrix products, arithmetic and copies ran while one was open for 5% -> 6% of each run, Pallas kernels for 0% -> 4%
where the time goes in v3:
time: 113 us
  blocking collectives  42.6 us (38%)
  waiting for transfers between devices  27.8 us (25%)
  Pallas kernels  18 us (16%)
  starting transfers between devices  15.6 us (14%)
  other arithmetic  7.03 us (6%)
    all_to_all x1, blocking collectives, local(): lax.all_to_all(chip_terms, NEAR, split_axis=0, concat_axis=0, tiled=True)  17.3 us
    all_to_all x1, blocking collectives, local(): lax.all_to_all(spread_piece, NEAR, split_axis=0, concat_axis=0, tiled=True)  15.6 us
    ppermute x7, waiting for transfers between devices, swap(): return lax.ppermute(value, axis, [(i, i ^ bit) for i in range(size)])  14.8 us
    all_to_all x1, waiting for transfers between devices, local(): lax.all_to_all(chip_sum, CHIPS, split_axis=0, concat_axis=0, tiled=True)  13 us
    all_to_all x1, blocking collectives, local(): lax.all_to_all(jnp.broadcast_to(mixed_own[None], (near_owners, own, chann...  9.7 us
    all_to_all x1, starting transfers between devices, local(): lax.all_to_all(chip_sum, CHIPS, split_axis=0, concat_axis=0, tiled=True)  7.93 us
    ppermute x7, starting transfers between devices, swap(): return lax.ppermute(value, axis, [(i, i ^ bit) for i in range(size)])  7.7 us
    pallas_call x1, Pallas kernels, local(): pl.pallas_call(project_kernel, out_shape=(pltpu.VMEM((rows // 2, sent_wid...  7.52 us
  transfers between devices with their start and end apart: 8, of which 8 were waited for; matrix products, arithmetic and copies ran while one was open for 6% of the time, Pallas kernels for 4%

profile of v3, /device:TPU:0, one launch (start us, length us, event | category | flops | bytes accessed | tf_op | source)
XLA Modules:
  0.0 113.0 jit_solution(329470393342846240)
XLA Ops:
  0.6 0.0 copy-start
  0.7 0.0 copy-start.1
  0.7 0.0 copy-start.2
  0.7 0.0 copy-start.3
  0.7 0.0 copy-start.5
  0.7 0.0 copy-start.6
  0.7 0.0 copy-start.7
  0.7 0.0 copy-start.8
  0.7 7.5 %shard_map.193 = (bf16[64,4480]{1,0:T(8,128)(2,1)S(1)}, bf16[64,4480]{1,0:T(8,128)(2,1)S(1)}, bf16[128,128]{1,0:T(8,128)(2,1)S(1)}, f32[128,128]{1,0:T(8,128)S(1)}, bf16[128,512]{1,0:T(8,128)(2,1)S(1)}) custom-call(s32[1,128]{1,0:T(1,128)} %bitcast.59, s32[1,128]{1,0:T(1,128)} %bitcast.60, bf16[128,8192]{1,0:T(8,128)(2,1)} %hidden.1, ...), custom_call_target="tpu_custom_call" | custom-call | tf_op jit(solution)/shard_map/pallas_call | solution.py:375
  8.3 0.1 collective-permute-start
  8.3 2.0 %collective-permute-done = bf16[8,8,4480]{2,1,0:T(8,128)(2,1)S(1)} collective-permute-done((bf16[8,8,4480]{2,1,0:T(8,128)(2,1)S(1)}, bf16[8,8,4480]{2,1,0:T(8,128)(2,1)S(1)}, u32[]{:S(2)}, u32[]{:S(2)}) %collective-permute-start) | collective-permute-done | bytes 573472 | tf_op jit(solution)/shard_map/ppermute | solution.py:26
  10.3 0.1 fusion.4
  10.4 17.3 %all_to_all.20.pieces = bf16[8,8,4480]{2,1,0:T(8,128)(2,1)S(1)} all-to-all(bf16[8,8,4480]{2,1,0:T(8,128)(2,1)S(1)} %fusion.4), channel_id=1, replica_groups=mesh['x'=4,'yh'=2,'z'=4,'yl'=2,'c'=2] {'z','yl'}, dimensions={0} | all-to-all | bytes 1146880 | tf_op jit(solution)/shard_map/all_to_all | solution.py:416
  27.7 0.0 copy-done.1
  27.7 0.0 copy-done.2
  27.7 0.0 copy-done.3
  27.7 0.0 copy-done.5
  27.7 0.0 copy-done.6
  27.8 0.0 copy-done.7
  27.8 0.0 copy-done.8
  27.8 2.1 %shard_map.194 = (bf16[8,2048]{1,0:T(8,128)(2,1)S(1)}, bf16[3,8,2304]{2,1,0:T(8,128)(2,1)}, f32[8,2048]{1,0:T(8,128)S(1)}, f32[8,128]{1,0:T(8,128)S(1)}, f32[8,32]{1,0:T(8,128)S(1)}) custom-call(bf16[8,8,4480]{2,1,0:T(8,128)(2,1)S(1)} %all_to_all.20.pieces, f32[128,128]{1,0:T(8,128)S(1)} %get-tuple-element.22.past, bf16[3,8,2304]{2,1,0:T(8,128)(2,1)S(1)} %bitcast.47, ...), custom_call_target="tpu_custom_call" | custom-call | tf_op jit(solution)/shard_map/pallas_call | solution.py:417
  29.9 9.7 %all_to_all.21 = bf16[8,8,2048]{2,1,0:T(8,128)(2,1)S(1)} all-to-all(bf16[8,8,2048]{2,1,0:T(8,128)(2,1)S(1)} %broadcast_in_dim.2), channel_id=1, replica_groups=mesh['x'=4,'yh'=2,'z'=4,'yl'=2,'c'=2] {'z','yl'}, dimensions={0} | all-to-all | bytes 524288 | tf_op jit(solution)/shard_map/all_to_all | solution.py:440
  39.6 0.0 collective-permute-start.1
  39.6 0.0 copy-done
  39.6 0.5 fusion.5
  40.1 1.0 collective-permute-done.1
  41.2 0.5 fusion.8
  41.7 1.6 %collective-permute-start.2 = (bf16[128,512]{1,0:T(8,128)(2,1)S(1)}, bf16[128,512]{1,0:T(8,128)(2,1)S(1)}, u32[]{:S(2)}, u32[]{:S(2)}) collective-permute-start(bf16[128,512]{1,0:T(8,128)(2,1)S(1)} %pad_maximum_fusion), channel_id=1, source_target_pairs={{0,32},{32,0},{64,96},{96,64},{1,33},{33,1},{65,97},{97,65},{2,34}... | collective-permute-start | bytes 393224 | tf_op jit(solution)/shard_map/ppermute | solution.py:26
  43.2 4.0 %collective-permute-done.2 = bf16[128,512]{1,0:T(8,128)(2,1)S(1)} collective-permute-done((bf16[128,512]{1,0:T(8,128)(2,1)S(1)}, bf16[128,512]{1,0:T(8,128)(2,1)S(1)}, u32[]{:S(2)}, u32[]{:S(2)}) %collective-permute-start.2) | collective-permute-done | bytes 131104 | tf_op jit(solution)/shard_map/ppermute | solution.py:26
  47.3 2.8 %collective-permute-start.3 = (bf16[128,512]{1,0:T(8,128)(2,1)S(1)}, bf16[128,512]{1,0:T(8,128)(2,1)S(1)}, u32[]{:S(2)}, u32[]{:S(2)}) collective-permute-start(bf16[128,512]{1,0:T(8,128)(2,1)S(1)} %add_convert_fusion.2), channel_id=1, source_target_pairs={{0,96},{32,64},{64,32},{96,0},{1,97},{33,65},{65,33},{97,1},{2,98}... | collective-permute-start | bytes 393224 | tf_op jit(solution)/shard_map/ppermute | solution.py:26
  50.2 3.4 %collective-permute-done.3 = bf16[128,512]{1,0:T(8,128)(2,1)S(1)} collective-permute-done((bf16[128,512]{1,0:T(8,128)(2,1)S(1)}, bf16[128,512]{1,0:T(8,128)(2,1)S(1)}, u32[]{:S(2)}, u32[]{:S(2)}) %collective-permute-start.3) | collective-permute-done | bytes 131104 | tf_op jit(solution)/shard_map/ppermute | solution.py:26
  53.6 3.0 %collective-permute-start.4 = (bf16[128,512]{1,0:T(8,128)(2,1)S(1)}, bf16[128,512]{1,0:T(8,128)(2,1)S(1)}, u32[]{:S(2)}, u32[]{:S(2)}) collective-permute-start(bf16[128,512]{1,0:T(8,128)(2,1)S(1)} %add_convert_fusion.1.after.mixed), channel_id=1, source_target_pairs={{0,16},{16,0},{1,17},{17,1},{2,18},{18,2},{3,19},{19,3},{4,20},{20... | collective-permute-start | bytes 393224 | tf_op jit(solution)/shard_map/ppermute | solution.py:26
  56.6 2.2 %shard_map.195.down = bf16[256,8192]{1,0:T(8,128)(2,1)S(1)} custom-call(bf16[128,512]{1,0:T(8,128)(2,1)S(1)} %add_convert_fusion.1.after.mixed, bf16[256,8192]{1,0:T(8,128)(2,1)} %source.1), custom_call_target="tpu_custom_call" | custom-call | bytes 8388608 | tf_op jit(solution)/shard_map/pallas_call | solution.py:270
  58.8 1.4 %collective-permute-done.4.other = bf16[128,512]{1,0:T(8,128)(2,1)S(1)} collective-permute-done((bf16[128,512]{1,0:T(8,128)(2,1)S(1)}, bf16[128,512]{1,0:T(8,128)(2,1)S(1)}, u32[]{:S(2)}, u32[]{:S(2)}) %collective-permute-start.4) | collective-permute-done | bytes 131104 | tf_op jit(solution)/shard_map/ppermute | solution.py:26
  60.2 0.2 shard_map.196
  60.4 15.6 %all_to_all.22.after.near = bf16[8,128,512]{2,1,0:T(8,128)(2,1)S(1)} all-to-all(bf16[8,128,512]{2,1,0:T(8,128)(2,1)S(1)} %shard_map.196), channel_id=1, replica_groups=mesh['x'=4,'yh'=2,'z'=4,'yl'=2,'c'=2] {'z','yl'}, dimensions={0} | all-to-all | bytes 2097152 | tf_op jit(solution)/shard_map/all_to_all | solution.py:467
  76.1 0.0 collective-permute-start.5
  76.1 0.0 copy-start.4
  76.1 2.2 %shard_map.197.up = bf16[16,512,256]{2,1,0:T(8,128)(2,1)S(1)} custom-call(bf16[8,128,512]{2,1,0:T(8,128)(2,1)S(1)} %all_to_all.22.after.near, bf16[16,512,256]{2,1,0:T(8,128)(2,1)} %bitcast.55), custom_call_target="tpu_custom_call" | custom-call | bytes 8388608 | tf_op jit(solution)/shard_map/pallas_call | solution.py:270
  78.3 0.4 collective-permute-done.5.far
  78.7 0.0 copy-done.4
  78.7 2.5 %shard_map.198 = (bf16[64,64,128]{2,1,0:T(8,128)(2,1)S(1)}, bf16[64,64,128]{2,1,0:T(8,128)(2,1)S(1)}, f32[64,128]{1,0:T(8,128)S(1)}) custom-call(bf16[8,128,512]{2,1,0:T(8,128)(2,1)S(1)} %all_to_all.22.after.near, bf16[8,128,512]{2,1,0:T(8,128)(2,1)S(1)} %collective-permute-done.5.far, bf16[64,128]{1,0:T(8,128)(2,1)S(1)} %bitcast.49, ...), custom_call_target="tpu_custom_call" | custom-call | tf_op jit(solution)/shard_map/pallas_call | solution.py:473
  81.2 0.2 collective-permute-start.6
  81.4 2.5 %collective-permute-done.6.right = bf16[64,64,128]{2,1,0:T(8,128)(2,1)S(1)} collective-permute-done((bf16[64,64,128]{2,1,0:T(8,128)(2,1)S(1)}, bf16[64,64,128]{2,1,0:T(8,128)(2,1)S(1)}, u32[]{:S(2)}, u32[]{:S(2)}) %collective-permute-start.6) | collective-permute-done | bytes 1048608 | tf_op jit(solution)/shard_map/ppermute | solution.py:26
  83.9 1.2 %shard_map.199 = bf16[64,64,128]{2,1,0:T(8,128)(2,1)} custom-call(bf16[64,64,128]{2,1,0:T(8,128)(2,1)S(1)} %get-tuple-element.31.left, bf16[64,64,128]{2,1,0:T(8,128)(2,1)S(1)} %collective-permute-done.6.right), custom_call_target="tpu_custom_call" | custom-call | tf_op jit(solution)/shard_map/pallas_call | solution.py:494
  85.2 7.9 %all-to-all-start.3 = ((bf16[64,64,128]{2,1,0:T(8,128)(2,1)}), bf16[64,64,128]{2,1,0:T(8,128)(2,1)S(1)}, u32[]{:S(2)}, u32[]{:S(2)}) async-start(bf16[64,64,128]{2,1,0:T(8,128)(2,1)} %shard_map.199), calls=%async_computation.3 | async-start | bytes 2097152 | tf_op jit(solution)/shard_map/all_to_all | solution.py:501
  93.1 0.1 mul.25
  93.2 6.0 %add_convert_fusion = bf16[8,32,64,128]{3,2,1,0:T(8,128)(2,1)} fusion(bf16[8,32,64,128]{3,2,1,0:T(8,128)(2,1)} %param.30, f32[8,128]{1,0:T(8,128)S(1)} %get-tuple-element.35, f32[8,32,64]{2,1,0:T(8,128)S(1)} %mul.25, f32[8,32]{1,0:T(8,128)S(1)} %get-tuple-element.33), kind=kLoop, calls=%fused_computation | loop fusion | flops 10485760 | bytes 8459264 | tf_op jit(solution)/shard_map/convert_element_type | solution.py:507
  99.2 13.0 %all-to-all-done.3 = bf16[64,64,128]{2,1,0:T(8,128)(2,1)S(1)} async-done(((bf16[64,64,128]{2,1,0:T(8,128)(2,1)}), bf16[64,64,128]{2,1,0:T(8,128)(2,1)S(1)}, u32[]{:S(2)}, u32[]{:S(2)}) %all-to-all-start.3) | async-done | bytes 1048608 | tf_op jit(solution)/shard_map/all_to_all | solution.py:501
  112.2 0.2 convert_reduce_fusion
  112.4 0.6 fusion.13
  (4 shorter events, 0.1 us)
Async XLA Ops:
  0.6 39.0 %copy-start = (bf16[1,2048,512]{2,1,0:T(8,128)(2,1)S(1)}, bf16[1,2048,512]{2,1,0:T(8,128)(2,1)}, u32[]{:S(2)}) copy-start(bf16[1,2048,512]{2,1,0:T(8,128)(2,1)} %param.32) | copy-start | bytes 6291460
  0.7 27.1 %copy-start.1 = (bf16[8,32,64,128]{3,2,1,0:T(8,128)(2,1)S(1)}, bf16[8,32,64,128]{3,2,1,0:T(8,128)(2,1)}, u32[]{:S(2)}) copy-start(bf16[8,32,64,128]{3,2,1,0:T(8,128)(2,1)} %param.30) | copy-start | bytes 12582916
  0.7 27.1 %copy-start.2 = (bf16[8,3,1,2304]{3,0,2,1:T(8,128)(2,1)S(1)}, bf16[8,3,1,2304]{3,0,2,1:T(8,128)(2,1)}, u32[]{:S(2)}) copy-start(bf16[8,3,1,2304]{3,0,2,1:T(8,128)(2,1)} %param.29) | copy-start | bytes 331780
  0.7 27.1 %copy-start.3 = (bf16[5,1,2304]{2,0,1:T(8,128)(2,1)S(1)}, bf16[5,1,2304]{2,0,1:T(8,128)(2,1)}, u32[]{:S(2)}) copy-start(bf16[5,1,2304]{2,0,1:T(8,128)(2,1)} %param.28) | copy-start | bytes 69124
  0.7 27.1 %copy-start.5 = (bf16[1,2048]{1,0:T(2,128)(2,1)S(1)}, bf16[1,2048]{1,0:T(2,128)(2,1)}, u32[]{:S(2)}) copy-start(bf16[1,2048]{1,0:T(2,128)(2,1)} %gain.1) | copy-start | bytes 12292
  0.7 27.1 %copy-start.6 = (f32[32]{0:T(128)S(1)}, f32[32]{0:T(128)}, u32[]{:S(2)}) copy-start(f32[32]{0:T(128)} %param.25) | copy-start | bytes 388
  0.7 27.1 %copy-start.7 = (f32[32]{0:T(128)S(1)}, f32[32]{0:T(128)}, u32[]{:S(2)}) copy-start(f32[32]{0:T(128)} %param.26) | copy-start | bytes 388
  0.7 27.1 %copy-start.8 = (f32[32]{0:T(128)S(1)}, f32[32]{0:T(128)}, u32[]{:S(2)}) copy-start(f32[32]{0:T(128)} %param.27) | copy-start | bytes 388
  8.3 2.1 %collective-permute-start = (bf16[8,8,4480]{2,1,0:T(8,128)(2,1)S(1)}, bf16[8,8,4480]{2,1,0:T(8,128)(2,1)S(1)}, u32[]{:S(2)}, u32[]{:S(2)}) collective-permute-start(bf16[8,8,4480]{2,1,0:T(8,128)(2,1)S(1)} %bitcast.53), channel_id=1, source_target_pairs={{0,1},{1,0},{2,3},{3,2},{4,5},{5,4},{6,7},{7,6},{8,9},{9,8},{10,11... | collective-permute-start | bytes 1720328 | tf_op jit(solution)/shard_map/ppermute | solution.py:26
  39.6 1.5 %collective-permute-start.1 = (bf16[8,8,2048]{2,1,0:T(8,128)(2,1)S(1)}, bf16[8,8,2048]{2,1,0:T(8,128)(2,1)S(1)}, u32[]{:S(2)}, u32[]{:S(2)}) collective-permute-start(bf16[8,8,2048]{2,1,0:T(8,128)(2,1)S(1)} %all_to_all.21), channel_id=1, source_target_pairs={{0,1},{1,0},{2,3},{3,2},{4,5},{5,4},{6,7},{7,6},{8,9},{9,8},{10,11... | collective-permute-start | bytes 786440 | tf_op jit(solution)/shard_map/ppermute | solution.py:26
  41.7 5.6 %collective-permute-start.2 = (bf16[128,512]{1,0:T(8,128)(2,1)S(1)}, bf16[128,512]{1,0:T(8,128)(2,1)S(1)}, u32[]{:S(2)}, u32[]{:S(2)}) collective-permute-start(bf16[128,512]{1,0:T(8,128)(2,1)S(1)} %pad_maximum_fusion), channel_id=1, source_target_pairs={{0,32},{32,0},{64,96},{96,64},{1,33},{33,1},{65,97},{97,65},{2,34}... | collective-permute-start | bytes 393224 | tf_op jit(solution)/shard_map/ppermute | solution.py:26
  47.3 6.3 %collective-permute-start.3 = (bf16[128,512]{1,0:T(8,128)(2,1)S(1)}, bf16[128,512]{1,0:T(8,128)(2,1)S(1)}, u32[]{:S(2)}, u32[]{:S(2)}) collective-permute-start(bf16[128,512]{1,0:T(8,128)(2,1)S(1)} %add_convert_fusion.2), channel_id=1, source_target_pairs={{0,96},{32,64},{64,32},{96,0},{1,97},{33,65},{65,33},{97,1},{2,98}... | collective-permute-start | bytes 393224 | tf_op jit(solution)/shard_map/ppermute | solution.py:26
  53.6 6.6 %collective-permute-start.4 = (bf16[128,512]{1,0:T(8,128)(2,1)S(1)}, bf16[128,512]{1,0:T(8,128)(2,1)S(1)}, u32[]{:S(2)}, u32[]{:S(2)}) collective-permute-start(bf16[128,512]{1,0:T(8,128)(2,1)S(1)} %add_convert_fusion.1.after.mixed), channel_id=1, source_target_pairs={{0,16},{16,0},{1,17},{17,1},{2,18},{18,2},{3,19},{19,3},{4,20},{20... | collective-permute-start | bytes 393224 | tf_op jit(solution)/shard_map/ppermute | solution.py:26
  76.1 2.7 %collective-permute-start.5 = (bf16[8,128,512]{2,1,0:T(8,128)(2,1)S(1)}, bf16[8,128,512]{2,1,0:T(8,128)(2,1)S(1)}, u32[]{:S(2)}, u32[]{:S(2)}) collective-permute-start(bf16[8,128,512]{2,1,0:T(8,128)(2,1)S(1)} %all_to_all.22.after.near), channel_id=1, source_target_pairs={{0,1},{1,0},{2,3},{3,2},{4,5},{5,4},{6,7},{7,6},{8,9},{9,8},{10,11... | collective-permute-start | bytes 3145736 | tf_op jit(solution)/shard_map/ppermute | solution.py:26
  76.1 2.7 %copy-start.4 = (bf16[8192]{0:T(1024)(128)(2,1)S(1)}, bf16[8192]{0:T(1024)(128)(2,1)}, u32[]{:S(2)}) copy-start(bf16[8192]{0:T(1024)(128)(2,1)} %param.33) | copy-start | bytes 49156
  81.2 2.7 %collective-permute-start.6 = (bf16[64,64,128]{2,1,0:T(8,128)(2,1)S(1)}, bf16[64,64,128]{2,1,0:T(8,128)(2,1)S(1)}, u32[]{:S(2)}, u32[]{:S(2)}) collective-permute-start(bf16[64,64,128]{2,1,0:T(8,128)(2,1)S(1)} %get-tuple-element.32), channel_id=1, source_target_pairs={{0,1},{1,0},{2,3},{3,2},{4,5},{5,4},{6,7},{7,6},{8,9},{9,8},{10,11... | collective-permute-start | bytes 3145736 | tf_op jit(solution)/shard_map/ppermute | solution.py:26
  85.2 27.0 %all-to-all-start.3 = ((bf16[64,64,128]{2,1,0:T(8,128)(2,1)}), bf16[64,64,128]{2,1,0:T(8,128)(2,1)S(1)}, u32[]{:S(2)}, u32[]{:S(2)}) async-start(bf16[64,64,128]{2,1,0:T(8,128)(2,1)} %shard_map.199), calls=%async_computation.3 | async-start | bytes 2097152 | tf_op jit(solution)/shard_map/all_to_all | solution.py:501

commit v4 on v3

--- a/solution.py
+++ b/solution.py
@@ -444,6 +444,9 @@
         concat_axis=0,
         tiled=True,
     )
+    near_mix, inputs_step, in_coef, decay = lax.optimization_barrier(
+        (near_mix, inputs_step, in_coef, decay)
+    )
     far_mix = swap(near_mix, "c", 1)
     out_weight = output_proj.reshape(channels, part)
     mixed = jnp.concatenate(
@@ -452,8 +455,16 @@
             for mix in (near_mix, far_mix)
         ]
     ).astype(BF16)
+    step_input = inputs_step.reshape(own, heads, head_width)
+    state_next = (
+        decay[..., None, None] * state_cache.astype(F32)
+        + step_input[..., None] * in_coef[:, None, None, :]
+    ).astype(BF16)
     for bit in (1, 3):
-        mixed = add(mixed, swap(mixed, "x", bit))
+        other = swap(mixed, "x", bit)
+        if bit == 1:
+            other, state_next = lax.optimization_barrier((other, state_next))
+        mixed = add(mixed, other)
     other = swap(mixed, "yh", 1)
     down_near = fetch(mixed, down_weight)
     other, down_near = lax.optimization_barrier((other, down_near))
@@ -500,11 +511,6 @@
     )(keep, swap(give, "c", 1))
     spread = lax.all_to_all(chip_sum, CHIPS, split_axis=0, concat_axis=0, tiled=True)
     block_out = (residual_slice + jnp.sum(spread.astype(F32), axis=0)).astype(BF16).T
-    step_input = inputs_step.reshape(own, heads, head_width)
-    state_next = (
-        decay[..., None, None] * state_cache.astype(F32)
-        + step_input[..., None] * in_coef[:, None, None, :]
-    ).astype(BF16)
     window_out = window_next.reshape(taps - 2, 1, own, conv_width).transpose(2, 0, 1, 3)
     return (block_out, state_next, window_out)
 

time: 113 us -> 112 us (level)
  blocking collectives: 42.6 us -> 69.1 us
  waiting for transfers between devices: 27.8 us -> 11.1 us
  starting transfers between devices: 15.6 us -> 7.71 us
  other arithmetic: 7.03 us -> 5.09 us
    all_to_all x0 -> x1, blocking collectives: none -> 25.7 us  [local(): lax.all_to_all(chip_sum, CHIPS, split_axis=0, concat_axis=0, tiled=True)]
    all_to_all x1 -> x0, waiting for transfers between devices: 13 us -> none  [local(): lax.all_to_all(chip_sum, CHIPS, split_axis=0, concat_axis=0, tiled=True)]
    all_to_all x1 -> x0, starting transfers between devices: 7.93 us -> none  [local(): lax.all_to_all(chip_sum, CHIPS, split_axis=0, concat_axis=0, tiled=True)]
    ppermute x7, waiting for transfers between devices: 14.8 us -> 11.1 us  [swap(): return lax.ppermute(value, axis, [(i, i ^ bit) for i in range(size)])]
    convert_element_type x1, other arithmetic: 6.04 us -> 4.09 us  [local(): state_next = (decay[..., None, None] * state_cache.astype(F32) + step_inp...]
  transfers between devices with their start and end apart: 8 -> 7, of which waited for: 8 -> 6; matrix products, arithmetic and copies ran while one was open for 6% -> 4% of each run, Pallas kernels for 4% -> 4%
where the time goes in v4:
time: 112 us
  blocking collectives  69.1 us (62%)
  Pallas kernels  17 us (15%)
  waiting for transfers between devices  11.1 us (10%)
  starting transfers between devices  7.71 us (7%)
  other arithmetic  5.09 us (5%)
    all_to_all x1, blocking collectives, local(): lax.all_to_all(chip_sum, CHIPS, split_axis=0, concat_axis=0, tiled=True)  25.7 us
    all_to_all x1, blocking collectives, local(): lax.all_to_all(chip_terms, NEAR, split_axis=0, concat_axis=0, tiled=True)  17.3 us
    all_to_all x1, blocking collectives, local(): lax.all_to_all(spread_piece, NEAR, split_axis=0, concat_axis=0, tiled=True)  16.4 us
    ppermute x7, waiting for transfers between devices, swap(): return lax.ppermute(value, axis, [(i, i ^ bit) for i in range(size)])  11.1 us
    all_to_all x1, blocking collectives, local(): lax.all_to_all(jnp.broadcast_to(mixed_own[None], (near_owners, own, chann...  9.7 us
    ppermute x7, starting transfers between devices, swap(): return lax.ppermute(value, axis, [(i, i ^ bit) for i in range(size)])  7.71 us
    pallas_call x1, Pallas kernels, local(): pl.pallas_call(project_kernel, out_shape=(pltpu.VMEM((rows // 2, sent_wid...  7.52 us
    pallas_call x2, Pallas kernels, fetch(): pl.pallas_call(fetch_kernel, out_shape=pltpu.VMEM(source.shape, source.dt...  4.4 us
  transfers between devices with their start and end apart: 7, of which 6 were waited for; matrix products, arithmetic and copies ran while one was open for 4% of the time, Pallas kernels for 4%

profile of v4, /device:TPU:0, one launch (start us, length us, event | category | flops | bytes accessed | tf_op | source)
XLA Modules:
  0.0 112.0 jit_solution(1116037181681294979)
XLA Ops:
  0.6 0.0 copy-start
  0.7 0.0 copy-start.1
  0.7 0.0 copy-start.3
  0.7 0.0 copy-start.4
  0.7 0.0 copy-start.6
  0.7 0.0 copy-start.7
  0.7 0.0 copy-start.8
  0.7 0.0 copy-start.9
  0.7 7.5 %shard_map.193 = (bf16[64,4480]{1,0:T(8,128)(2,1)S(1)}, bf16[64,4480]{1,0:T(8,128)(2,1)S(1)}, bf16[128,128]{1,0:T(8,128)(2,1)S(1)}, f32[128,128]{1,0:T(8,128)S(1)}, bf16[128,512]{1,0:T(8,128)(2,1)S(1)}) custom-call(s32[1,128]{1,0:T(1,128)} %bitcast.59, s32[1,128]{1,0:T(1,128)} %bitcast.60, bf16[128,8192]{1,0:T(8,128)(2,1)} %hidden.1, ...), custom_call_target="tpu_custom_call" | custom-call | tf_op jit(solution)/shard_map/pallas_call | solution.py:375
  8.3 0.1 collective-permute-start
  8.3 2.0 %collective-permute-done = bf16[8,8,4480]{2,1,0:T(8,128)(2,1)S(1)} collective-permute-done((bf16[8,8,4480]{2,1,0:T(8,128)(2,1)S(1)}, bf16[8,8,4480]{2,1,0:T(8,128)(2,1)S(1)}, u32[]{:S(2)}, u32[]{:S(2)}) %collective-permute-start) | collective-permute-done | bytes 573472 | tf_op jit(solution)/shard_map/ppermute | solution.py:26
  10.3 0.1 fusion.4
  10.4 17.3 %all_to_all.20.pieces = bf16[8,8,4480]{2,1,0:T(8,128)(2,1)S(1)} all-to-all(bf16[8,8,4480]{2,1,0:T(8,128)(2,1)S(1)} %fusion.4), channel_id=1, replica_groups=mesh['x'=4,'yh'=2,'z'=4,'yl'=2,'c'=2] {'z','yl'}, dimensions={0} | all-to-all | bytes 1146880 | tf_op jit(solution)/shard_map/all_to_all | solution.py:416
  27.7 0.0 copy-done.1
  27.7 0.0 copy-done.3
  27.7 0.0 copy-done.4
  27.7 0.0 copy-done.6
  27.7 0.0 copy-done.7
  27.8 0.0 copy-done.8
  27.8 0.0 copy-done.9
  27.8 2.1 %shard_map.194 = (bf16[8,2048]{1,0:T(8,128)(2,1)S(1)}, bf16[3,8,2304]{2,1,0:T(8,128)(2,1)}, f32[8,2048]{1,0:T(8,128)S(1)}, f32[8,128]{1,0:T(8,128)S(1)}, f32[8,32]{1,0:T(8,128)S(1)}) custom-call(bf16[8,8,4480]{2,1,0:T(8,128)(2,1)S(1)} %all_to_all.20.pieces, f32[128,128]{1,0:T(8,128)S(1)} %get-tuple-element.28.past, bf16[3,8,2304]{2,1,0:T(8,128)(2,1)S(1)} %bitcast.47, ...), custom_call_target="tpu_custom_call" | custom-call | tf_op jit(solution)/shard_map/pallas_call | solution.py:417
  29.9 9.7 %all_to_all.21 = bf16[8,8,2048]{2,1,0:T(8,128)(2,1)S(1)} all-to-all(bf16[8,8,2048]{2,1,0:T(8,128)(2,1)S(1)} %broadcast_in_dim.2), channel_id=1, replica_groups=mesh['x'=4,'yh'=2,'z'=4,'yl'=2,'c'=2] {'z','yl'}, dimensions={0} | all-to-all | bytes 524288 | tf_op jit(solution)/shard_map/all_to_all | solution.py:440
  39.6 0.1 mul.25
  39.7 0.0 copy-start.2
  39.7 0.1 collective-permute-start.1
  39.8 0.0 copy-done
  39.8 0.5 fusion.5
  40.3 1.0 collective-permute-done.1
  41.3 0.5 fusion.8
  41.8 1.6 %collective-permute-start.2 = (bf16[128,512]{1,0:T(8,128)(2,1)S(1)}, bf16[128,512]{1,0:T(8,128)(2,1)S(1)}, u32[]{:S(2)}, u32[]{:S(2)}) collective-permute-start(bf16[128,512]{1,0:T(8,128)(2,1)S(1)} %pad_maximum_fusion), channel_id=1, source_target_pairs={{0,32},{32,0},{64,96},{96,64},{1,33},{33,1},{65,97},{97,65},{2,34}... | collective-permute-start | bytes 393224 | tf_op jit(solution)/shard_map/ppermute | solution.py:26
  43.4 0.0 copy-done.2
  43.4 4.1 %add_convert_fusion = bf16[8,32,64,128]{3,2,1,0:T(8,128)(2,1)} fusion(bf16[8,32,64,128]{3,2,1,0:T(8,128)(2,1)S(1)} %copy-done.2, f32[8,128]{1,0:T(8,128)S(1)} %get-tuple-element.36, f32[8,32,64]{2,1,0:T(8,128)S(1)} %mul.25, f32[8,32]{1,0:T(8,128)S(1)} %get-tuple-element.34), kind=kLoop, calls=%fused_computation | loop fusion | flops 10485760 | bytes 8459264 | tf_op jit(solution)/shard_map/convert_element_type | solution.py:462
  47.5 0.0 collective-permute-done.2
  47.5 2.8 %collective-permute-start.3 = (bf16[128,512]{1,0:T(8,128)(2,1)S(1)}, bf16[128,512]{1,0:T(8,128)(2,1)S(1)}, u32[]{:S(2)}, u32[]{:S(2)}) collective-permute-start(bf16[128,512]{1,0:T(8,128)(2,1)S(1)} %add_convert_fusion.2), channel_id=1, source_target_pairs={{0,96},{32,64},{64,32},{96,0},{1,97},{33,65},{65,33},{97,1},{2,98}... | collective-permute-start | bytes 393224 | tf_op jit(solution)/shard_map/ppermute | solution.py:26
  50.3 3.8 %collective-permute-done.3 = bf16[128,512]{1,0:T(8,128)(2,1)S(1)} collective-permute-done((bf16[128,512]{1,0:T(8,128)(2,1)S(1)}, bf16[128,512]{1,0:T(8,128)(2,1)S(1)}, u32[]{:S(2)}, u32[]{:S(2)}) %collective-permute-start.3) | collective-permute-done | bytes 131104 | tf_op jit(solution)/shard_map/ppermute | solution.py:26
  54.1 3.0 %collective-permute-start.4 = (bf16[128,512]{1,0:T(8,128)(2,1)S(1)}, bf16[128,512]{1,0:T(8,128)(2,1)S(1)}, u32[]{:S(2)}, u32[]{:S(2)}) collective-permute-start(bf16[128,512]{1,0:T(8,128)(2,1)S(1)} %add_convert_fusion.1.after.mixed), channel_id=1, source_target_pairs={{0,16},{16,0},{1,17},{17,1},{2,18},{18,2},{3,19},{19,3},{4,20},{20... | collective-permute-start | bytes 393224 | tf_op jit(solution)/shard_map/ppermute | solution.py:26
  57.1 2.2 %shard_map.195.down = bf16[256,8192]{1,0:T(8,128)(2,1)S(1)} custom-call(bf16[128,512]{1,0:T(8,128)(2,1)S(1)} %add_convert_fusion.1.after.mixed, bf16[256,8192]{1,0:T(8,128)(2,1)} %source.1), custom_call_target="tpu_custom_call" | custom-call | bytes 8388608 | tf_op jit(solution)/shard_map/pallas_call | solution.py:270
  59.3 1.4 %collective-permute-done.4.other = bf16[128,512]{1,0:T(8,128)(2,1)S(1)} collective-permute-done((bf16[128,512]{1,0:T(8,128)(2,1)S(1)}, bf16[128,512]{1,0:T(8,128)(2,1)S(1)}, u32[]{:S(2)}, u32[]{:S(2)}) %collective-permute-start.4) | collective-permute-done | bytes 131104 | tf_op jit(solution)/shard_map/ppermute | solution.py:26
  60.7 0.2 shard_map.196
  60.9 16.4 %all_to_all.22.after.near = bf16[8,128,512]{2,1,0:T(8,128)(2,1)S(1)} all-to-all(bf16[8,128,512]{2,1,0:T(8,128)(2,1)S(1)} %shard_map.196), channel_id=1, replica_groups=mesh['x'=4,'yh'=2,'z'=4,'yl'=2,'c'=2] {'z','yl'}, dimensions={0} | all-to-all | bytes 2097152 | tf_op jit(solution)/shard_map/all_to_all | solution.py:478
  77.3 0.0 collective-permute-start.5
  77.3 0.0 copy-start.5
  77.3 2.2 %shard_map.197.up = bf16[16,512,256]{2,1,0:T(8,128)(2,1)S(1)} custom-call(bf16[8,128,512]{2,1,0:T(8,128)(2,1)S(1)} %all_to_all.22.after.near, bf16[16,512,256]{2,1,0:T(8,128)(2,1)} %bitcast.55), custom_call_target="tpu_custom_call" | custom-call | bytes 8388608 | tf_op jit(solution)/shard_map/pallas_call | solution.py:270
  79.6 0.4 collective-permute-done.5.far
  80.0 0.0 copy-done.5
  80.0 2.5 %shard_map.198 = (bf16[64,64,128]{2,1,0:T(8,128)(2,1)S(1)}, bf16[64,64,128]{2,1,0:T(8,128)(2,1)S(1)}, f32[64,128]{1,0:T(8,128)S(1)}) custom-call(bf16[8,128,512]{2,1,0:T(8,128)(2,1)S(1)} %all_to_all.22.after.near, bf16[8,128,512]{2,1,0:T(8,128)(2,1)S(1)} %collective-permute-done.5.far, bf16[64,128]{1,0:T(8,128)(2,1)S(1)} %bitcast.49, ...), custom_call_target="tpu_custom_call" | custom-call | tf_op jit(solution)/shard_map/pallas_call | solution.py:484
  82.5 0.2 collective-permute-start.6
  82.7 2.5 %collective-permute-done.6.right = bf16[64,64,128]{2,1,0:T(8,128)(2,1)S(1)} collective-permute-done((bf16[64,64,128]{2,1,0:T(8,128)(2,1)S(1)}, bf16[64,64,128]{2,1,0:T(8,128)(2,1)S(1)}, u32[]{:S(2)}, u32[]{:S(2)}) %collective-permute-start.6) | collective-permute-done | bytes 1048608 | tf_op jit(solution)/shard_map/ppermute | solution.py:26
  85.2 0.2 shard_map.199
  85.5 25.7 %all_to_all.23 = bf16[64,64,128]{2,1,0:T(8,128)(2,1)S(1)} all-to-all(bf16[64,64,128]{2,1,0:T(8,128)(2,1)S(1)} %shard_map.199), channel_id=1, replica_groups=mesh['x'=4,'yh'=2,'z'=4,'yl'=2,'c'=2] {'x','yh','z','yl'}, dimensions={0} | all-to-all | bytes 2097152 | tf_op jit(solution)/shard_map/all_to_all | solution.py:512
  111.2 0.2 convert_reduce_fusion
  111.4 0.6 fusion.13
  (4 shorter events, 0.1 us)
Async XLA Ops:
  0.6 39.2 %copy-start = (bf16[1,2048,512]{2,1,0:T(8,128)(2,1)S(1)}, bf16[1,2048,512]{2,1,0:T(8,128)(2,1)}, u32[]{:S(2)}) copy-start(bf16[1,2048,512]{2,1,0:T(8,128)(2,1)} %param.32) | copy-start | bytes 6291460
  0.7 27.1 %copy-start.1 = (bf16[8,32,64,128]{3,2,1,0:T(8,128)(2,1)S(1)}, bf16[8,32,64,128]{3,2,1,0:T(8,128)(2,1)}, u32[]{:S(2)}) copy-start(bf16[8,32,64,128]{3,2,1,0:T(8,128)(2,1)} %param.30) | copy-start | bytes 12582916
  0.7 27.1 %copy-start.3 = (bf16[8,3,1,2304]{3,0,2,1:T(8,128)(2,1)S(1)}, bf16[8,3,1,2304]{3,0,2,1:T(8,128)(2,1)}, u32[]{:S(2)}) copy-start(bf16[8,3,1,2304]{3,0,2,1:T(8,128)(2,1)} %param.29) | copy-start | bytes 331780
  0.7 27.1 %copy-start.4 = (bf16[5,1,2304]{2,0,1:T(8,128)(2,1)S(1)}, bf16[5,1,2304]{2,0,1:T(8,128)(2,1)}, u32[]{:S(2)}) copy-start(bf16[5,1,2304]{2,0,1:T(8,128)(2,1)} %param.28) | copy-start | bytes 69124
  0.7 27.1 %copy-start.6 = (bf16[1,2048]{1,0:T(2,128)(2,1)S(1)}, bf16[1,2048]{1,0:T(2,128)(2,1)}, u32[]{:S(2)}) copy-start(bf16[1,2048]{1,0:T(2,128)(2,1)} %gain.1) | copy-start | bytes 12292
  0.7 27.1 %copy-start.7 = (f32[32]{0:T(128)S(1)}, f32[32]{0:T(128)}, u32[]{:S(2)}) copy-start(f32[32]{0:T(128)} %param.25) | copy-start | bytes 388
  0.7 27.1 %copy-start.8 = (f32[32]{0:T(128)S(1)}, f32[32]{0:T(128)}, u32[]{:S(2)}) copy-start(f32[32]{0:T(128)} %param.26) | copy-start | bytes 388
  0.7 27.1 %copy-start.9 = (f32[32]{0:T(128)S(1)}, f32[32]{0:T(128)}, u32[]{:S(2)}) copy-start(f32[32]{0:T(128)} %param.27) | copy-start | bytes 388
  8.3 2.1 %collective-permute-start = (bf16[8,8,4480]{2,1,0:T(8,128)(2,1)S(1)}, bf16[8,8,4480]{2,1,0:T(8,128)(2,1)S(1)}, u32[]{:S(2)}, u32[]{:S(2)}) collective-permute-start(bf16[8,8,4480]{2,1,0:T(8,128)(2,1)S(1)} %bitcast.53), channel_id=1, source_target_pairs={{0,1},{1,0},{2,3},{3,2},{4,5},{5,4},{6,7},{7,6},{8,9},{9,8},{10,11... | collective-permute-start | bytes 1720328 | tf_op jit(solution)/shard_map/ppermute | solution.py:26
  39.7 3.7 %copy-start.2 = (bf16[8,32,64,128]{3,2,1,0:T(8,128)(2,1)S(1)}, bf16[8,32,64,128]{3,2,1,0:T(8,128)(2,1)}, u32[]{:S(2)}) copy-start(bf16[8,32,64,128]{3,2,1,0:T(8,128)(2,1)} %param.30) | copy-start | bytes 12582916
  39.7 1.6 %collective-permute-start.1 = (bf16[8,8,2048]{2,1,0:T(8,128)(2,1)S(1)}, bf16[8,8,2048]{2,1,0:T(8,128)(2,1)S(1)}, u32[]{:S(2)}, u32[]{:S(2)}) collective-permute-start(bf16[8,8,2048]{2,1,0:T(8,128)(2,1)S(1)} %all_to_all.21), channel_id=1, source_target_pairs={{0,1},{1,0},{2,3},{3,2},{4,5},{5,4},{6,7},{7,6},{8,9},{9,8},{10,11... | collective-permute-start | bytes 786440 | tf_op jit(solution)/shard_map/ppermute | solution.py:26
  41.8 5.7 %collective-permute-start.2 = (bf16[128,512]{1,0:T(8,128)(2,1)S(1)}, bf16[128,512]{1,0:T(8,128)(2,1)S(1)}, u32[]{:S(2)}, u32[]{:S(2)}) collective-permute-start(bf16[128,512]{1,0:T(8,128)(2,1)S(1)} %pad_maximum_fusion), channel_id=1, source_target_pairs={{0,32},{32,0},{64,96},{96,64},{1,33},{33,1},{65,97},{97,65},{2,34}... | collective-permute-start | bytes 393224 | tf_op jit(solution)/shard_map/ppermute | solution.py:26
  47.5 6.5 %collective-permute-start.3 = (bf16[128,512]{1,0:T(8,128)(2,1)S(1)}, bf16[128,512]{1,0:T(8,128)(2,1)S(1)}, u32[]{:S(2)}, u32[]{:S(2)}) collective-permute-start(bf16[128,512]{1,0:T(8,128)(2,1)S(1)} %add_convert_fusion.2), channel_id=1, source_target_pairs={{0,96},{32,64},{64,32},{96,0},{1,97},{33,65},{65,33},{97,1},{2,98}... | collective-permute-start | bytes 393224 | tf_op jit(solution)/shard_map/ppermute | solution.py:26
  54.1 6.6 %collective-permute-start.4 = (bf16[128,512]{1,0:T(8,128)(2,1)S(1)}, bf16[128,512]{1,0:T(8,128)(2,1)S(1)}, u32[]{:S(2)}, u32[]{:S(2)}) collective-permute-start(bf16[128,512]{1,0:T(8,128)(2,1)S(1)} %add_convert_fusion.1.after.mixed), channel_id=1, source_target_pairs={{0,16},{16,0},{1,17},{17,1},{2,18},{18,2},{3,19},{19,3},{4,20},{20... | collective-permute-start | bytes 393224 | tf_op jit(solution)/shard_map/ppermute | solution.py:26
  77.3 2.7 %collective-permute-start.5 = (bf16[8,128,512]{2,1,0:T(8,128)(2,1)S(1)}, bf16[8,128,512]{2,1,0:T(8,128)(2,1)S(1)}, u32[]{:S(2)}, u32[]{:S(2)}) collective-permute-start(bf16[8,128,512]{2,1,0:T(8,128)(2,1)S(1)} %all_to_all.22.after.near), channel_id=1, source_target_pairs={{0,1},{1,0},{2,3},{3,2},{4,5},{5,4},{6,7},{7,6},{8,9},{9,8},{10,11... | collective-permute-start | bytes 3145736 | tf_op jit(solution)/shard_map/ppermute | solution.py:26
  77.3 2.7 %copy-start.5 = (bf16[8192]{0:T(1024)(128)(2,1)S(1)}, bf16[8192]{0:T(1024)(128)(2,1)}, u32[]{:S(2)}) copy-start(bf16[8192]{0:T(1024)(128)(2,1)} %param.33) | copy-start | bytes 49156
  82.5 2.7 %collective-permute-start.6 = (bf16[64,64,128]{2,1,0:T(8,128)(2,1)S(1)}, bf16[64,64,128]{2,1,0:T(8,128)(2,1)S(1)}, u32[]{:S(2)}, u32[]{:S(2)}) collective-permute-start(bf16[64,64,128]{2,1,0:T(8,128)(2,1)S(1)} %get-tuple-element.46), channel_id=1, source_target_pairs={{0,1},{1,0},{2,3},{3,2},{4,5},{5,4},{6,7},{7,6},{8,9},{9,8},{10,11... | collective-permute-start | bytes 3145736 | tf_op jit(solution)/shard_map/ppermute | solution.py:26

commit v5 on v4

--- a/solution.py
+++ b/solution.py
@@ -1,3 +1,5 @@
+import functools
+
 import jax
 import jax.numpy as jnp
 from jax import lax
@@ -74,15 +76,14 @@
     select_held,
     step_held,
     sems,
-    hidden_sems,
+    own_sem,
     small_sems,
 ):
     head = lax.axis_index(HEAD)
     core = lax.axis_index("c")
     count, part = tiles.shape[:2]
     rows, width = hidden.shape
-    blocks = width // part
-    own_rows = rows // blocks
+    own_rows = rows * part // width
     half = rows // 2
     smalls = [
         pltpu.make_async_copy(source, target, small_sems.at[i])
@@ -96,18 +97,14 @@
             )
         )
     ]
-    loads = [
-        pltpu.make_async_copy(
-            hidden.at[:, pl.ds(i * part, part)], held.at[i], hidden_sems.at[i]
-        )
-        for i in range(blocks)
-    ]
+    own_load = pltpu.make_async_copy(
+        hidden.at[:, pl.ds(pl.multiple_of(head * part, part), part)], held, own_sem
+    )
     copies = [
         pltpu.make_async_copy(weights.at[:, i], tiles.at[i], sems.at[i]) for i in range(count)
     ]
-    for copy in smalls[:3] + loads:
+    for copy in smalls[:3] + [own_load] + copies + smalls[3:]:
         copy.start()
-    later = copies + smalls[3:]
     for copy in smalls[:3]:
         copy.wait()
     gains[...] = gain_held[...].astype(F32)
@@ -125,28 +122,25 @@
     sent = (inner // own_rows) * (2 * own_rows) + lax.rem(inner, own_rows) + shift
     ordering = jnp.where(rank == sent.astype(F32), 1.0, 0.0).astype(BF16)
     order[...] = ordering
-    source = lax.broadcasted_iota(jnp.int32, (part, 2 * part), 0)
-    target = lax.broadcasted_iota(jnp.int32, (part, 2 * part), 1)
+    source = lax.broadcasted_iota(jnp.int32, (LANES, 2 * LANES), 0)
+    target = lax.broadcasted_iota(jnp.int32, (LANES, 2 * LANES), 1)
     spread = jnp.where(target == 2 * source, 1.0, 0.0).astype(BF16)
-    squares = jnp.zeros((rows, LANES), F32)
-    for i in range(blocks):
-        loads[i].wait()
-        for copy in later[2 * i : 2 * i + 2]:
-            copy.start()
-        for q in range(part // LANES):
-            chunk = held[i, :, q * LANES : (q + 1) * LANES].astype(F32)
-            squares += chunk * chunk
-    scale = lax.rsqrt(jnp.sum(squares, axis=1, keepdims=True) / width + EPS)
-    normed = []
-    for q in range(part // LANES):
-        chunk = held[head, :, q * LANES : (q + 1) * LANES].astype(F32)
-        row = gains[pl.ds(head * (part // LANES) + q, 1), :]
-        normed.append((chunk * scale * row).astype(BF16))
-    base[...] = held[head]
-    plain = jnp.dot(ordering, jnp.concatenate(normed, axis=1), preferred_element_type=F32).astype(
-        BF16
-    )
-    even = jnp.dot(plain, spread, preferred_element_type=F32)
+    lanes = part // LANES
+    gain_row = jnp.concatenate(
+        [gains[pl.ds(head * lanes + q, 1), :] for q in range(lanes)], axis=1
+    )
+    own_load.wait()
+    base[...] = held[...]
+    ordered = jnp.dot(ordering, held[...], preferred_element_type=F32)
+    squares = jnp.sum(ordered * ordered, axis=1, keepdims=True)
+    plain = (ordered * gain_row).astype(BF16)
+    even = jnp.concatenate(
+        [
+            jnp.dot(plain[:, q * LANES : (q + 1) * LANES], spread, preferred_element_type=F32)
+            for q in range(lanes)
+        ],
+        axis=1,
+    )
     odd = pltpu.roll(even, 1, axis=1)
     left = jnp.concatenate([even.astype(BF16), odd.astype(BF16)], axis=0)
 
@@ -171,11 +165,12 @@
     put(at, both[:rows])
     put(at + LANES, both[rows:])
     steps = contract(plain, step_held[...], 1, 1)
-    missing = LANES - steps.shape[1]
-    put(at + 2 * LANES, jnp.concatenate([steps, jnp.zeros((rows, missing), F32)], axis=1))
+    missing = LANES - steps.shape[1] - 1
+    put(at + 2 * LANES, jnp.concatenate([steps, squares, jnp.zeros((rows, missing), F32)], axis=1))
 
 
 def mixer_kernel(
+    model,
     pieces,
     past,
     window,
@@ -198,6 +193,8 @@
     total = pieces[0].astype(F32)
     for i in range(1, senders):
         total += pieces[i].astype(F32)
+    at = 2 * channels + 2 * LANES + heads
+    total = total * lax.rsqrt(total[:, at : at + 1] / model + EPS)
     gate = total[:, :channels]
     fresh = total[:, channels : 2 * channels + 2 * LANES].astype(BF16).astype(F32)
     step_raw = total[:, 2 * channels + 2 * LANES : 2 * channels + 2 * LANES + heads]
@@ -384,7 +381,7 @@
         in_specs=[HBM] * 7,
         out_specs=(VMEM,) * 5,
         scratch_shapes=[
-            pltpu.VMEM((heads_axis, rows, part), BF16),
+            pltpu.VMEM((rows, part), BF16),
             pltpu.VMEM((1, rows), jnp.int32),
             pltpu.VMEM((1, rows), jnp.int32),
             pltpu.VMEM((model // LANES, LANES), BF16),
@@ -393,7 +390,7 @@
             pltpu.VMEM((2 * part, state_size), BF16),
             pltpu.VMEM((heads, part), BF16),
             pltpu.SemaphoreType.DMA((tile_count,)),
-            pltpu.SemaphoreType.DMA((heads_axis,)),
+            pltpu.SemaphoreType.DMA,
             pltpu.SemaphoreType.DMA((5,)),
         ],
         compiler_params=params(PREP),
@@ -415,7 +412,7 @@
     chip_terms = add(keep, swap(give, "c", 1))
     pieces = lax.all_to_all(chip_terms, NEAR, split_axis=0, concat_axis=0, tiled=True)
     mixed_own, window_next, inputs_step, in_coef, decay = pl.pallas_call(
-        mixer_kernel,
+        functools.partial(mixer_kernel, model),
         out_shape=(
             shape((own, channels), BF16),
             shape((taps - 2, own, conv_width), BF16),

time: 112 us -> 112 us (level)
  no operation moved by 1% of the time
where the time goes in v5:
time: 112 us
  blocking collectives  69.1 us (62%)
  Pallas kernels  16.8 us (15%)
  waiting for transfers between devices  11.1 us (10%)
  starting transfers between devices  7.72 us (7%)
  other arithmetic  5.09 us (5%)
    all_to_all x1, blocking collectives, local(): lax.all_to_all(chip_sum, CHIPS, split_axis=0, concat_axis=0, tiled=True)  25.7 us
    all_to_all x1, blocking collectives, local(): lax.all_to_all(chip_terms, NEAR, split_axis=0, concat_axis=0, tiled=True)  17.3 us
    all_to_all x1, blocking collectives, local(): lax.all_to_all(spread_piece, NEAR, split_axis=0, concat_axis=0, tiled=True)  16.4 us
    ppermute x7, waiting for transfers between devices, swap(): return lax.ppermute(value, axis, [(i, i ^ bit) for i in range(size)])  11.1 us
    all_to_all x1, blocking collectives, local(): lax.all_to_all(jnp.broadcast_to(mixed_own[None], (near_owners, own, chann...  9.7 us
    ppermute x7, starting transfers between devices, swap(): return lax.ppermute(value, axis, [(i, i ^ bit) for i in range(size)])  7.72 us
    pallas_call x1, Pallas kernels, local(): pl.pallas_call(project_kernel, out_shape=(pltpu.VMEM((rows // 2, sent_wid...  7.24 us
    pallas_call x2, Pallas kernels, fetch(): pl.pallas_call(fetch_kernel, out_shape=pltpu.VMEM(source.shape, source.dt...  4.4 us
  transfers between devices with their start and end apart: 7, of which 6 were waited for; matrix products, arithmetic and copies ran while one was open for 4% of the time, Pallas kernels for 4%

profile of v5, /device:TPU:0, one launch (start us, length us, event | category | flops | bytes accessed | tf_op | source)
XLA Modules:
  0.0 111.7 jit_solution(14848983065976076588)
XLA Ops:
  0.6 0.0 copy-start
  0.7 0.0 copy-start.1
  0.7 0.0 copy-start.3
  0.7 0.0 copy-start.4
  0.7 0.0 copy-start.6
  0.7 0.0 copy-start.7
  0.7 0.0 copy-start.8
  0.7 0.0 copy-start.9
  0.7 7.2 %shard_map.193 = (bf16[64,4480]{1,0:T(8,128)(2,1)S(1)}, bf16[64,4480]{1,0:T(8,128)(2,1)S(1)}, bf16[128,128]{1,0:T(8,128)(2,1)S(1)}, f32[128,128]{1,0:T(8,128)S(1)}, bf16[128,512]{1,0:T(8,128)(2,1)S(1)}) custom-call(s32[1,128]{1,0:T(1,128)} %bitcast.59, s32[1,128]{1,0:T(1,128)} %bitcast.60, bf16[128,8192]{1,0:T(8,128)(2,1)} %hidden.1, ...), custom_call_target="tpu_custom_call" | custom-call | tf_op jit(solution)/shard_map/pallas_call | solution.py:372
  8.0 0.1 collective-permute-start
  8.1 2.0 %collective-permute-done = bf16[8,8,4480]{2,1,0:T(8,128)(2,1)S(1)} collective-permute-done((bf16[8,8,4480]{2,1,0:T(8,128)(2,1)S(1)}, bf16[8,8,4480]{2,1,0:T(8,128)(2,1)S(1)}, u32[]{:S(2)}, u32[]{:S(2)}) %collective-permute-start) | collective-permute-done | bytes 573472 | tf_op jit(solution)/shard_map/ppermute | solution.py:28
  10.0 0.1 fusion.4
  10.2 17.3 %all_to_all.20.pieces = bf16[8,8,4480]{2,1,0:T(8,128)(2,1)S(1)} all-to-all(bf16[8,8,4480]{2,1,0:T(8,128)(2,1)S(1)} %fusion.4), channel_id=1, replica_groups=mesh['x'=4,'yh'=2,'z'=4,'yl'=2,'c'=2] {'z','yl'}, dimensions={0} | all-to-all | bytes 1146880 | tf_op jit(solution)/shard_map/all_to_all | solution.py:413
  27.4 0.0 copy-done.1
  27.4 0.0 copy-done.3
  27.5 0.0 copy-done.4
  27.5 0.0 copy-done.6
  27.5 0.0 copy-done.7
  27.5 0.0 copy-done.8
  27.5 0.0 copy-done.9
  27.5 2.1 %shard_map.194 = (bf16[8,2048]{1,0:T(8,128)(2,1)S(1)}, bf16[3,8,2304]{2,1,0:T(8,128)(2,1)}, f32[8,2048]{1,0:T(8,128)S(1)}, f32[8,128]{1,0:T(8,128)S(1)}, f32[8,32]{1,0:T(8,128)S(1)}) custom-call(bf16[8,8,4480]{2,1,0:T(8,128)(2,1)S(1)} %all_to_all.20.pieces, f32[128,128]{1,0:T(8,128)S(1)} %get-tuple-element.28.past, bf16[3,8,2304]{2,1,0:T(8,128)(2,1)S(1)} %bitcast.47, ...), custom_call_target="tpu_custom_call" | custom-call | tf_op jit(solution)/shard_map/pallas_call | solution.py:414
  29.7 9.7 %all_to_all.21 = bf16[8,8,2048]{2,1,0:T(8,128)(2,1)S(1)} all-to-all(bf16[8,8,2048]{2,1,0:T(8,128)(2,1)S(1)} %broadcast_in_dim.2), channel_id=1, replica_groups=mesh['x'=4,'yh'=2,'z'=4,'yl'=2,'c'=2] {'z','yl'}, dimensions={0} | all-to-all | bytes 524288 | tf_op jit(solution)/shard_map/all_to_all | solution.py:437
  39.4 0.1 mul.25
  39.4 0.0 copy-start.2
  39.5 0.1 collective-permute-start.1
  39.5 0.0 copy-done
  39.5 0.5 fusion.5
  40.0 1.0 collective-permute-done.1
  41.1 0.5 fusion.8
  41.6 1.6 %collective-permute-start.2 = (bf16[128,512]{1,0:T(8,128)(2,1)S(1)}, bf16[128,512]{1,0:T(8,128)(2,1)S(1)}, u32[]{:S(2)}, u32[]{:S(2)}) collective-permute-start(bf16[128,512]{1,0:T(8,128)(2,1)S(1)} %pad_maximum_fusion), channel_id=1, source_target_pairs={{0,32},{32,0},{64,96},{96,64},{1,33},{33,1},{65,97},{97,65},{2,34}... | collective-permute-start | bytes 393224 | tf_op jit(solution)/shard_map/ppermute | solution.py:28
  43.1 0.0 copy-done.2
  43.1 4.1 %add_convert_fusion = bf16[8,32,64,128]{3,2,1,0:T(8,128)(2,1)} fusion(bf16[8,32,64,128]{3,2,1,0:T(8,128)(2,1)S(1)} %copy-done.2, f32[8,128]{1,0:T(8,128)S(1)} %get-tuple-element.36, f32[8,32,64]{2,1,0:T(8,128)S(1)} %mul.25, f32[8,32]{1,0:T(8,128)S(1)} %get-tuple-element.34), kind=kLoop, calls=%fused_computation | loop fusion | flops 10485760 | bytes 8459264 | tf_op jit(solution)/shard_map/convert_element_type | solution.py:459
  47.2 0.0 collective-permute-done.2
  47.3 2.8 %collective-permute-start.3 = (bf16[128,512]{1,0:T(8,128)(2,1)S(1)}, bf16[128,512]{1,0:T(8,128)(2,1)S(1)}, u32[]{:S(2)}, u32[]{:S(2)}) collective-permute-start(bf16[128,512]{1,0:T(8,128)(2,1)S(1)} %add_convert_fusion.2), channel_id=1, source_target_pairs={{0,96},{32,64},{64,32},{96,0},{1,97},{33,65},{65,33},{97,1},{2,98}... | collective-permute-start | bytes 393224 | tf_op jit(solution)/shard_map/ppermute | solution.py:28
  50.1 3.8 %collective-permute-done.3 = bf16[128,512]{1,0:T(8,128)(2,1)S(1)} collective-permute-done((bf16[128,512]{1,0:T(8,128)(2,1)S(1)}, bf16[128,512]{1,0:T(8,128)(2,1)S(1)}, u32[]{:S(2)}, u32[]{:S(2)}) %collective-permute-start.3) | collective-permute-done | bytes 131104 | tf_op jit(solution)/shard_map/ppermute | solution.py:28
  53.9 3.0 %collective-permute-start.4 = (bf16[128,512]{1,0:T(8,128)(2,1)S(1)}, bf16[128,512]{1,0:T(8,128)(2,1)S(1)}, u32[]{:S(2)}, u32[]{:S(2)}) collective-permute-start(bf16[128,512]{1,0:T(8,128)(2,1)S(1)} %add_convert_fusion.1.after.mixed), channel_id=1, source_target_pairs={{0,16},{16,0},{1,17},{17,1},{2,18},{18,2},{3,19},{19,3},{4,20},{20... | collective-permute-start | bytes 393224 | tf_op jit(solution)/shard_map/ppermute | solution.py:28
  56.8 2.2 %shard_map.195.down = bf16[256,8192]{1,0:T(8,128)(2,1)S(1)} custom-call(bf16[128,512]{1,0:T(8,128)(2,1)S(1)} %add_convert_fusion.1.after.mixed, bf16[256,8192]{1,0:T(8,128)(2,1)} %source.1), custom_call_target="tpu_custom_call" | custom-call | bytes 8388608 | tf_op jit(solution)/shard_map/pallas_call | solution.py:267
  59.0 1.4 %collective-permute-done.4.other = bf16[128,512]{1,0:T(8,128)(2,1)S(1)} collective-permute-done((bf16[128,512]{1,0:T(8,128)(2,1)S(1)}, bf16[128,512]{1,0:T(8,128)(2,1)S(1)}, u32[]{:S(2)}, u32[]{:S(2)}) %collective-permute-start.4) | collective-permute-done | bytes 131104 | tf_op jit(solution)/shard_map/ppermute | solution.py:28
  60.4 0.2 shard_map.196
  60.7 16.4 %all_to_all.22.after.near = bf16[8,128,512]{2,1,0:T(8,128)(2,1)S(1)} all-to-all(bf16[8,128,512]{2,1,0:T(8,128)(2,1)S(1)} %shard_map.196), channel_id=1, replica_groups=mesh['x'=4,'yh'=2,'z'=4,'yl'=2,'c'=2] {'z','yl'}, dimensions={0} | all-to-all | bytes 2097152 | tf_op jit(solution)/shard_map/all_to_all | solution.py:475
  77.1 0.0 collective-permute-start.5
  77.1 0.0 copy-start.5
  77.1 2.2 %shard_map.197.up = bf16[16,512,256]{2,1,0:T(8,128)(2,1)S(1)} custom-call(bf16[8,128,512]{2,1,0:T(8,128)(2,1)S(1)} %all_to_all.22.after.near, bf16[16,512,256]{2,1,0:T(8,128)(2,1)} %bitcast.55), custom_call_target="tpu_custom_call" | custom-call | bytes 8388608 | tf_op jit(solution)/shard_map/pallas_call | solution.py:267
  79.3 0.4 collective-permute-done.5.far
  79.7 0.0 copy-done.5
  79.7 2.5 %shard_map.198 = (bf16[64,64,128]{2,1,0:T(8,128)(2,1)S(1)}, bf16[64,64,128]{2,1,0:T(8,128)(2,1)S(1)}, f32[64,128]{1,0:T(8,128)S(1)}) custom-call(bf16[8,128,512]{2,1,0:T(8,128)(2,1)S(1)} %all_to_all.22.after.near, bf16[8,128,512]{2,1,0:T(8,128)(2,1)S(1)} %collective-permute-done.5.far, bf16[64,128]{1,0:T(8,128)(2,1)S(1)} %bitcast.49, ...), custom_call_target="tpu_custom_call" | custom-call | tf_op jit(solution)/shard_map/pallas_call | solution.py:481
  82.2 0.2 collective-permute-start.6
  82.4 2.5 %collective-permute-done.6.right = bf16[64,64,128]{2,1,0:T(8,128)(2,1)S(1)} collective-permute-done((bf16[64,64,128]{2,1,0:T(8,128)(2,1)S(1)}, bf16[64,64,128]{2,1,0:T(8,128)(2,1)S(1)}, u32[]{:S(2)}, u32[]{:S(2)}) %collective-permute-start.6) | collective-permute-done | bytes 1048608 | tf_op jit(solution)/shard_map/ppermute | solution.py:28
  85.0 0.2 shard_map.199
  85.2 25.7 %all_to_all.23 = bf16[64,64,128]{2,1,0:T(8,128)(2,1)S(1)} all-to-all(bf16[64,64,128]{2,1,0:T(8,128)(2,1)S(1)} %shard_map.199), channel_id=1, replica_groups=mesh['x'=4,'yh'=2,'z'=4,'yl'=2,'c'=2] {'x','yh','z','yl'}, dimensions={0} | all-to-all | bytes 2097152 | tf_op jit(solution)/shard_map/all_to_all | solution.py:509
  110.9 0.2 convert_reduce_fusion
  111.1 0.6 fusion.13
  (4 shorter events, 0.1 us)
Async XLA Ops:
  0.6 38.9 %copy-start = (bf16[1,2048,512]{2,1,0:T(8,128)(2,1)S(1)}, bf16[1,2048,512]{2,1,0:T(8,128)(2,1)}, u32[]{:S(2)}) copy-start(bf16[1,2048,512]{2,1,0:T(8,128)(2,1)} %param.32) | copy-start | bytes 6291460
  0.7 26.8 %copy-start.1 = (bf16[8,32,64,128]{3,2,1,0:T(8,128)(2,1)S(1)}, bf16[8,32,64,128]{3,2,1,0:T(8,128)(2,1)}, u32[]{:S(2)}) copy-start(bf16[8,32,64,128]{3,2,1,0:T(8,128)(2,1)} %param.30) | copy-start | bytes 12582916
  0.7 26.8 %copy-start.3 = (bf16[8,3,1,2304]{3,0,2,1:T(8,128)(2,1)S(1)}, bf16[8,3,1,2304]{3,0,2,1:T(8,128)(2,1)}, u32[]{:S(2)}) copy-start(bf16[8,3,1,2304]{3,0,2,1:T(8,128)(2,1)} %param.29) | copy-start | bytes 331780
  0.7 26.8 %copy-start.4 = (bf16[5,1,2304]{2,0,1:T(8,128)(2,1)S(1)}, bf16[5,1,2304]{2,0,1:T(8,128)(2,1)}, u32[]{:S(2)}) copy-start(bf16[5,1,2304]{2,0,1:T(8,128)(2,1)} %param.28) | copy-start | bytes 69124
  0.7 26.8 %copy-start.6 = (bf16[1,2048]{1,0:T(2,128)(2,1)S(1)}, bf16[1,2048]{1,0:T(2,128)(2,1)}, u32[]{:S(2)}) copy-start(bf16[1,2048]{1,0:T(2,128)(2,1)} %gain.1) | copy-start | bytes 12292
  0.7 26.8 %copy-start.7 = (f32[32]{0:T(128)S(1)}, f32[32]{0:T(128)}, u32[]{:S(2)}) copy-start(f32[32]{0:T(128)} %param.25) | copy-start | bytes 388
  0.7 26.8 %copy-start.8 = (f32[32]{0:T(128)S(1)}, f32[32]{0:T(128)}, u32[]{:S(2)}) copy-start(f32[32]{0:T(128)} %param.26) | copy-start | bytes 388
  0.7 26.8 %copy-start.9 = (f32[32]{0:T(128)S(1)}, f32[32]{0:T(128)}, u32[]{:S(2)}) copy-start(f32[32]{0:T(128)} %param.27) | copy-start | bytes 388
  8.0 2.1 %collective-permute-start = (bf16[8,8,4480]{2,1,0:T(8,128)(2,1)S(1)}, bf16[8,8,4480]{2,1,0:T(8,128)(2,1)S(1)}, u32[]{:S(2)}, u32[]{:S(2)}) collective-permute-start(bf16[8,8,4480]{2,1,0:T(8,128)(2,1)S(1)} %bitcast.53), channel_id=1, source_target_pairs={{0,1},{1,0},{2,3},{3,2},{4,5},{5,4},{6,7},{7,6},{8,9},{9,8},{10,11... | collective-permute-start | bytes 1720328 | tf_op jit(solution)/shard_map/ppermute | solution.py:28
  39.4 3.7 %copy-start.2 = (bf16[8,32,64,128]{3,2,1,0:T(8,128)(2,1)S(1)}, bf16[8,32,64,128]{3,2,1,0:T(8,128)(2,1)}, u32[]{:S(2)}) copy-start(bf16[8,32,64,128]{3,2,1,0:T(8,128)(2,1)} %param.30) | copy-start | bytes 12582916
  39.5 1.6 %collective-permute-start.1 = (bf16[8,8,2048]{2,1,0:T(8,128)(2,1)S(1)}, bf16[8,8,2048]{2,1,0:T(8,128)(2,1)S(1)}, u32[]{:S(2)}, u32[]{:S(2)}) collective-permute-start(bf16[8,8,2048]{2,1,0:T(8,128)(2,1)S(1)} %all_to_all.21), channel_id=1, source_target_pairs={{0,1},{1,0},{2,3},{3,2},{4,5},{5,4},{6,7},{7,6},{8,9},{9,8},{10,11... | collective-permute-start | bytes 786440 | tf_op jit(solution)/shard_map/ppermute | solution.py:28
  41.6 5.7 %collective-permute-start.2 = (bf16[128,512]{1,0:T(8,128)(2,1)S(1)}, bf16[128,512]{1,0:T(8,128)(2,1)S(1)}, u32[]{:S(2)}, u32[]{:S(2)}) collective-permute-start(bf16[128,512]{1,0:T(8,128)(2,1)S(1)} %pad_maximum_fusion), channel_id=1, source_target_pairs={{0,32},{32,0},{64,96},{96,64},{1,33},{33,1},{65,97},{97,65},{2,34}... | collective-permute-start | bytes 393224 | tf_op jit(solution)/shard_map/ppermute | solution.py:28
  47.3 6.5 %collective-permute-start.3 = (bf16[128,512]{1,0:T(8,128)(2,1)S(1)}, bf16[128,512]{1,0:T(8,128)(2,1)S(1)}, u32[]{:S(2)}, u32[]{:S(2)}) collective-permute-start(bf16[128,512]{1,0:T(8,128)(2,1)S(1)} %add_convert_fusion.2), channel_id=1, source_target_pairs={{0,96},{32,64},{64,32},{96,0},{1,97},{33,65},{65,33},{97,1},{2,98}... | collective-permute-start | bytes 393224 | tf_op jit(solution)/shard_map/ppermute | solution.py:28
  53.9 6.6 %collective-permute-start.4 = (bf16[128,512]{1,0:T(8,128)(2,1)S(1)}, bf16[128,512]{1,0:T(8,128)(2,1)S(1)}, u32[]{:S(2)}, u32[]{:S(2)}) collective-permute-start(bf16[128,512]{1,0:T(8,128)(2,1)S(1)} %add_convert_fusion.1.after.mixed), channel_id=1, source_target_pairs={{0,16},{16,0},{1,17},{17,1},{2,18},{18,2},{3,19},{19,3},{4,20},{20... | collective-permute-start | bytes 393224 | tf_op jit(solution)/shard_map/ppermute | solution.py:28
  77.1 2.7 %collective-permute-start.5 = (bf16[8,128,512]{2,1,0:T(8,128)(2,1)S(1)}, bf16[8,128,512]{2,1,0:T(8,128)(2,1)S(1)}, u32[]{:S(2)}, u32[]{:S(2)}) collective-permute-start(bf16[8,128,512]{2,1,0:T(8,128)(2,1)S(1)} %all_to_all.22.after.near), channel_id=1, source_target_pairs={{0,1},{1,0},{2,3},{3,2},{4,5},{5,4},{6,7},{7,6},{8,9},{9,8},{10,11... | collective-permute-start | bytes 3145736 | tf_op jit(solution)/shard_map/ppermute | solution.py:28
  77.1 2.7 %copy-start.5 = (bf16[8192]{0:T(1024)(128)(2,1)S(1)}, bf16[8192]{0:T(1024)(128)(2,1)}, u32[]{:S(2)}) copy-start(bf16[8192]{0:T(1024)(128)(2,1)} %param.33) | copy-start | bytes 49156
  82.2 2.7 %collective-permute-start.6 = (bf16[64,64,128]{2,1,0:T(8,128)(2,1)S(1)}, bf16[64,64,128]{2,1,0:T(8,128)(2,1)S(1)}, u32[]{:S(2)}, u32[]{:S(2)}) collective-permute-start(bf16[64,64,128]{2,1,0:T(8,128)(2,1)S(1)} %get-tuple-element.46), channel_id=1, source_target_pairs={{0,1},{1,0},{2,3},{3,2},{4,5},{5,4},{6,7},{7,6},{8,9},{9,8},{10,11... | collective-permute-start | bytes 3145736 | tf_op jit(solution)/shard_map/ppermute | solution.py:28

commit v6 on v5

--- a/solution.py
+++ b/solution.py
@@ -62,8 +62,11 @@
     weights,
     select,
     step,
-    keep,
-    give,
+    far_tail,
+    far_left,
+    near_tail,
+    near_left,
+    tiles,
     order,
     past,
     base,
@@ -72,7 +75,6 @@
     history_held,
     gain_held,
     gains,
-    tiles,
     select_held,
     step_held,
     sems,
@@ -142,31 +144,35 @@
         axis=1,
     )
     odd = pltpu.roll(even, 1, axis=1)
-    left = jnp.concatenate([even.astype(BF16), odd.astype(BF16)], axis=0)
-
-    def put(at, values):
-        width = values.shape[1]
-        for out, part in ((keep, values[:half]), (give, values[half:])):
-            out[:, at : at + width] = part.astype(BF16)
-
-    for i in range(0, count, 2):
-        copies[i].wait()
-        copies[i + 1].wait()
-        right = jnp.concatenate(
-            [tiles.at[i + k].reshape(2 * part, LANES)[...] for k in range(2)], axis=1
-        )
-        both = jnp.dot(left, right, preferred_element_type=F32)
-        put(i * LANES, both[:rows])
-        put((count + i) * LANES, both[rows:])
+    even, odd = even.astype(BF16), odd.astype(BF16)
+    near_left[...] = jnp.concatenate([even[:half], odd[:half]], axis=0)
+    far_left[...] = jnp.concatenate([even[half:], odd[half:]], axis=0)
     for copy in smalls[3:]:
         copy.wait()
-    both = jnp.dot(left, select_held[...], preferred_element_type=F32)
-    at = 2 * count * LANES
-    put(at, both[:rows])
-    put(at + LANES, both[rows:])
     steps = contract(plain, step_held[...], 1, 1)
     missing = LANES - steps.shape[1] - 1
-    put(at + 2 * LANES, jnp.concatenate([steps, squares, jnp.zeros((rows, missing), F32)], axis=1))
+    steps = jnp.concatenate([steps, squares, jnp.zeros((rows, missing), F32)], axis=1)
+    for out, left, part_steps in (
+        (near_tail, near_left, steps[:half]),
+        (far_tail, far_left, steps[half:]),
+    ):
+        both = jnp.dot(left[...], select_held[...], preferred_element_type=F32)
+        out[:, :LANES] = both[:half].astype(BF16)
+        out[:, LANES : 2 * LANES] = both[half:].astype(BF16)
+        out[:, 2 * LANES :] = part_steps.astype(BF16)
+    for copy in copies:
+        copy.wait()
+
+
+def half_kernel(left, tiles, tail, out):
+    count = tiles.shape[0]
+    half = out.shape[0]
+    for i in range(0, count, 2):
+        right = jnp.concatenate([tiles[i], tiles[i + 1]], axis=1)
+        both = jnp.dot(left[...], right, preferred_element_type=F32)
+        out[:, i * LANES : (i + 2) * LANES] = both[:half].astype(BF16)
+        out[:, (count + i) * LANES : (count + i + 2) * LANES] = both[half:].astype(BF16)
+    out[:, 2 * count * LANES :] = tail[...]
 
 
 def mixer_kernel(
@@ -369,24 +375,26 @@
     tiled = inner_proj.reshape(part, 2, tile_count, LANES).transpose(0, 2, 1, 3)
     sent_width = 2 * channels + 2 * state_size + LANES
     near_owners = heads_axis // 2
-    keep, give, order, past, base = pl.pallas_call(
+    far_tail, far_left, near_tail, near_left, tiles, order, past, base = pl.pallas_call(
         project_kernel,
         out_shape=(
-            pltpu.VMEM((rows // 2, sent_width), BF16),
-            pltpu.VMEM((rows // 2, sent_width), BF16),
+            pltpu.VMEM((rows // 2, sent_width - 2 * channels), BF16),
+            pltpu.VMEM((rows, 2 * part), BF16),
+            pltpu.VMEM((rows // 2, sent_width - 2 * channels), BF16),
+            pltpu.VMEM((rows, 2 * part), BF16),
+            pltpu.VMEM((tile_count, part, 2, LANES), BF16),
             shape((rows, rows), BF16),
             pltpu.VMEM((rows, LANES), F32),
             shape((rows, part), BF16),
         ),
         in_specs=[HBM] * 7,
-        out_specs=(VMEM,) * 5,
+        out_specs=(VMEM,) * 8,
         scratch_shapes=[
             pltpu.VMEM((rows, part), BF16),
             pltpu.VMEM((1, rows), jnp.int32),
             pltpu.VMEM((1, rows), jnp.int32),
             pltpu.VMEM((model // LANES, LANES), BF16),
             pltpu.VMEM((model // LANES, LANES), F32),
-            pltpu.VMEM((tile_count, part, 2, LANES), BF16),
             pltpu.VMEM((2 * part, state_size), BF16),
             pltpu.VMEM((heads, part), BF16),
             pltpu.SemaphoreType.DMA((tile_count,)),
@@ -408,6 +416,19 @@
             )
         )
     )
+    half_call = pl.pallas_call(
+        half_kernel,
+        out_shape=pltpu.VMEM((rows // 2, sent_width), BF16),
+        in_specs=[VMEM] * 3,
+        out_specs=VMEM,
+        compiler_params=params(8),
+        cost_estimate=pl.CostEstimate(
+            flops=8 * rows * part * channels, bytes_accessed=8 * part * channels, transcendentals=0
+        ),
+    )
+    tiles = tiles.reshape(tile_count, 2 * part, LANES)
+    give = half_call(far_left, tiles, far_tail)
+    keep = half_call(near_left, tiles, near_tail)
     keep, give = (value.reshape(near_owners, own, sent_width) for value in (keep, give))
     chip_terms = add(keep, swap(give, "c", 1))
     pieces = lax.all_to_all(chip_terms, NEAR, split_axis=0, concat_axis=0, tiled=True)

time: 112 us -> 109 us (0.973)
  Pallas kernels: 16.8 us -> 14.6 us
    pallas_call x1, Pallas kernels: 7.24 us -> 3.65 us  [local(): pl.pallas_call(project_kernel, out_shape=(pltpu.VMEM((rows // 2, sent_wid...]
    pallas_call x0 -> x2, Pallas kernels: none -> 1.46 us  [the longest x1 0.74 us: local(): keep = half_call(near_left, tiles, near_tail)]
  transfers between devices with their start and end apart: 7 -> 7, of which waited for: 6 -> 6; matrix products, arithmetic and copies ran while one was open for 4% -> 4% of each run, Pallas kernels for 4% -> 5%
where the time goes in v6:
time: 109 us
  blocking collectives  69.1 us (63%)
  Pallas kernels  14.6 us (13%)
  waiting for transfers between devices  10.4 us (10%)
  starting transfers between devices  7.71 us (7%)
  other arithmetic  5.09 us (5%)
    all_to_all x1, blocking collectives, local(): lax.all_to_all(chip_sum, CHIPS, split_axis=0, concat_axis=0, tiled=True)  25.7 us
    all_to_all x1, blocking collectives, local(): lax.all_to_all(chip_terms, NEAR, split_axis=0, concat_axis=0, tiled=True)  17.3 us
    all_to_all x1, blocking collectives, local(): lax.all_to_all(spread_piece, NEAR, split_axis=0, concat_axis=0, tiled=True)  16.4 us
    ppermute x7, waiting for transfers between devices, swap(): return lax.ppermute(value, axis, [(i, i ^ bit) for i in range(size)])  10.4 us
    all_to_all x1, blocking collectives, local(): lax.all_to_all(jnp.broadcast_to(mixed_own[None], (near_owners, own, chann...  9.7 us
    ppermute x7, starting transfers between devices, swap(): return lax.ppermute(value, axis, [(i, i ^ bit) for i in range(size)])  7.71 us
    pallas_call x2, Pallas kernels, fetch(): pl.pallas_call(fetch_kernel, out_shape=pltpu.VMEM(source.shape, source.dt...  4.4 us
    convert_element_type x1, other arithmetic, local(): state_next = (decay[..., None, None] * state_cache.astype(F32) + step_inp...  4.09 us
  transfers between devices with their start and end apart: 7, of which 6 were waited for; matrix products, arithmetic and copies ran while one was open for 4% of the time, Pallas kernels for 5%

profile of v6, /device:TPU:0, one launch (start us, length us, event | category | flops | bytes accessed | tf_op | source)
XLA Modules:
  0.0 108.8 jit_solution(4717084837416947191)
XLA Ops:
  0.6 0.0 copy-start
  0.6 3.7 %shard_map.193 = (bf16[64,384]{1,0:T(8,128)(2,1)S(1)}, bf16[128,1024]{1,0:T(8,128)(2,1)S(1)}, bf16[64,384]{1,0:T(8,128)(2,1)S(1)}, bf16[128,1024]{1,0:T(8,128)(2...) custom-call(s32[1,128]{1,0:T(1,128)} %bitcast.62, ...), custom_call_target="tpu_custom_call" | custom-call | tf_op jit(solution)/shard_map/pallas_call | solution.py:378
  4.3 0.7 shard_map.195
  5.0 0.0 copy-start.1
  5.0 0.0 copy-start.3
  5.1 0.0 copy-start.4
  5.1 0.0 copy-start.6
  5.1 0.0 copy-start.7
  5.1 0.0 copy-start.8
  5.1 0.0 copy-start.9
  5.1 0.1 collective-permute-start
  5.2 0.7 shard_map.194
  6.0 1.2 %collective-permute-done = bf16[8,8,4480]{2,1,0:T(8,128)(2,1)S(1)} collective-permute-done((bf16[8,8,4480]{2,1,0:T(8,128)(2,1)S(1)}, bf16[8,8,4480]{2,1,0:T(8,128)(2,1)S(1)}, u32[]{:S(2)}, u32[]{:S(2)}) %collective-permute-start) | collective-permute-done | bytes 573472 | tf_op jit(solution)/shard_map/ppermute | solution.py:28
  7.2 0.1 fusion.4
  7.3 17.3 %all_to_all.20.pieces = bf16[8,8,4480]{2,1,0:T(8,128)(2,1)S(1)} all-to-all(bf16[8,8,4480]{2,1,0:T(8,128)(2,1)S(1)} %fusion.4), channel_id=1, replica_groups=mesh['x'=4,'yh'=2,'z'=4,'yl'=2,'c'=2] {'z','yl'}, dimensions={0} | all-to-all | bytes 1146880 | tf_op jit(solution)/shard_map/all_to_all | solution.py:434
  24.6 0.0 copy-done.1
  24.6 0.0 copy-done.3
  24.6 0.0 copy-done.4
  24.6 0.0 copy-done.6
  24.6 0.0 copy-done.7
  24.6 0.0 copy-done.8
  24.6 0.0 copy-done.9
  24.6 2.1 %shard_map.196 = (bf16[8,2048]{1,0:T(8,128)(2,1)S(1)}, bf16[3,8,2304]{2,1,0:T(8,128)(2,1)}, f32[8,2048]{1,0:T(8,128)S(1)}, f32[8,128]{1,0:T(8,128)S(1)}, f32[8,32]{1,0:T(8,128)S(1)}) custom-call(bf16[8,8,4480]{2,1,0:T(8,128)(2,1)S(1)} %all_to_all.20.pieces, f32[128,128]{1,0:T(8,128)S(1)} %get-tuple-element.34.past, bf16[3,8,2304]{2,1,0:T(8,128)(2,1)S(1)} %bitcast.51, ...), custom_call_target="tpu_custom_call" | custom-call | tf_op jit(solution)/shard_map/pallas_call | solution.py:435
  26.8 9.7 %all_to_all.21 = bf16[8,8,2048]{2,1,0:T(8,128)(2,1)S(1)} all-to-all(bf16[8,8,2048]{2,1,0:T(8,128)(2,1)S(1)} %broadcast_in_dim.2), channel_id=1, replica_groups=mesh['x'=4,'yh'=2,'z'=4,'yl'=2,'c'=2] {'z','yl'}, dimensions={0} | all-to-all | bytes 524288 | tf_op jit(solution)/shard_map/all_to_all | solution.py:458
  36.5 0.1 mul.25
  36.6 0.0 copy-start.2
  36.6 0.1 collective-permute-start.1
  36.7 0.0 copy-done
  36.7 0.5 fusion.5
  37.2 1.0 collective-permute-done.1
  38.2 0.5 fusion.8
  38.7 1.6 %collective-permute-start.2 = (bf16[128,512]{1,0:T(8,128)(2,1)S(1)}, bf16[128,512]{1,0:T(8,128)(2,1)S(1)}, u32[]{:S(2)}, u32[]{:S(2)}) collective-permute-start(bf16[128,512]{1,0:T(8,128)(2,1)S(1)} %pad_maximum_fusion), channel_id=1, source_target_pairs={{0,32},{32,0},{64,96},{96,64},{1,33},{33,1},{65,97},{97,65},{2,34}... | collective-permute-start | bytes 393224 | tf_op jit(solution)/shard_map/ppermute | solution.py:28
  40.3 0.0 copy-done.2
  40.3 4.1 %add_convert_fusion = bf16[8,32,64,128]{3,2,1,0:T(8,128)(2,1)} fusion(bf16[8,32,64,128]{3,2,1,0:T(8,128)(2,1)S(1)} %copy-done.2, f32[8,128]{1,0:T(8,128)S(1)} %get-tuple-element.42, f32[8,32,64]{2,1,0:T(8,128)S(1)} %mul.25, f32[8,32]{1,0:T(8,128)S(1)} %get-tuple-element.40), kind=kLoop, calls=%fused_computation | loop fusion | flops 10485760 | bytes 8459264 | tf_op jit(solution)/shard_map/convert_element_type | solution.py:480
  44.4 0.0 collective-permute-done.2
  44.4 2.8 %collective-permute-start.3 = (bf16[128,512]{1,0:T(8,128)(2,1)S(1)}, bf16[128,512]{1,0:T(8,128)(2,1)S(1)}, u32[]{:S(2)}, u32[]{:S(2)}) collective-permute-start(bf16[128,512]{1,0:T(8,128)(2,1)S(1)} %add_convert_fusion.2), channel_id=1, source_target_pairs={{0,96},{32,64},{64,32},{96,0},{1,97},{33,65},{65,33},{97,1},{2,98}... | collective-permute-start | bytes 393224 | tf_op jit(solution)/shard_map/ppermute | solution.py:28
  47.2 3.8 %collective-permute-done.3 = bf16[128,512]{1,0:T(8,128)(2,1)S(1)} collective-permute-done((bf16[128,512]{1,0:T(8,128)(2,1)S(1)}, bf16[128,512]{1,0:T(8,128)(2,1)S(1)}, u32[]{:S(2)}, u32[]{:S(2)}) %collective-permute-start.3) | collective-permute-done | bytes 131104 | tf_op jit(solution)/shard_map/ppermute | solution.py:28
  51.0 3.0 %collective-permute-start.4 = (bf16[128,512]{1,0:T(8,128)(2,1)S(1)}, bf16[128,512]{1,0:T(8,128)(2,1)S(1)}, u32[]{:S(2)}, u32[]{:S(2)}) collective-permute-start(bf16[128,512]{1,0:T(8,128)(2,1)S(1)} %add_convert_fusion.1.after.mixed), channel_id=1, source_target_pairs={{0,16},{16,0},{1,17},{17,1},{2,18},{18,2},{3,19},{19,3},{4,20},{20... | collective-permute-start | bytes 393224 | tf_op jit(solution)/shard_map/ppermute | solution.py:28
  54.0 2.2 %shard_map.197.down = bf16[256,8192]{1,0:T(8,128)(2,1)S(1)} custom-call(bf16[128,512]{1,0:T(8,128)(2,1)S(1)} %add_convert_fusion.1.after.mixed, bf16[256,8192]{1,0:T(8,128)(2,1)} %source.1), custom_call_target="tpu_custom_call" | custom-call | bytes 8388608 | tf_op jit(solution)/shard_map/pallas_call | solution.py:273
  56.2 1.4 %collective-permute-done.4.other = bf16[128,512]{1,0:T(8,128)(2,1)S(1)} collective-permute-done((bf16[128,512]{1,0:T(8,128)(2,1)S(1)}, bf16[128,512]{1,0:T(8,128)(2,1)S(1)}, u32[]{:S(2)}, u32[]{:S(2)}) %collective-permute-start.4) | collective-permute-done | bytes 131104 | tf_op jit(solution)/shard_map/ppermute | solution.py:28
  57.5 0.2 shard_map.198
  57.8 16.4 %all_to_all.22.after.near = bf16[8,128,512]{2,1,0:T(8,128)(2,1)S(1)} all-to-all(bf16[8,128,512]{2,1,0:T(8,128)(2,1)S(1)} %shard_map.198), channel_id=1, replica_groups=mesh['x'=4,'yh'=2,'z'=4,'yl'=2,'c'=2] {'z','yl'}, dimensions={0} | all-to-all | bytes 2097152 | tf_op jit(solution)/shard_map/all_to_all | solution.py:496
  74.2 0.0 collective-permute-start.5
  74.2 0.0 copy-start.5
  74.2 2.2 %shard_map.199.up = bf16[16,512,256]{2,1,0:T(8,128)(2,1)S(1)} custom-call(bf16[8,128,512]{2,1,0:T(8,128)(2,1)S(1)} %all_to_all.22.after.near, bf16[16,512,256]{2,1,0:T(8,128)(2,1)} %bitcast.58), custom_call_target="tpu_custom_call" | custom-call | bytes 8388608 | tf_op jit(solution)/shard_map/pallas_call | solution.py:273
  76.4 0.4 collective-permute-done.5.far
  76.9 0.0 copy-done.5
  76.9 2.5 %shard_map.200 = (bf16[64,64,128]{2,1,0:T(8,128)(2,1)S(1)}, bf16[64,64,128]{2,1,0:T(8,128)(2,1)S(1)}, f32[64,128]{1,0:T(8,128)S(1)}) custom-call(bf16[8,128,512]{2,1,0:T(8,128)(2,1)S(1)} %all_to_all.22.after.near, bf16[8,128,512]{2,1,0:T(8,128)(2,1)S(1)} %collective-permute-done.5.far, bf16[64,128]{1,0:T(8,128)(2,1)S(1)} %bitcast.53, ...), custom_call_target="tpu_custom_call" | custom-call | tf_op jit(solution)/shard_map/pallas_call | solution.py:502
  79.4 0.2 collective-permute-start.6
  79.6 2.5 %collective-permute-done.6.right = bf16[64,64,128]{2,1,0:T(8,128)(2,1)S(1)} collective-permute-done((bf16[64,64,128]{2,1,0:T(8,128)(2,1)S(1)}, bf16[64,64,128]{2,1,0:T(8,128)(2,1)S(1)}, u32[]{:S(2)}, u32[]{:S(2)}) %collective-permute-start.6) | collective-permute-done | bytes 1048608 | tf_op jit(solution)/shard_map/ppermute | solution.py:28
  82.1 0.2 shard_map.201
  82.3 25.7 %all_to_all.23 = bf16[64,64,128]{2,1,0:T(8,128)(2,1)S(1)} all-to-all(bf16[64,64,128]{2,1,0:T(8,128)(2,1)S(1)} %shard_map.201), channel_id=1, replica_groups=mesh['x'=4,'yh'=2,'z'=4,'yl'=2,'c'=2] {'x','yh','z','yl'}, dimensions={0} | all-to-all | bytes 2097152 | tf_op jit(solution)/shard_map/all_to_all | solution.py:530
  108.0 0.2 convert_reduce_fusion
  108.2 0.6 fusion.13
  (4 shorter events, 0.1 us)
Async XLA Ops:
  0.6 36.1 %copy-start = (bf16[1,2048,512]{2,1,0:T(8,128)(2,1)S(1)}, bf16[1,2048,512]{2,1,0:T(8,128)(2,1)}, u32[]{:S(2)}) copy-start(bf16[1,2048,512]{2,1,0:T(8,128)(2,1)} %param.32) | copy-start | bytes 6291460
  5.0 19.6 %copy-start.1 = (bf16[8,32,64,128]{3,2,1,0:T(8,128)(2,1)S(1)}, bf16[8,32,64,128]{3,2,1,0:T(8,128)(2,1)}, u32[]{:S(2)}) copy-start(bf16[8,32,64,128]{3,2,1,0:T(8,128)(2,1)} %param.30) | copy-start | bytes 12582916
  5.0 19.6 %copy-start.3 = (bf16[8,3,1,2304]{3,0,2,1:T(8,128)(2,1)S(1)}, bf16[8,3,1,2304]{3,0,2,1:T(8,128)(2,1)}, u32[]{:S(2)}) copy-start(bf16[8,3,1,2304]{3,0,2,1:T(8,128)(2,1)} %param.29) | copy-start | bytes 331780
  5.1 19.5 %copy-start.4 = (bf16[5,1,2304]{2,0,1:T(8,128)(2,1)S(1)}, bf16[5,1,2304]{2,0,1:T(8,128)(2,1)}, u32[]{:S(2)}) copy-start(bf16[5,1,2304]{2,0,1:T(8,128)(2,1)} %param.28) | copy-start | bytes 69124
  5.1 19.5 %copy-start.6 = (bf16[1,2048]{1,0:T(2,128)(2,1)S(1)}, bf16[1,2048]{1,0:T(2,128)(2,1)}, u32[]{:S(2)}) copy-start(bf16[1,2048]{1,0:T(2,128)(2,1)} %gain.1) | copy-start | bytes 12292
  5.1 19.5 %copy-start.7 = (f32[32]{0:T(128)S(1)}, f32[32]{0:T(128)}, u32[]{:S(2)}) copy-start(f32[32]{0:T(128)} %param.25) | copy-start | bytes 388
  5.1 19.5 %copy-start.8 = (f32[32]{0:T(128)S(1)}, f32[32]{0:T(128)}, u32[]{:S(2)}) copy-start(f32[32]{0:T(128)} %param.26) | copy-start | bytes 388
  5.1 19.5 %copy-start.9 = (f32[32]{0:T(128)S(1)}, f32[32]{0:T(128)}, u32[]{:S(2)}) copy-start(f32[32]{0:T(128)} %param.27) | copy-start | bytes 388
  5.1 2.1 %collective-permute-start = (bf16[8,8,4480]{2,1,0:T(8,128)(2,1)S(1)}, bf16[8,8,4480]{2,1,0:T(8,128)(2,1)S(1)}, u32[]{:S(2)}, u32[]{:S(2)}) collective-permute-start(bf16[8,8,4480]{2,1,0:T(8,128)(2,1)S(1)} %bitcast.50), channel_id=1, source_target_pairs={{0,1},{1,0},{2,3},{3,2},{4,5},{5,4},{6,7},{7,6},{8,9},{9,8},{10,11... | collective-permute-start | bytes 1720328 | tf_op jit(solution)/shard_map/ppermute | solution.py:28
  36.6 3.7 %copy-start.2 = (bf16[8,32,64,128]{3,2,1,0:T(8,128)(2,1)S(1)}, bf16[8,32,64,128]{3,2,1,0:T(8,128)(2,1)}, u32[]{:S(2)}) copy-start(bf16[8,32,64,128]{3,2,1,0:T(8,128)(2,1)} %param.30) | copy-start | bytes 12582916
  36.6 1.6 %collective-permute-start.1 = (bf16[8,8,2048]{2,1,0:T(8,128)(2,1)S(1)}, bf16[8,8,2048]{2,1,0:T(8,128)(2,1)S(1)}, u32[]{:S(2)}, u32[]{:S(2)}) collective-permute-start(bf16[8,8,2048]{2,1,0:T(8,128)(2,1)S(1)} %all_to_all.21), channel_id=1, source_target_pairs={{0,1},{1,0},{2,3},{3,2},{4,5},{5,4},{6,7},{7,6},{8,9},{9,8},{10,11... | collective-permute-start | bytes 786440 | tf_op jit(solution)/shard_map/ppermute | solution.py:28
  38.7 5.7 %collective-permute-start.2 = (bf16[128,512]{1,0:T(8,128)(2,1)S(1)}, bf16[128,512]{1,0:T(8,128)(2,1)S(1)}, u32[]{:S(2)}, u32[]{:S(2)}) collective-permute-start(bf16[128,512]{1,0:T(8,128)(2,1)S(1)} %pad_maximum_fusion), channel_id=1, source_target_pairs={{0,32},{32,0},{64,96},{96,64},{1,33},{33,1},{65,97},{97,65},{2,34}... | collective-permute-start | bytes 393224 | tf_op jit(solution)/shard_map/ppermute | solution.py:28
  44.4 6.5 %collective-permute-start.3 = (bf16[128,512]{1,0:T(8,128)(2,1)S(1)}, bf16[128,512]{1,0:T(8,128)(2,1)S(1)}, u32[]{:S(2)}, u32[]{:S(2)}) collective-permute-start(bf16[128,512]{1,0:T(8,128)(2,1)S(1)} %add_convert_fusion.2), channel_id=1, source_target_pairs={{0,96},{32,64},{64,32},{96,0},{1,97},{33,65},{65,33},{97,1},{2,98}... | collective-permute-start | bytes 393224 | tf_op jit(solution)/shard_map/ppermute | solution.py:28
  51.0 6.6 %collective-permute-start.4 = (bf16[128,512]{1,0:T(8,128)(2,1)S(1)}, bf16[128,512]{1,0:T(8,128)(2,1)S(1)}, u32[]{:S(2)}, u32[]{:S(2)}) collective-permute-start(bf16[128,512]{1,0:T(8,128)(2,1)S(1)} %add_convert_fusion.1.after.mixed), channel_id=1, source_target_pairs={{0,16},{16,0},{1,17},{17,1},{2,18},{18,2},{3,19},{19,3},{4,20},{20... | collective-permute-start | bytes 393224 | tf_op jit(solution)/shard_map/ppermute | solution.py:28
  74.2 2.7 %collective-permute-start.5 = (bf16[8,128,512]{2,1,0:T(8,128)(2,1)S(1)}, bf16[8,128,512]{2,1,0:T(8,128)(2,1)S(1)}, u32[]{:S(2)}, u32[]{:S(2)}) collective-permute-start(bf16[8,128,512]{2,1,0:T(8,128)(2,1)S(1)} %all_to_all.22.after.near), channel_id=1, source_target_pairs={{0,1},{1,0},{2,3},{3,2},{4,5},{5,4},{6,7},{7,6},{8,9},{9,8},{10,11... | collective-permute-start | bytes 3145736 | tf_op jit(solution)/shard_map/ppermute | solution.py:28
  74.2 2.7 %copy-start.5 = (bf16[8192]{0:T(1024)(128)(2,1)S(1)}, bf16[8192]{0:T(1024)(128)(2,1)}, u32[]{:S(2)}) copy-start(bf16[8192]{0:T(1024)(128)(2,1)} %param.33) | copy-start | bytes 49156
  79.4 2.7 %collective-permute-start.6 = (bf16[64,64,128]{2,1,0:T(8,128)(2,1)S(1)}, bf16[64,64,128]{2,1,0:T(8,128)(2,1)S(1)}, u32[]{:S(2)}, u32[]{:S(2)}) collective-permute-start(bf16[64,64,128]{2,1,0:T(8,128)(2,1)S(1)} %get-tuple-element.52), channel_id=1, source_target_pairs={{0,1},{1,0},{2,3},{3,2},{4,5},{5,4},{6,7},{7,6},{8,9},{9,8},{10,11... | collective-permute-start | bytes 3145736 | tf_op jit(solution)/shard_map/ppermute | solution.py:28
